TPU v7x, 32 devices: a whole 2x2x4 slice. The times are simulated.
32 devices in a mesh: dp: 8 (over z, x), tp: 4 (over y, core).
Axes of the slice: x: 2, y: 2, z: 4, core: 2. Of those that a mesh axis runs over, the one named last changes fastest.
Arguments:
- layer_input: bfloat16 [8, 2048, 768], P('dp', 'tp'), may hold values from -6 to 6
- norm_gain: float32 [3, 768], replicated, may hold values from 0.5 to 1.5
- norm_bias: float32 [3, 768], replicated, may hold values from -3 to 3
- self_input_weight: bfloat16 [768, 3, 768], P(None, None, 'tp'), may hold values from -0.21875 to 0.21875
- self_input_bias: float32 [3, 768], P(None, 'tp'), may hold values from -2 to 2
- self_output_weight: bfloat16 [768, 768], P('tp'), may hold values from -0.875 to 0.875
- out_bias: float32 [3, 768], replicated, may hold values from -2 to 2
- cross_query_weight: bfloat16 [768, 768], P(None, 'tp'), may hold values from -0.21875 to 0.21875
- b_cross_q: float32 [768], P('tp'), may hold values from -2 to 2
- w_cross_kv: bfloat16 [768, 2, 768], P(None, None, 'tp'), may hold values from -0.21875 to 0.21875
- b_cross_v: float32 [768], P('tp'), may hold values from -2 to 2
- cross_output_weight: bfloat16 [768, 768], P('tp'), may hold values from -0.875 to 0.875
- expand_weight_1: bfloat16 [768, 3072], P(None, 'tp'), may hold values from -0.21875 to 0.21875
- expand_bias_1: float32 [3072], P('tp'), may hold values from -3 to 3
- contract_weight_2: bfloat16 [3072, 768], P('tp'), may hold values from -0.109375 to 0.109375
- neighbours: bfloat16 [8, 64, 128, 768], P('dp', 'tp'), may hold values from -6 to 6
- segment_ids: int32 [8, 2048], P('dp'), may hold values from 0 to 4, as said below
- span_map: int32 [8, 64], P('dp'), may hold values from 0 to 63, each once within a row
- cotangent: float32 [8, 2048, 768], P('dp', 'tp'), may hold values from -6 to 6
Outputs:
- layer_output: float32 [8, 2048, 768], P('dp', 'tp')
- grad_input: float32 [8, 2048, 768], P('dp', 'tp')
- grad_neighbours: float32 [8, 64, 128, 768], P('dp', 'tp')
- grad_norm_gain: float32 [3, 768], replicated
- grad_norm_bias: float32 [3, 768], replicated
- grad_w_qkv: float32 [768, 3, 768], P(None, None, 'tp')
- grad_b_qkv: float32 [3, 768], P(None, 'tp')
- grad_w_attn_out: float32 [768, 768], P('tp')
- grad_out_bias: float32 [3, 768], replicated
- grad_w_cross_q: float32 [768, 768], P(None, 'tp')
- grad_b_cross_q: float32 [768], P('tp')
- grad_w_cross_kv: float32 [768, 2, 768], P(None, None, 'tp')
- grad_b_cross_v: float32 [768], P('tp')
- grad_w_cross_out: float32 [768, 768], P('tp')
- expand_weight_gradient_1: float32 [768, 3072], P(None, 'tp')
- grad_b_fc1: float32 [3072], P('tp')
- contract_weight_gradient_2: float32 [3072, 768], P('tp')
Inputs may be any that keep to these rules, and one draw needn't show every extreme that they name: `segment_ids`: ids never fall along a row, start at 0 in every row and rise by one at each new document; every row holds five documents. `span_map`: each row is a permutation of 0 to 63.
All inputs are finite; a program needn't handle non-finite values.
Results may differ from a plain program's by a relative error of at most 0.029.
Values may be sent and summed in bfloat16 or wider, within the bound.
No kernel may reach another device: no remote copies, remote signals or barrier semaphores. Data moves between devices by JAX's collectives and lax.ppermute only.
A program may use at most 256 MiB of HBM per device.

v0:
```python
import math

import jax
import jax.numpy as jnp
from jax import lax
from jax.sharding import PartitionSpec as P

HEAD_DIM = 64
SPAN = 64
QBLOCK = 512


NEGATIVE = -1e30
NORM_EPS = 1e-05


def layer_norm(values, norm_scale, norm_shift):
    centre = values - jnp.mean(values, -1, keepdims=True)
    variance = jnp.mean(centre * centre, -1, keepdims=True)
    return centre * lax.rsqrt(variance + NORM_EPS) * norm_scale + norm_shift


def rotary_tables(full_length, head_width):
    halfway = head_width // 2
    frequency = 10000.0 ** (-jnp.arange(halfway, dtype=jnp.float32) / halfway)
    angles = jnp.arange(full_length, dtype=jnp.float32)[:, None] * frequency[None, :]
    cosine = jnp.concatenate([jnp.cos(angles), jnp.cos(angles)], -1)[:, None, :]
    sine_table = jnp.concatenate([jnp.sin(angles), jnp.sin(angles)], -1)[:, None, :]
    return (cosine, sine_table)


def rotate(values, cosine, sine_table):
    halfway = values.shape[-1] // 2
    turned = jnp.concatenate([-values[..., halfway:], values[..., :halfway]], -1)
    return values * cosine + turned * sine_table


def spread_rows(values):
    return lax.all_gather(values, "tp", axis=1, tiled=True)


def collect_rows(values):
    return lax.psum_scatter(
        values.astype(jnp.bfloat16), "tp", scatter_dimension=1, tiled=True
    ).astype(jnp.float32)


def masked_scores(query_block, key_vals, segments, row_start):
    block_rows = query_block.shape[1]
    full_length = key_vals.shape[1]
    scores = jnp.einsum(
        "sbhe,skhe->shbk", query_block, key_vals, preferred_element_type=jnp.float32
    )
    row_ids = row_start + lax.iota(jnp.int32, block_rows)
    columns = lax.iota(jnp.int32, full_length)
    row_segment = lax.dynamic_slice_in_dim(segments, row_start, block_rows, 1)
    allowed = (columns[None, None, :] <= row_ids[None, :, None]) & (
        row_segment[:, :, None] == segments[:, None, :]
    )
    return jnp.where(allowed[:, None], scores, NEGATIVE)


def shards(
    layer_input,
    norm_gain,
    norm_bias,
    self_input_weight,
    self_input_bias,
    self_output_weight,
    out_bias,
    cross_query_weight,
    b_cross_q,
    w_cross_kv,
    b_cross_v,
    cross_output_weight,
    expand_weight_1,
    expand_bias_1,
    contract_weight_2,
    neighbours,
    segment_ids,
    span_map,
    cotangent,
):
    seq_count = layer_input.shape[0]
    full_length = segment_ids.shape[1]
    local_width = self_input_weight.shape[2]
    local_heads = local_width // HEAD_DIM
    span_count = full_length // SPAN
    block_rows = QBLOCK
    block_count = full_length // block_rows
    pool_size = span_map.shape[1]
    neigh_len = neighbours.shape[2]
    per_span = pool_size // span_count * neigh_len
    scale_q = 1.0 / math.sqrt(HEAD_DIM)
    cosine, sine_table = rotary_tables(full_length, HEAD_DIM)
    inputs32 = layer_input.astype(jnp.float32)
    block_ids = jnp.arange(block_count, dtype=jnp.int32)
    normalized_first = spread_rows(
        layer_norm(inputs32, norm_gain[0], norm_bias[0]).astype(jnp.bfloat16)
    )
    project = (
        jnp.einsum(
            "aur,rch->auch", normalized_first, self_input_weight, preferred_element_type=jnp.float32
        )
        + self_input_bias
    )
    shaped = project.reshape(seq_count, full_length, 3, local_heads, HEAD_DIM)
    query16 = (rotate(shaped[:, :, 0], cosine, sine_table) * scale_q).astype(jnp.bfloat16)
    key16 = rotate(shaped[:, :, 1], cosine, sine_table).astype(jnp.bfloat16)
    value16 = shaped[:, :, 2].astype(jnp.bfloat16)

    def forward_block(carry, block_index):
        row_start = block_index * block_rows
        query_block = lax.dynamic_slice_in_dim(query16, row_start, block_rows, 1)
        scores = masked_scores(query_block, key16, segment_ids, row_start)
        maxima = jnp.max(scores, -1, keepdims=True)
        shifted = jnp.exp(scores - maxima)
        row_total = jnp.sum(shifted, -1, keepdims=True)
        attn_prob = shifted / row_total
        mixed_block = jnp.einsum(
            "shbk,skhe->sbhe",
            attn_prob.astype(jnp.bfloat16),
            value16,
            preferred_element_type=jnp.float32,
        )
        return (carry, (mixed_block, (maxima + jnp.log(row_total))[..., 0]))

    _, (mixed_blocks, log_totals) = lax.scan(forward_block, 0, block_ids)
    attended_half = (
        jnp.moveaxis(mixed_blocks, 0, 1)
        .reshape(seq_count, full_length, local_width)
        .astype(jnp.bfloat16)
    )
    self_out = collect_rows(
        jnp.einsum(
            "tgq,qf->tgf", attended_half, self_output_weight, preferred_element_type=jnp.float32
        )
    )
    after_self = inputs32 + self_out + out_bias[0]
    normalized_second = spread_rows(
        layer_norm(after_self, norm_gain[1], norm_bias[1]).astype(jnp.bfloat16)
    )
    cross_query = (
        (
            jnp.einsum(
                "uct,to->uco",
                normalized_second,
                cross_query_weight,
                preferred_element_type=jnp.float32,
            )
            + b_cross_q
        )
        * scale_q
    ).astype(jnp.bfloat16)
    cross_query = cross_query.reshape(seq_count, span_count, SPAN, local_heads, HEAD_DIM)
    memory = lax.all_gather(neighbours, "tp", axis=1, tiled=True)
    kv_bias = jnp.stack([jnp.zeros_like(b_cross_v), b_cross_v])
    memory_kv = (
        jnp.einsum("spnd,dte->spnte", memory, w_cross_kv, preferred_element_type=jnp.float32)
        + kv_bias
    ).astype(jnp.bfloat16)
    chosen = jax.vmap(lambda kv_table, pick_rows: kv_table[pick_rows])(memory_kv, span_map)
    chosen = chosen.reshape(seq_count, span_count, per_span, 2, local_heads, HEAD_DIM)
    cross_key = chosen[:, :, :, 0]
    cross_value = chosen[:, :, :, 1]
    cross_scores = jnp.einsum(
        "scqhe,sckhe->schqk", cross_query, cross_key, preferred_element_type=jnp.float32
    )
    cross_max = jnp.max(cross_scores, -1, keepdims=True)
    cross_exp = jnp.exp(cross_scores - cross_max)
    cross_prob = cross_exp / jnp.sum(cross_exp, -1, keepdims=True)
    cross_prob16 = cross_prob.astype(jnp.bfloat16)
    cross_mixed = jnp.einsum(
        "schqk,sckhe->scqhe", cross_prob16, cross_value, preferred_element_type=jnp.float32
    )
    cross_half = cross_mixed.reshape(seq_count, full_length, local_width).astype(jnp.bfloat16)
    cross_out = collect_rows(
        jnp.einsum(
            "tgq,qf->tgf", cross_half, cross_output_weight, preferred_element_type=jnp.float32
        )
    )
    after_cross = after_self + cross_out + out_bias[1]
    normalized_middle = spread_rows(
        layer_norm(after_cross, norm_gain[2], norm_bias[2]).astype(jnp.bfloat16)
    )
    before_gelu = (
        jnp.einsum(
            "zpv,vm->zpm", normalized_middle, expand_weight_1, preferred_element_type=jnp.float32
        )
        + expand_bias_1
    )
    hidden_half = jax.nn.gelu(before_gelu).astype(jnp.bfloat16)
    mlp_out = collect_rows(
        jnp.einsum(
            "wji,ic->wjc", hidden_half, contract_weight_2, preferred_element_type=jnp.float32
        )
    )
    layer_output = after_cross + mlp_out + out_bias[2]
    grad_bias_two = jnp.sum(cotangent, (0, 1))
    gradient_half = spread_rows(cotangent.astype(jnp.bfloat16))
    contract_weight_gradient_2 = jnp.einsum(
        "opc,opx->cx", hidden_half, gradient_half, preferred_element_type=jnp.float32
    )
    hidden_gradient = jnp.einsum(
        "jik,wk->jiw", gradient_half, contract_weight_2, preferred_element_type=jnp.float32
    )
    _, gelu_pull = jax.vjp(jax.nn.gelu, before_gelu)
    preact_gradient_half = gelu_pull(hidden_gradient)[0].astype(jnp.bfloat16)
    grad_b_fc1 = jnp.sum(preact_gradient_half, (0, 1), dtype=jnp.float32)
    expand_weight_gradient_1 = jnp.einsum(
        "xar,xai->ri", normalized_middle, preact_gradient_half, preferred_element_type=jnp.float32
    )
    grad_normed_m = collect_rows(
        jnp.einsum(
            "bwc,vc->bwv", preact_gradient_half, expand_weight_1, preferred_element_type=jnp.float32
        )
    )
    _, norm_pull_two = jax.vjp(layer_norm, after_cross, norm_gain[2], norm_bias[2])
    part_two, grad_gain_two, grad_shift_two = norm_pull_two(grad_normed_m)
    grad_cross = cotangent + part_two
    grad_bias_one = jnp.sum(grad_cross, (0, 1))
    cross_gradient_half = spread_rows(grad_cross.astype(jnp.bfloat16))
    grad_w_cross_out = jnp.einsum(
        "rtx,rtz->xz", cross_half, cross_gradient_half, preferred_element_type=jnp.float32
    )
    grad_mixed16 = jnp.einsum(
        "tmy,fy->tmf", cross_gradient_half, cross_output_weight, preferred_element_type=jnp.float32
    ).astype(jnp.bfloat16)
    grad_mixed16 = grad_mixed16.reshape(seq_count, span_count, SPAN, local_heads, HEAD_DIM)
    grad_cprob = jnp.einsum(
        "scqhe,sckhe->schqk", grad_mixed16, cross_value, preferred_element_type=jnp.float32
    )
    grad_cvalue = jnp.einsum(
        "schqk,scqhe->sckhe", cross_prob16, grad_mixed16, preferred_element_type=jnp.float32
    )
    grad_cscores16 = (
        cross_prob * (grad_cprob - jnp.sum(cross_prob * grad_cprob, -1, keepdims=True))
    ).astype(jnp.bfloat16)
    grad_cquery = jnp.einsum(
        "schqk,sckhe->scqhe", grad_cscores16, cross_key, preferred_element_type=jnp.float32
    )
    grad_ckey = jnp.einsum(
        "schqk,scqhe->sckhe", grad_cscores16, cross_query, preferred_element_type=jnp.float32
    )
    query_gradient_half = (
        (grad_cquery * scale_q).astype(jnp.bfloat16).reshape(seq_count, full_length, local_width)
    )
    grad_b_cross_q = jnp.sum(query_gradient_half, (0, 1), dtype=jnp.float32)
    grad_w_cross_q = jnp.einsum(
        "kbf,kbt->ft", normalized_second, query_gradient_half, preferred_element_type=jnp.float32
    )
    grad_normed_b = jnp.einsum(
        "amn,wn->amw", query_gradient_half, cross_query_weight, preferred_element_type=jnp.float32
    )
    grad_chosen = jnp.stack([grad_ckey, grad_cvalue], 3).reshape(
        seq_count, pool_size, neigh_len, 2, local_width
    )
    grad_memory_kv = jax.vmap(
        lambda kv_table, pick_rows, updates: kv_table.at[pick_rows].add(updates)
    )(jnp.zeros(memory_kv.shape, jnp.float32), span_map, grad_chosen).astype(jnp.bfloat16)
    grad_b_cross_v = jnp.sum(grad_memory_kv[:, :, :, 1], (0, 1, 2), dtype=jnp.float32)
    grad_w_cross_kv = jnp.einsum(
        "spnd,spnte->dte", memory, grad_memory_kv, preferred_element_type=jnp.float32
    )
    grad_neighbours = lax.psum_scatter(
        jnp.einsum(
            "spnte,dte->spnd", grad_memory_kv, w_cross_kv, preferred_element_type=jnp.float32
        ).astype(jnp.bfloat16),
        "tp",
        scatter_dimension=1,
        tiled=True,
    ).astype(jnp.float32)
    grad_normed_local = collect_rows(grad_normed_b)
    _, norm_pull_one = jax.vjp(layer_norm, after_self, norm_gain[1], norm_bias[1])
    part_one, grad_gain_one, grad_shift_one = norm_pull_one(grad_normed_local)
    grad_self = grad_cross + part_one
    grad_bias_zero = jnp.sum(grad_self, (0, 1))
    self_gradient_half = spread_rows(grad_self.astype(jnp.bfloat16))
    grad_w_attn_out = jnp.einsum(
        "rtx,rtz->xz", attended_half, self_gradient_half, preferred_element_type=jnp.float32
    )
    grad_att16 = jnp.einsum(
        "tmy,fy->tmf", self_gradient_half, self_output_weight, preferred_element_type=jnp.float32
    ).astype(jnp.bfloat16)
    grad_att16 = grad_att16.reshape(seq_count, full_length, local_heads, HEAD_DIM)

    def backward_block(carry, block_index):
        grad_key_acc, grad_value_acc = carry
        row_start = block_index * block_rows
        query_block = lax.dynamic_slice_in_dim(query16, row_start, block_rows, 1)
        grad_block = lax.dynamic_slice_in_dim(grad_att16, row_start, block_rows, 1)
        scores = masked_scores(query_block, key16, segment_ids, row_start)
        attn_prob = jnp.exp(scores - log_totals[block_index][..., None])
        grad_prob = jnp.einsum(
            "sbhe,skhe->shbk", grad_block, value16, preferred_element_type=jnp.float32
        )
        grad_scores16 = (
            attn_prob * (grad_prob - jnp.sum(attn_prob * grad_prob, -1, keepdims=True))
        ).astype(jnp.bfloat16)
        grad_query_block = jnp.einsum(
            "shbk,skhe->sbhe", grad_scores16, key16, preferred_element_type=jnp.float32
        )
        grad_key_acc = grad_key_acc + jnp.einsum(
            "shbk,sbhe->skhe", grad_scores16, query_block, preferred_element_type=jnp.float32
        )
        grad_value_acc = grad_value_acc + jnp.einsum(
            "shbk,sbhe->skhe",
            attn_prob.astype(jnp.bfloat16),
            grad_block,
            preferred_element_type=jnp.float32,
        )
        return ((grad_key_acc, grad_value_acc), grad_query_block)

    empty_acc = jnp.zeros(key16.shape, jnp.float32)
    (grad_key, grad_value), grad_query_blocks = lax.scan(
        backward_block, (empty_acc, empty_acc), block_ids
    )
    grad_query = jnp.moveaxis(grad_query_blocks, 0, 1).reshape(
        seq_count, full_length, local_heads, HEAD_DIM
    )

    def rotary_map(query_part, key_part):
        return (
            rotate(query_part, cosine, sine_table) * scale_q,
            rotate(key_part, cosine, sine_table),
        )

    _, rotary_pull = jax.vjp(rotary_map, shaped[:, :, 0], shaped[:, :, 1])
    grad_query_pre, grad_key_pre = rotary_pull((grad_query, grad_key))
    projection_gradient_half = (
        jnp.stack([grad_query_pre, grad_key_pre, grad_value], 2)
        .reshape(seq_count, full_length, 3, local_width)
        .astype(jnp.bfloat16)
    )
    grad_b_qkv = jnp.sum(projection_gradient_half, (0, 1), dtype=jnp.float32)
    grad_w_qkv = jnp.einsum(
        "bzf,bzio->fio",
        normalized_first,
        projection_gradient_half,
        preferred_element_type=jnp.float32,
    )
    grad_normed_a = collect_rows(
        jnp.einsum(
            "whgo,bgo->whb",
            projection_gradient_half,
            self_input_weight,
            preferred_element_type=jnp.float32,
        )
    )
    _, norm_pull_zero = jax.vjp(layer_norm, inputs32, norm_gain[0], norm_bias[0])
    part_zero, grad_gain_zero, grad_shift_zero = norm_pull_zero(grad_normed_a)
    grad_input = grad_self + part_zero
    (
        grad_w_qkv,
        grad_b_qkv,
        grad_w_attn_out,
        grad_w_cross_q,
        grad_b_cross_q,
        grad_w_cross_kv,
        grad_b_cross_v,
        grad_w_cross_out,
        expand_weight_gradient_1,
        grad_b_fc1,
        contract_weight_gradient_2,
    ) = lax.psum(
        (
            grad_w_qkv,
            grad_b_qkv,
            grad_w_attn_out,
            grad_w_cross_q,
            grad_b_cross_q,
            grad_w_cross_kv,
            grad_b_cross_v,
            grad_w_cross_out,
            expand_weight_gradient_1,
            grad_b_fc1,
            contract_weight_gradient_2,
        ),
        "dp",
    )
    grad_norm_gain, grad_norm_bias, grad_out_bias = lax.psum(
        (
            jnp.stack([grad_gain_zero, grad_gain_one, grad_gain_two]),
            jnp.stack([grad_shift_zero, grad_shift_one, grad_shift_two]),
            jnp.stack([grad_bias_zero, grad_bias_one, grad_bias_two]),
        ),
        ("dp", "tp"),
    )
    return (
        layer_output,
        grad_input,
        grad_neighbours,
        grad_norm_gain,
        grad_norm_bias,
        grad_w_qkv,
        grad_b_qkv,
        grad_w_attn_out,
        grad_out_bias,
        grad_w_cross_q,
        grad_b_cross_q,
        grad_w_cross_kv,
        grad_b_cross_v,
        grad_w_cross_out,
        expand_weight_gradient_1,
        grad_b_fc1,
        contract_weight_gradient_2,
    )


def solution(mesh):
    return jax.shard_map(
        shards,
        mesh=mesh,
        in_specs=(
            P("dp", "tp", None),
            P(),
            P(),
            P(None, None, "tp"),
            P(None, "tp"),
            P("tp", None),
            P(),
            P(None, "tp"),
            P("tp"),
            P(None, None, "tp"),
            P("tp"),
            P("tp", None),
            P(None, "tp"),
            P("tp"),
            P("tp", None),
            P("dp", "tp", None, None),
            P("dp", None),
            P("dp", None),
            P("dp", "tp", None),
        ),
        out_specs=(
            P("dp", "tp", None),
            P("dp", "tp", None),
            P("dp", "tp", None, None),
            P(),
            P(),
            P(None, None, "tp"),
            P(None, "tp"),
            P("tp", None),
            P(),
            P(None, "tp"),
            P("tp"),
            P(None, None, "tp"),
            P("tp"),
            P("tp", None),
            P(None, "tp"),
            P("tp"),
            P("tp", None),
        ),
        check_vma=False,
    )
```

profile of v0, /device:TPU:0, one launch (start us, length us, event | category | flops | bytes accessed | tf_op | source)
XLA Modules:
  0.0 1468.1 jit_solution(17995825955681552850)
XLA Ops:
  19.1 28.3 %all-gather.8.cloned.1.call-done = bf16[1,2048,768]{2,1,0:T(8,128)(2,1)} async-done(((bf16[1,512,768]{2,1,0:T(8,128)(2,1)}), bf16[1,2048,768]{2,1,0:T(8,128)(2,1)}) %all-gather.8.cloned.1.call-update) | async-done | bytes 3145744 | tf_op jit(solution)/shard_map/all_gather | solution.py:39
  55.2 100.2 %while.27 = (s32[]{:T(128)}, bf16[4,1,512,3,64]{2,4,3,1,0:T(8,128)(2,1)}, f32[4,1,3,512]{3,2,1,0:T(4,128)}, s32[4]{0:T(128)S(1)}, s32[1,2048]{1,0:T(1,128)S(1)},...) while((s32[]{:T(128)}, ...), condition=%wide.region_5.6_spmd, body=%wide.region_2.5_spmd.sunk | while | flops 836762624 | bytes 50471168 | solution.py:128
  162.6 36.8 %reduce-scatter.8.cloned.1.call-done = bf16[1,512,768]{2,1,0:T(8,128)(2,1)} async-done(((bf16[1,2048,768]{2,1,0:T(8,128)(2,1)}), bf16[1,512,768]{2,1,0:T(8,128)(2,1)}) %reduce-scatter.8.cloned.1.call-update) | async-done | bytes 786448 | tf_op jit(solution)/shard_map/reduce_scatter | solution.py:43
  208.6 25.9 %all-gather.12.cloned.1.call-done = bf16[1,2048,768]{2,1,0:T(8,128)(2,1)} async-done(((bf16[1,512,768]{2,1,0:T(8,128)(2,1)}), bf16[1,2048,768]{2,1,0:T(8,128)(2,1)}) %all-gather.12.cloned.1.call-update) | async-done | bytes 3145744 | tf_op jit(solution)/shard_map/all_gather | solution.py:39
  241.9 76.2 %all-gather.10.cloned.1.call-done = bf16[1,64,128,768]{3,2,0,1:T(8,128)(2,1)} async-done(((bf16[1,16,128,768]{3,2,0,1:T(8,128)(2,1)}), bf16[1,64,128,768]{3,2,0,1:T(8,128)(2,1)}) %all-gather.10.cloned.1.call-update) | async-done | bytes 12582928 | tf_op jit(solution)/shard_map/all_gather | solution.py:156
  361.3 12.0 fusion.176
  390.7 38.1 %reduce-scatter.10.cloned.1.call-done = bf16[1,512,768]{2,1,0:T(8,128)(2,1)} async-done(((bf16[1,2048,768]{2,1,0:T(8,128)(2,1)}), bf16[1,512,768]{2,1,0:T(8,128)(2,1)}) %reduce-scatter.10.cloned.1.call-update) | async-done | bytes 786448 | tf_op jit(solution)/shard_map/reduce_scatter | solution.py:43
  436.6 27.9 %all-gather.14.cloned.1.call-done = bf16[1,2048,768]{2,1,0:T(8,128)(2,1)} async-done(((bf16[1,512,768]{2,1,0:T(8,128)(2,1)}), bf16[1,2048,768]{2,1,0:T(8,128)(2,1)}) %all-gather.14.cloned.1.call-update) | async-done | bytes 3145744 | tf_op jit(solution)/shard_map/all_gather | solution.py:39
  472.0 23.3 %all-gather.16.cloned.1.call-done = bf16[1,2048,768]{2,1,0:T(8,128)(2,1)} async-done(((bf16[1,512,768]{2,1,0:T(8,128)(2,1)}), bf16[1,2048,768]{2,1,0:T(8,128)(2,1)}) %all-gather.16.cloned.1.call-update) | async-done | bytes 3145744 | tf_op jit(solution)/shard_map/all_gather | solution.py:39
  495.3 10.9 convert_reduce_fusion
  521.0 29.1 %reduce-scatter.14.cloned.1.call-done = bf16[1,512,768]{2,1,0:T(8,128)(2,1)} async-done(((bf16[1,2048,768]{2,1,0:T(8,128)(2,1)}), bf16[1,512,768]{2,1,0:T(8,128)(2,1)}) %reduce-scatter.14.cloned.1.call-update) | async-done | bytes 786448 | tf_op jit(solution)/shard_map/reduce_scatter | solution.py:43
  555.9 34.9 %reduce-scatter.12.cloned.1.call-done = bf16[1,512,768]{2,1,0:T(8,128)(2,1)} async-done(((bf16[1,2048,768]{2,1,0:T(8,128)(2,1)}), bf16[1,512,768]{2,1,0:T(8,128)(2,1)}) %reduce-scatter.12.cloned.1.call-update) | async-done | bytes 786448 | tf_op jit(solution)/shard_map/reduce_scatter | solution.py:43
  597.5 28.6 %all-gather.18.cloned.1.call-done = bf16[1,2048,768]{2,1,0:T(8,128)(2,1)} async-done(((bf16[1,512,768]{2,1,0:T(8,128)(2,1)}), bf16[1,2048,768]{2,1,0:T(8,128)(2,1)}) %all-gather.18.cloned.1.call-update) | async-done | bytes 3145744 | tf_op jit(solution)/shard_map/all_gather | solution.py:39
  631.9 10.9 multiply_reduce_fusion.1
  662.3 38.1 %reduce-scatter.16.cloned.1.call-done = bf16[1,512,768]{2,1,0:T(8,128)(2,1)} async-done(((bf16[1,2048,768]{2,1,0:T(8,128)(2,1)}), bf16[1,512,768]{2,1,0:T(8,128)(2,1)}) %reduce-scatter.16.cloned.1.call-update) | async-done | bytes 786448 | tf_op jit(solution)/shard_map/reduce_scatter | solution.py:43
  708.2 28.6 %all-gather.20.cloned.1.call-done = bf16[1,2048,768]{2,1,0:T(8,128)(2,1)} async-done(((bf16[1,512,768]{2,1,0:T(8,128)(2,1)}), bf16[1,2048,768]{2,1,0:T(8,128)(2,1)}) %all-gather.20.cloned.1.call-update) | async-done | bytes 3145744 | tf_op jit(solution)/shard_map/all_gather | solution.py:39
  739.9 172.1 %while.28 = (s32[]{:T(128)}, f32[1,2048,3,64]{1,3,2,0:T(8,128)}, f32[1,2048,3,64]{1,3,2,0:T(8,128)}, f32[4,1,512,3,64]{2,0,4,3,1:T(4,128)}, s32[4]{0:T(128)S(1)}...) while((s32[]{:T(128)}, f32[1,2048,3,64]{1,3,2,0:T(8,128)}, ...), condition=%wide.region_24.25_spmd.clone, body=%wide.region_22.24_spmd.clone.sunk | while | flops 2055732224 | bytes 151976400 | solution.py:315
  960.3 11.9 maximum_bitcast_fusion
  972.3 16.4 %copy.70 = f32[64,128,2,192]{1,3,2,0:T(8,128)} copy(f32[64,128,2,192]{1,0,3,2:T(8,128)} %maximum_bitcast_fusion) | data formatting | bytes 25165824 | tf_op jit(solution)/shard_map/stack | solution.py:255
  994.8 32.2 %scatter_fusion = f32[64,128,2,192]{1,3,2,0:T(8,128)} fusion(f32[64,128,2,192]{1,3,2,0:T(8,128)} %broadcast.423, s32[64]{0:T(128)S(1)} %copy-done.91, f32[64,128,2,192]{1,3,2,0:T(8,128)} %copy.70), kind=kCustom, calls=%fused_computation.1 | custom fusion | flops 3145728 | bytes 37748992 | tf_op jit(solution)/shard_map/vmap()/scatter-add | solution.py:259
  1027.0 14.4 fusion.45
  1092.5 37.2 %all-reduce.6 = (f32[3,192]{1,0:T(4,128)}, f32[192]{0:T(256)}, f32[192]{0:T(256)}, f32[768]{0:T(1024)}) all-reduce(f32[3,192]{1,0:T(4,128)S(1)} %convert_reduce_fusion.2, f32[192]{0:T(256)S(1)} %reduce_sum.303, f32[192]{0:T(256)S(1)} %convert_reduce_fusion.1, f32[768]{0:T(1024)S(1)} %copy-done.90), channel_id=1, replica_groups=mesh['dp'=8,'tp'=4] {'dp'}, use_global_device_ids=true, to_apply=%region_40.41 | all-reduce | flops 1728 | bytes 13824 | tf_op jit(solution)/shard_map/psum | solution.py:365
  1133.6 40.2 %all-reduce.5 = (f32[3,768]{1,0:T(4,128)}, f32[3,768]{1,0:T(4,128)}, f32[3,768]{1,0:T(4,128)}) all-reduce(f32[3,768]{1,0:T(4,128)S(1)} %pad_maximum_fusion.3, f32[3,768]{1,0:T(4,128)S(1)} %pad_maximum_fusion.4, f32[3,768]{1,0:T(4,128)S(1)} %pad_maximum_fusion.5), channel_id=1, replica_groups=mesh['dp'=8,'tp'=4] {'dp','tp'}, use_global_device_ids=true, to_apply=%region_33.34 | all-reduce | flops 6912 | bytes 55296 | tf_op jit(solution)/shard_map/psum | solution.py:381
  1180.9 270.1 %all-reduce.10.cloned.1.call-done = (f32[768,3,192]{0,2,1:T(8,128)}, f32[192,768]{1,0:T(8,128)}, f32[768,192]{0,1:T(8,128)}, f32[768,2,192]{0,2,1:T(8,128)}, f32...) async-done(((f32[768,3,192]{0,2,1:T(8,128)}, f32[192,768]{1,0:T(8,128)}, f32[768,192]{0,1:T(8,128)}, f32[768,2,192]{0,2,1:T(8,128)}, f32[192,768]{1,0:T(8,128)}, ...) | async-done | bytes 9437200 | tf_op jit(solution)/shard_map/psum | solution.py:365
  (511 shorter events, 567.1 us)
Async XLA Ops:
  7.2 488.1 %copy-start = (bf16[768,768]{1,0:T(8,128)(2,1)S(1)}, bf16[768,768]{1,0:T(8,128)(2,1)}, u32[]{:S(2)}) copy-start(bf16[768,768]{1,0:T(8,128)(2,1)} %param.37) | copy-start | bytes 3538948
  7.2 40.2 %all-gather.8.cloned.1.call-start = ((), (), s32[]{:S(2)}) async-start(), calls=%async_computation.7 | async-start | bytes 3932160 | tf_op jit(solution)/shard_map/all_gather | solution.py:39
  16.1 183.3 %reduce-scatter.8.cloned.1.call-start = ((), (), s32[]{:S(2)}) async-start(), calls=%async_computation.8 | async-start | bytes 3932160 | tf_op jit(solution)/shard_map/reduce_scatter | solution.py:43
  161.3 42.4 %copy-start.57 = (f32[768]{0:T(1024)S(1)}, f32[768]{0:T(1024)}, u32[]{:S(2)}) copy-start(f32[768]{0:T(1024)} %get-tuple-element.177) | copy-start | bytes 9220
  161.3 73.2 %all-gather.12.cloned.1.call-start = ((), (), s32[]{:S(2)}) async-start(), calls=%async_computation.10 | async-start | bytes 3932160 | tf_op jit(solution)/shard_map/all_gather | solution.py:39
  205.8 112.3 %all-gather.10.cloned.1.call-start = ((), (), s32[]{:S(2)}) async-start(), calls=%async_computation.9 | async-start | bytes 15728640 | tf_op jit(solution)/shard_map/all_gather | solution.py:156
  206.3 222.4 %reduce-scatter.10.cloned.1.call-start = ((), (), s32[]{:S(2)}) async-start(), calls=%async_computation.11 | async-start | bytes 3932160 | tf_op jit(solution)/shard_map/reduce_scatter | solution.py:43
  390.6 73.9 %all-gather.14.cloned.1.call-start = ((), (), s32[]{:S(2)}) async-start(), calls=%async_computation.12 | async-start | bytes 3932160 | tf_op jit(solution)/shard_map/all_gather | solution.py:39
  435.8 59.4 %all-gather.16.cloned.1.call-start = ((), (), s32[]{:S(2)}) async-start(), calls=%async_computation.14 | async-start | bytes 3932160 | tf_op jit(solution)/shard_map/all_gather | solution.py:39
  436.6 113.5 %reduce-scatter.14.cloned.1.call-start = ((), (), s32[]{:S(2)}) async-start(), calls=%async_computation.15 | async-start | bytes 3932160 | tf_op jit(solution)/shard_map/reduce_scatter | solution.py:43
  512.0 78.8 %reduce-scatter.12.cloned.1.call-start = ((), (), s32[]{:S(2)}) async-start(), calls=%async_computation.13 | async-start | bytes 3932160 | tf_op jit(solution)/shard_map/reduce_scatter | solution.py:43
  521.0 69.8 %copy-start.80 = (f32[768]{0:T(1024)S(1)}, f32[768]{0:T(1024)}, u32[]{:S(2)}) copy-start(f32[768]{0:T(1024)} %get-tuple-element.172) | copy-start | bytes 9220
  521.0 105.1 %all-gather.18.cloned.1.call-start = ((), (), s32[]{:S(2)}) async-start(), calls=%async_computation.16 | async-start | bytes 3932160 | tf_op jit(solution)/shard_map/all_gather | solution.py:39
  597.4 102.9 %reduce-scatter.16.cloned.1.call-start = ((), (), s32[]{:S(2)}) async-start(), calls=%async_computation.17 | async-start | bytes 3932160 | tf_op jit(solution)/shard_map/reduce_scatter | solution.py:43
  662.2 40.8 %copy-start.76 = (f32[512]{0:T(512)S(1)}, f32[512]{0:T(512)}, u32[]{:S(2)}) copy-start(f32[512]{0:T(512)} %copy-done.75) | copy-start | bytes 6148
  662.2 40.8 %copy-start.70 = (f32[512]{0:T(512)S(1)}, f32[512]{0:T(512)}, u32[]{:S(2)}) copy-start(f32[512]{0:T(512)} %copy-done.69) | copy-start | bytes 6148
  662.2 74.5 %all-gather.20.cloned.1.call-start = ((), (), s32[]{:S(2)}) async-start(), calls=%async_computation.18 | async-start | bytes 3932160 | tf_op jit(solution)/shard_map/all_gather | solution.py:39
  708.1 421.6 %reduce-scatter.18.cloned.1.call-start = ((), (), s32[]{:S(2)}) async-start(), calls=%async_computation.19 | async-start | bytes 3932160 | tf_op jit(solution)/shard_map/reduce_scatter | solution.py:43
  919.0 152.4 %copy-start.22 = (bf16[1,2048,3,64]{1,3,2,0:T(8,128)(2,1)}, bf16[1,2048,3,64]{1,3,2,0:T(8,128)(2,1)S(1)}, u32[]{:S(2)}) copy-start(bf16[1,2048,3,64]{1,3,2,0:T(8,128)(2,1)S(1)} %add_convert_fusion.1) | copy-start | bytes 2359300
  924.9 250.7 %reduce-scatter.20.cloned.1.call-start = ((), (), s32[]{:S(2)}) async-start(), calls=%async_computation.20 | async-start | bytes 15728640 | tf_op jit(solution)/shard_map/reduce_scatter | solution.py:265
  1041.4 409.6 %all-reduce.10.cloned.1.call-start = ((), (), s32[]{:S(2)}) async-start(), calls=%async_computation.21 | async-start | bytes 18874368 | tf_op jit(solution)/shard_map/psum | solution.py:365
  1089.0 40.7 %copy-start.7 = (bf16[1,512,768]{2,1,0:T(8,128)(2,1)S(1)}, bf16[1,512,768]{2,1,0:T(8,128)(2,1)}, u32[]{:S(2)}) copy-start(bf16[1,512,768]{2,1,0:T(8,128)(2,1)} %param.23) | copy-start | bytes 2359300
  1092.1 81.8 %copy-start.15 = (f32[1,512,768]{2,1,0:T(8,128)S(1)}, f32[1,512,768]{2,1,0:T(8,128)}, u32[]{:S(2)}) copy-start(f32[1,512,768]{2,1,0:T(8,128)} %copy-done.14) | copy-start | bytes 4718596
  1129.7 44.2 %copy-start.21 = (bf16[1,512,768]{2,1,0:T(8,128)(2,1)S(1)}, bf16[1,512,768]{2,1,0:T(8,128)(2,1)}, u32[]{:S(2)}) copy-start(bf16[1,512,768]{2,1,0:T(8,128)(2,1)} %reduce-scatter.18.cloned.1.call-done) | copy-start | bytes 2359300
  (123 other events, 1073.5 us)
Sparse Core Ops, SparseCore 0:
  16.2 31.2 all-gather.7
  161.4 37.9 reduce-scatter.7
  205.9 28.5 all-gather.11
  235.9 82.1 all-gather.9
  390.8 37.9 reduce-scatter.9
  436.0 28.5 all-gather.13
  466.7 28.5 all-gather.15
  512.1 37.9 reduce-scatter.13
  552.8 37.9 reduce-scatter.11
  597.5 28.5 all-gather.17
  662.4 37.9 reduce-scatter.15
  708.2 28.5 all-gather.19
  925.0 37.9 reduce-scatter.17
  1041.5 99.3 reduce-scatter.19
  1147.9 303.0 all-reduce.9
where the time goes:
time: 1480 us; the launch traced here: 1470 us
  waiting for transfers between devices  687 us (46%)
  matrix products  307 us (21%)
  local copies, waits for them, and re-layouts  185 us (12%)
  other arithmetic  182 us (12%)
  blocking collectives  77.4 us (5%)
  between operations  15.1 us (1%)
    psum x1, waiting for transfers between devices, shards(): lax.psum((grad_w_qkv, grad_b_qkv, grad_w_attn_out, grad_w_cross_q, grad_b...  270 us
    reduce_scatter x6, waiting for transfers between devices, collect_rows(): lax.psum_scatter(values.astype(jnp.bfloat16), 'tp', scatter_dimension=1,...  177 us
    all_gather x6, waiting for transfers between devices, spread_rows(): return lax.all_gather(values, 'tp', axis=1, tiled=True)  163 us
    all_gather x1, waiting for transfers between devices, shards(): memory = lax.all_gather(neighbours, 'tp', axis=1, tiled=True)  76.2 us
    dot_general x8, matrix products, masked_scores(): jnp.einsum('sbhe,skhe->shbk', query_block, key_vals, preferred_element_ty...  42.3 us
    psum x1, blocking collectives, shards(): lax.psum((jnp.stack([grad_gain_zero, grad_gain_one, grad_gain_two]), jnp....  40.2 us
    psum x1, blocking collectives, shards(): lax.psum((grad_w_qkv, grad_b_qkv, grad_w_attn_out, grad_w_cross_q, grad_b...  37.2 us
    dynamic_update_slice x8, local copies, waits for them, and re-layouts, shards(): _, (mixed_blocks, log_totals) = lax.scan(forward_block, 0, block_ids)  36.1 us
  transfers between devices with their start and end apart: 15, of which 13 were waited for; matrix products, arithmetic and copies ran while one was open for 14% of the time, Pallas kernels for 0%

commit v1 on v0

v1 whole, which is shorter than its diff:
```python
import functools
import math

import jax
import jax.numpy as jnp
from jax import lax
from jax.experimental import pallas as pl
from jax.experimental.pallas import tpu as pltpu
from jax.sharding import PartitionSpec as P

HEAD_DIM = 64
SPAN = 64
LANES = 128
QUERY_ROWS = 256
NEGATIVE = -1e30
NORM_EPS = 1e-05
BF = jnp.bfloat16
F32 = jnp.float32
VMEM_BYTES = 56 * 1024 * 1024

DOCS = 5
MASK_LANE = HEAD_DIM
LSE_LANE = HEAD_DIM + DOCS


def nn(a, b):
    return lax.dot_general(a, b, (((1,), (0,)), ((), ())), preferred_element_type=F32)


def nt(a, b):
    return lax.dot_general(a, b, (((1,), (1,)), ((), ())), preferred_element_type=F32)


def tn(a, b):
    return lax.dot_general(a, b, (((0,), (0,)), ((), ())), preferred_element_type=F32)


def call(body, name, grid, in_specs, out_specs, out_shape, args, scratch=(), prefetch=0, flops=0):
    moved = sum(a.size * a.dtype.itemsize for a in args)
    moved += sum(math.prod(o.shape) * jnp.dtype(o.dtype).itemsize for o in jax.tree.leaves(out_shape))
    return pl.pallas_call(
        body,
        out_shape=out_shape,
        grid_spec=pltpu.PrefetchScalarGridSpec(
            num_scalar_prefetch=prefetch,
            grid=grid,
            in_specs=in_specs,
            out_specs=out_specs,
            scratch_shapes=list(scratch),
        ),
        compiler_params=pltpu.CompilerParams(
            vmem_limit_bytes=VMEM_BYTES, dimension_semantics=("arbitrary",) * len(grid)
        ),
        cost_estimate=pl.CostEstimate(flops=int(flops), bytes_accessed=int(moved), transcendentals=0),
        name=name,
    )(*args)


def whole(array):
    zeros = (0,) * array.ndim
    return pl.BlockSpec(array.shape, lambda *_: zeros)


def rows_of(tile, width):
    return pl.BlockSpec((tile, width), lambda i, *_: (i, 0))


def shape_of(shape, dtype):
    return jax.ShapeDtypeStruct(shape, dtype)


def standardize(values):
    centre = values - jnp.mean(values, -1, keepdims=True)
    inverse = lax.rsqrt(jnp.mean(centre * centre, -1, keepdims=True) + NORM_EPS)
    return centre * inverse, inverse


def norm_pull(grad, normed, inverse, gain):
    scaled = grad * gain
    return inverse * (
        scaled
        - jnp.mean(scaled, -1, keepdims=True)
        - normed * jnp.mean(scaled * normed, -1, keepdims=True)
    )


def column_sum(values):
    return jnp.sum(values, 0, keepdims=True)


def add_rows(out_ref, rows):
    @pl.when(pl.program_id(0) == 0)
    def _():
        out_ref[...] = jnp.zeros_like(out_ref)

    for index, row in enumerate(rows):
        out_ref[index : index + 1, :] += row


def spread(values, partners):
    core, chip, _ = partners
    across = lax.ppermute(values, "tp", chip)
    beside = lax.ppermute(values, "tp", core)
    return [values, beside, across, lax.ppermute(across, "tp", core)]


def collect(parts, partners):
    core, chip, _ = partners
    far = lax.ppermute(parts[3], "tp", core)
    near = lax.ppermute(parts[1], "tp", core)
    sent = (parts[2].astype(F32) + far.astype(F32)).astype(BF)
    across = lax.ppermute(sent, "tp", chip)
    return (parts[0].astype(F32) + near.astype(F32)).astype(BF), across


def exchange(parts, partners):
    return [parts[0]] + [lax.ppermute(parts[r], "tp", partners[r - 1]) for r in (1, 2, 3)]


def qkv_body(t_ref, x_ref, gain_ref, shift_ref, w_ref, b_ref, cos_ref, sa_ref, sb_ref, a_ref, out_ref):
    heads = out_ref.shape[1]
    normed, _ = standardize(x_ref[...].astype(F32))
    a = (normed * gain_ref[0:1, :] + shift_ref[0:1, :]).astype(BF)
    a_ref[...] = a
    proj = nn(a, w_ref[...]) + b_ref[...]
    cos, sa, sb = cos_ref[...], sa_ref[...], sb_ref[...]
    for j in range(3 * heads):
        part = proj[:, j * LANES : (j + 1) * LANES]
        if j < 2 * heads:
            part = part * cos + pltpu.roll(part, 96, 1) * sa + pltpu.roll(part, 32, 1) * sb
        if j < heads:
            part = part * (1.0 / math.sqrt(HEAD_DIM))
        out_ref[j // heads, j % heads] = part.astype(BF)


def project_rows(rel, t, x, gain, shift, w, b, tables, heads):
    rows, width = x.shape
    tile = min(256, rows)
    steps = rows // tile
    table = pl.BlockSpec((tile, LANES), lambda i, t_ref: ((t_ref[0] ^ rel) * steps + i, 0))
    return call(
        qkv_body,
        f"qkv_{rel}",
        (steps,),
        [rows_of(tile, width), whole(gain), whole(shift), whole(w), whole(b), table, table, table],
        [rows_of(tile, width), pl.BlockSpec((3, heads, tile, LANES), lambda i, t_ref: (0, 0, i, 0))],
        [shape_of((rows, width), BF), shape_of((3, heads, rows, LANES), BF)],
        (t, x, gain, shift, w, b, *tables),
        prefetch=1,
        flops=2 * rows * width * w.shape[1],
    )


def causal_corner(scores):
    keys = lax.broadcasted_iota(jnp.int32, scores.shape, 0)
    queries = lax.broadcasted_iota(jnp.int32, scores.shape, 1)
    return jnp.where(keys <= queries, scores, NEGATIVE)


def attend_body(t_ref, c0, c1, c2, c3, qx_ref, kx_ref, vx_ref, qe_ref, ke_ref, ve_ref, ot_ref, lse_ref, vt_ref):
    t = t_ref[0]
    rows = c0.shape[2]
    for rel, chunk in enumerate((c0, c1, c2, c3)):
        place = pl.ds(pl.multiple_of((t ^ rel) * rows, rows), rows)
        qe_ref[0, place, :] = chunk[0, 0] + qx_ref[place, :]
        ke_ref[0, place, :] = chunk[1, 0] + kx_ref[place, :]
        values = chunk[2, 0] + vx_ref[...]
        ve_ref[0, place, :] = values
        vt_ref[:, place] = values.astype(F32).T.astype(BF)
    step = QUERY_ROWS
    for low in range(0, qe_ref.shape[1], step):
        high = low + step
        query = qe_ref[0, low:high, :]
        corner = causal_corner(nt(ke_ref[0, low:high, :], query))
        top = jnp.max(corner, 0, keepdims=True)
        if low:
            earlier = nt(ke_ref[0, :low, :], query)
            top = jnp.maximum(top, jnp.max(earlier, 0, keepdims=True))
        mixed = nn(vt_ref[:, low:high], jnp.exp(corner - top).astype(BF))
        if low:
            mixed = mixed + nn(vt_ref[:, :low], jnp.exp(earlier - top).astype(BF))
        total = mixed[HEAD_DIM : HEAD_DIM + 1, :]
        lse_ref[0, :, low:high] = top + jnp.log(total)
        begin = low % rows
        ot_ref[t ^ (low // rows), :, begin : begin + step] = (mixed[:HEAD_DIM] / total).astype(BF)


def attend(t, chunks, qx, kx, vx):
    _, heads, rows, _ = chunks[0].shape
    length = qx.shape[0]
    chunk = pl.BlockSpec((3, 1, rows, LANES), lambda h, t_ref: (0, h, 0, 0))
    plane = pl.BlockSpec((1, length, LANES), lambda h, t_ref: (h, 0, 0))
    padded = shape_of((heads, length, LANES), BF)
    return call(
        attend_body,
        "attend",
        (heads,),
        [chunk] * 4 + [whole(qx), whole(kx), whole(vx)],
        [
            plane,
            plane,
            plane,
            pl.BlockSpec((4, HEAD_DIM, rows), lambda h, t_ref: (0, h, 0)),
            pl.BlockSpec((1, 1, length), lambda h, t_ref: (h, 0, 0)),
        ],
        [padded, padded, padded, shape_of((4, heads * HEAD_DIM, rows), BF), shape_of((heads, 1, length), F32)],
        (t, *chunks, qx, kx, vx),
        scratch=[pltpu.VMEM((LANES, length), BF)],
        prefetch=1,
        flops=heads * length * length * 512,
    )


def three_parts(values):
    first = values.astype(BF).astype(F32)
    second = (values - first).astype(BF).astype(F32)
    return first, second, values - first - second


def attend_back_body(
    t_ref, qe_ref, ke_ref, ve_ref, d0, d1, d2, d3, ot_ref, lse_ref, cos_ref, sa_ref, sb_ref, out_ref,
    qt_ref, kt_ref, dt_ref, dk_ref, dv_ref,
):
    t = t_ref[0]
    rows = d0.shape[1]
    step = QUERY_ROWS
    length = qe_ref.shape[1]
    for rel, chunk in enumerate((d0, d1, d2, d3)):
        place = pl.ds(pl.multiple_of((t ^ rel) * rows, rows), rows)
        grad = chunk[...].astype(F32)
        delta = three_parts(jnp.sum(grad * ot_ref[rel].astype(F32), 0, keepdims=True))
        padded = jnp.concatenate([grad, jnp.zeros_like(grad)], 0)
        row = lax.broadcasted_iota(jnp.int32, padded.shape, 0)
        for index in range(3):
            padded = jnp.where(row == HEAD_DIM + index, -delta[index], padded)
        dt_ref[:, place] = padded.astype(BF)
    for low in range(0, length, rows):
        high = low + rows
        kt_ref[:, low:high] = ke_ref[0, low:high, :].astype(F32).T.astype(BF)
        turned = qe_ref[0, low:high, :].astype(F32).T
        row = lax.broadcasted_iota(jnp.int32, turned.shape, 0)
        pieces = three_parts(lse_ref[0, :, low:high])
        for index in range(3):
            turned = jnp.where(row == LSE_LANE + index, -pieces[index], turned)
        qt_ref[:, low:high] = turned.astype(BF)
    dk_ref[...] = jnp.zeros_like(dk_ref)
    dv_ref[...] = jnp.zeros_like(dv_ref)

    def unrotate(grad, place):
        return (
            grad * cos_ref[place, :]
            - pltpu.roll(grad, 96, 1) * sa_ref[place, :]
            - pltpu.roll(grad, 32, 1) * sb_ref[place, :]
        )

    for low in range(0, length, step):
        high = low + step
        query, query_t, grad_t = qe_ref[0, low:high, :], qt_ref[:, low:high], dt_ref[:, low:high]
        dq_t = None
        for begin, end in ((0, low), (low, high)):
            if begin == end:
                continue
            scores = nn(ke_ref[0, begin:end, :], query_t)
            if begin == low:
                scores = causal_corner(scores)
            prob = jnp.exp(scores)
            grad_scores = (prob * nn(ve_ref[0, begin:end, :], grad_t)).astype(BF)
            dv_ref[begin:end, :] += nt(prob.astype(BF), grad_t)
            dk_ref[begin:end, :] += nn(grad_scores, query)
            part = nn(kt_ref[:, begin:end], grad_scores)
            dq_t = part if dq_t is None else dq_t + part
        start = low % rows
        grad_query = unrotate(dq_t.T, slice(low, high)) * (1.0 / math.sqrt(HEAD_DIM))
        out_ref[t ^ (low // rows), 0, 0, start : start + step, :] = grad_query.astype(BF)
    for low in range(0, length, rows):
        place = slice(low, low + rows)
        rel = t ^ (low // rows)
        out_ref[rel, 1, 0] = unrotate(dk_ref[place, :], place).astype(BF)
        lane = lax.broadcasted_iota(jnp.int32, (rows, LANES), 1)
        out_ref[rel, 2, 0] = jnp.where(lane < HEAD_DIM, dv_ref[place, :], 0.0).astype(BF)


def attend_back(t, qe, ke, ve, grads, ot, lse, tables):
    heads, length, _ = qe.shape
    rows = grads[0].shape[1]
    plane = pl.BlockSpec((1, length, LANES), lambda h, t_ref: (h, 0, 0))
    grad = pl.BlockSpec((HEAD_DIM, rows), lambda h, t_ref: (h, 0))
    return call(
        attend_back_body,
        "attend_back",
        (heads,),
        [plane] * 3
        + [grad] * 4
        + [
            pl.BlockSpec((4, HEAD_DIM, rows), lambda h, t_ref: (0, h, 0)),
            pl.BlockSpec((1, 1, length), lambda h, t_ref: (h, 0, 0)),
        ]
        + [whole(table) for table in tables],
        pl.BlockSpec((4, 3, 1, rows, LANES), lambda h, t_ref: (0, 0, h, 0, 0)),
        shape_of((4, 3, heads, rows, LANES), BF),
        (t, qe, ke, ve, *grads, ot, lse, *tables),
        scratch=[pltpu.VMEM((LANES, length), BF)] * 3 + [pltpu.VMEM((length, LANES), F32)] * 2,
        prefetch=1,
        flops=heads * length * length * 1280,
    )


def input_back_body(x_ref, dp_ref, w_ref, out_ref, small_ref):
    heads = dp_ref.shape[2]
    grads = jnp.concatenate([dp_ref[0, j // heads, j % heads] for j in range(3 * heads)], 1)
    grad = nt(grads, w_ref[...])
    normed, _ = standardize(x_ref[...].astype(F32))
    out_ref[...] = grad.astype(BF)
    add_rows(small_ref, [column_sum(grad * normed), column_sum(grad)])


def input_back(rel, x, dp, w):
    rows, width = x.shape
    heads = dp.shape[2]
    tile = min(256, rows)
    return call(
        input_back_body,
        f"input_back_{rel}",
        (rows // tile,),
        [
            rows_of(tile, width),
            pl.BlockSpec((1, 3, heads, tile, LANES), lambda i: (rel, 0, 0, i, 0)),
            whole(w),
        ],
        [rows_of(tile, width), pl.BlockSpec((8, width), lambda i: (0, 0))],
        [shape_of((rows, width), BF), shape_of((8, width), F32)],
        (x, dp, w),
        flops=2 * rows * width * w.shape[1],
    )


def qkv_weight_body(dp_ref, a0, a1, a2, a3, out_ref, bias_ref):
    heads = dp_ref.shape[2]
    total, sums = None, None
    for rel, a_ref in enumerate((a0, a1, a2, a3)):
        grads = jnp.concatenate([dp_ref[rel, 0, h] for h in range(heads)], 1)
        part, part_sum = tn(grads, a_ref[...]), column_sum(grads.astype(F32))
        total = part if total is None else total + part
        sums = part_sum if sums is None else sums + part_sum
    for h in range(heads):
        out_ref[h * HEAD_DIM : (h + 1) * HEAD_DIM, :] = total[h * LANES : h * LANES + HEAD_DIM].astype(BF)
    bias_ref[0] = sums


def qkv_weight(dp, normed):
    _, _, heads, rows, _ = dp.shape
    width = normed[0].shape[1]
    local = heads * HEAD_DIM
    return call(
        qkv_weight_body,
        "qkv_weight",
        (3,),
        [pl.BlockSpec((4, 1, heads, rows, LANES), lambda j: (0, j, 0, 0, 0))] + [whole(a) for a in normed],
        [rows_of(local, width), pl.BlockSpec((1, 1, heads * LANES), lambda j: (j, 0, 0))],
        [shape_of((3 * local, width), BF), shape_of((3, 1, heads * LANES), F32)],
        (dp, *normed),
        flops=2 * 4 * rows * 3 * heads * LANES * width,
    )


def after_attend_body(
    x_ref, o0, o1, o2, o3, w0, w1, w2, w3, bias_ref, gain_ref, shift_ref, wq_ref, bq_ref, x1_ref, b_ref, cq_ref
):
    total = x_ref[...].astype(F32) + bias_ref[0:1, :]
    for o_ref, w_ref in ((o0, w0), (o1, w1), (o2, w2), (o3, w3)):
        total = total + tn(o_ref[...], w_ref[...])
    x1_ref[...] = total
    normed, _ = standardize(total)
    b = (normed * gain_ref[1:2, :] + shift_ref[1:2, :]).astype(BF)
    b_ref[...] = b
    weight = wq_ref[...].reshape(-1, wq_ref.shape[2])
    cq_ref[...] = ((nt(b, weight) + bq_ref[...]) * (1.0 / math.sqrt(HEAD_DIM))).astype(BF)


def after_attend(x, mixed, packs, weights, out_bias, gain, shift, bq):
    rows, width = x.shape
    local = mixed[0].shape[0]
    tile = min(256, rows)
    return call(
        after_attend_body,
        "after_attend",
        (rows // tile,),
        [rows_of(tile, width)]
        + [pl.BlockSpec((local, tile), lambda i: (0, i))] * 4
        + [pl.BlockSpec((local, width), lambda i: (1, 0))] * 4
        + [whole(out_bias), whole(gain), whole(shift)]
        + [pl.BlockSpec((4, local, width), lambda i: (0, 0, 0)), whole(bq)],
        [rows_of(tile, width)] * 3,
        [shape_of((rows, width), F32), shape_of((rows, width), BF), shape_of((rows, width), BF)],
        (x, *mixed, *packs, out_bias, gain, shift, weights, bq),
        flops=4 * rows * width * width,
    )


def head_lanes(width):
    heads = width // HEAD_DIM
    count = -(-heads // 16) * 16
    row = lax.broadcasted_iota(jnp.int32, (count, width), 0)
    lane = lax.broadcasted_iota(jnp.int32, (count, width), 1)
    return (lax.shift_right_logical(lane, 6) == row).astype(BF)


def two_parts(values):
    first = values.astype(BF)
    return first, (values - first.astype(F32)).astype(BF)


def merge_parts(first, first_lse, second, second_lse):
    weight = 1.0 / (1.0 + jnp.exp(second_lse - first_lse))
    expand = head_lanes(first.shape[1])
    high, low = two_parts(weight)
    share = tn(high, expand) + tn(low, expand)
    second = second.astype(F32)
    merged = second + share * (first.astype(F32) - second)
    gap = -jnp.abs(first_lse - second_lse)
    return merged, jnp.maximum(first_lse, second_lse) + jnp.log(1.0 + jnp.exp(gap))


def merge_body(a_ref, al_ref, b_ref, bl_ref, out_ref, lse_ref):
    merged, lse = merge_parts(a_ref[0], al_ref[0], b_ref[...], bl_ref[...])
    out_ref[...] = merged.astype(BF)
    lse_ref[...] = lse


def merge(rel, parts, lses, other, other_lse):
    _, rows, width = parts.shape
    count = lses.shape[1]
    tile = min(256, rows)
    return call(
        merge_body,
        f"merge_{rel}",
        (rows // tile,),
        [
            pl.BlockSpec((1, tile, width), lambda i: (rel, i, 0)),
            pl.BlockSpec((1, count, tile), lambda i: (rel, 0, i)),
            rows_of(tile, width),
            pl.BlockSpec((count, tile), lambda i: (0, i)),
        ],
        [rows_of(tile, width), pl.BlockSpec((count, tile), lambda i: (0, i))],
        [shape_of((rows, width), BF), shape_of((count, rows), F32)],
        (parts, lses, other, other_lse),
        flops=4 * rows * width * count,
    )


def after_cross_body(
    a_ref, al_ref, b_ref, bl_ref, x1_ref, w_ref, bias_ref, gain_ref, shift_ref, co_ref, lse_ref, x2_ref, m_ref
):
    merged, lse = merge_parts(a_ref[...], al_ref[...], b_ref[...], bl_ref[...])
    mixed = merged.astype(BF)
    co_ref[...] = mixed
    lse_ref[...] = lse
    weight = w_ref[...].reshape(-1, w_ref.shape[2])
    total = x1_ref[...] + nn(mixed, weight) + bias_ref[1:2, :]
    x2_ref[...] = total
    normed, _ = standardize(total)
    m_ref[...] = (normed * gain_ref[2:3, :] + shift_ref[2:3, :]).astype(BF)


def after_cross(a, a_lse, b, b_lse, x1, weights, local, out_bias, gain, shift):
    rows, width = x1.shape
    count = a_lse.shape[0]
    tile = min(256, rows)
    stats = pl.BlockSpec((count, tile), lambda i: (0, i))
    return call(
        after_cross_body,
        "after_cross",
        (rows // tile,),
        [rows_of(tile, width), stats, rows_of(tile, width), stats, rows_of(tile, width)]
        + [pl.BlockSpec((4, local, width), lambda i: (0, 4, 0)), whole(out_bias), whole(gain), whole(shift)],
        [rows_of(tile, width), stats, rows_of(tile, width), rows_of(tile, width)],
        [
            shape_of((rows, width), BF),
            shape_of((count, rows), F32),
            shape_of((rows, width), F32),
            shape_of((rows, width), BF),
        ],
        (a, a_lse, b, b_lse, x1, weights, out_bias, gain, shift),
        flops=2 * rows * width * width,
    )


def before_cross_body(
    x2_ref, da_ref, db_ref, g_ref, co_ref, w_ref, gain_ref, g2_ref, g2r_ref, dco_ref, delta_ref, small_ref
):
    grad = da_ref[...].astype(F32) + db_ref[...].astype(F32)
    normed, inverse = standardize(x2_ref[...])
    g = g_ref[...]
    g2 = g + norm_pull(grad, normed, inverse, gain_ref[2:3, :])
    g2_ref[...] = g2
    g2r = g2.astype(BF)
    g2r_ref[...] = g2r
    weight = w_ref[...].reshape(-1, w_ref.shape[2])
    dco = nt(g2r, weight).astype(BF)
    dco_ref[...] = dco
    high, low = two_parts(dco.astype(F32) * co_ref[...].astype(F32))
    expand = head_lanes(high.shape[1])
    delta_ref[...] = nt(expand, high) + nt(expand, low)
    add_rows(small_ref, [column_sum(grad * normed), column_sum(grad), column_sum(g), column_sum(g2)])


def before_cross(x2, da, db, g, co, weights, local, gain, count):
    rows, width = x2.shape
    tile = min(256, rows)
    row = rows_of(tile, width)
    return call(
        before_cross_body,
        "before_cross",
        (rows // tile,),
        [row] * 5 + [pl.BlockSpec((4, local, width), lambda i: (0, 4, 0)), whole(gain)],
        [row, row, row, pl.BlockSpec((count, tile), lambda i: (0, i)), pl.BlockSpec((8, width), lambda i: (0, 0))],
        [
            shape_of((rows, width), F32),
            shape_of((rows, width), BF),
            shape_of((rows, width), BF),
            shape_of((count, rows), F32),
            shape_of((8, width), F32),
        ],
        (x2, da, db, g, co, weights, gain),
        flops=2 * rows * width * width,
    )


def before_attend_body(
    x1_ref, qa_ref, qb_ref, g2_ref, wq_ref, w0, w1, w2, w3, gain_ref,
    g1_ref, g1r_ref, dqc_ref, d0, d1, d2, d3, small_ref,
):
    dqc = ((qa_ref[...].astype(F32) + qb_ref[...].astype(F32)) * (1.0 / math.sqrt(HEAD_DIM))).astype(BF)
    dqc_ref[...] = dqc
    grad = nn(dqc, wq_ref[...].reshape(-1, wq_ref.shape[2]))
    normed, inverse = standardize(x1_ref[...])
    g1 = g2_ref[...] + norm_pull(grad, normed, inverse, gain_ref[1:2, :])
    g1_ref[...] = g1
    g1r = g1.astype(BF)
    g1r_ref[...] = g1r
    for w_ref, d_ref in ((w0, d0), (w1, d1), (w2, d2), (w3, d3)):
        d_ref[...] = nt(w_ref[...], g1r).astype(BF)
    add_rows(
        small_ref, [column_sum(grad * normed), column_sum(grad), column_sum(g1), column_sum(dqc.astype(F32))]
    )


def before_attend(x1, qa, qb, g2, weights, packs, local, gain):
    rows, width = x1.shape
    tile = min(256, rows)
    row = rows_of(tile, width)
    turned = pl.BlockSpec((local, tile), lambda i: (0, i))
    return call(
        before_attend_body,
        "before_attend",
        (rows // tile,),
        [row] * 4
        + [pl.BlockSpec((4, local, width), lambda i: (0, 0, 0))]
        + [pl.BlockSpec((local, width), lambda i: (1, 0))] * 4
        + [whole(gain)],
        [row, row, row] + [turned] * 4 + [pl.BlockSpec((8, width), lambda i: (0, 0))],
        [shape_of((rows, width), F32), shape_of((rows, width), BF), shape_of((rows, width), BF)]
        + [shape_of((local, rows), BF)] * 4
        + [shape_of((8, width), F32)],
        (x1, qa, qb, g2, weights, *packs, gain),
        flops=4 * rows * width * width,
    )


def split_pair(values):
    lane = lax.broadcasted_iota(jnp.int32, values.shape, 1)
    zero = jnp.zeros_like(values)
    return jnp.concatenate(
        [jnp.where(lane < HEAD_DIM, values, zero), jnp.where(lane >= HEAD_DIM, values, zero)], 0
    )


def join_pair(values):
    rows = values.shape[0] // 2
    lane = lax.broadcasted_iota(jnp.int32, (rows, values.shape[1]), 1)
    return jnp.where(lane < HEAD_DIM, values[:rows], values[rows:])


def span_place(t, slot, per_span, chunk_rows):
    first = (slot // per_span) * SPAN
    chunk = first // chunk_rows
    return pl.multiple_of((t ^ chunk) * chunk_rows + first - chunk * chunk_rows, SPAN)


def cross_body(t_ref, slot_ref, q0, q1, q2, q3, kv_ref, out_ref, lse_ref, q_ref, o_ref, st_ref, *, per_span):
    t = t_ref[0]
    rows, width = q0.shape
    blocks = slot_ref.shape[0]
    length = kv_ref.shape[0] // blocks
    for rel, ref in enumerate((q0, q1, q2, q3)):
        q_ref[rel * rows : (rel + 1) * rows, :] = ref[...]
    o_ref[...] = jnp.zeros_like(o_ref)
    st_ref[...] = jnp.full_like(st_ref, NEGATIVE)

    def one_block(p, carry):
        place = pl.ds(span_place(t, slot_ref[p], per_span, rows), SPAN)
        keys = pl.ds(pl.multiple_of(p * length, length), length)
        stats = st_ref[place, :]
        lane = lax.broadcasted_iota(jnp.int32, stats.shape, 1)
        pair_lane = lax.broadcasted_iota(jnp.int32, (SPAN, LANES), 1)
        fresh = stats
        for j in range(width // LANES):
            cut = slice(j * LANES, (j + 1) * LANES)
            scores = nt(split_pair(q_ref[place, cut]), kv_ref[keys, cut])
            top = jnp.max(scores, 1, keepdims=True)
            shifted = jnp.exp(scores - top)
            total = jnp.sum(shifted, 1, keepdims=True)
            value_cut = slice(width + j * LANES, width + (j + 1) * LANES)
            mixed = join_pair(nn(shifted.astype(BF), kv_ref[keys, value_cut]) / total)
            own = top + jnp.log(total)
            shares = []
            for side in range(2):
                mine = own[side * SPAN : (side + 1) * SPAN]
                head = 2 * j + side
                before = jnp.sum(jnp.where(lane == head, stats, 0.0), 1, keepdims=True)
                shares.append(1.0 / (1.0 + jnp.exp(before - mine)))
                both = jnp.maximum(mine, before) + jnp.log(1.0 + jnp.exp(-jnp.abs(mine - before)))
                fresh = jnp.where(lane == head, both, fresh)
            share = jnp.where(pair_lane < HEAD_DIM, shares[0], shares[1])
            old = o_ref[place, cut]
            o_ref[place, cut] = old + share * (mixed - old)
        st_ref[place, :] = fresh
        return carry

    lax.fori_loop(0, blocks, one_block, 0)
    for rel in range(4):
        place = slice(rel * rows, (rel + 1) * rows)
        out_ref[rel] = o_ref[place, :].astype(BF)
        lse_ref[rel] = st_ref[place, :].T[: lse_ref.shape[1]]


def cross(t, slots, queries, kv, per_span, count):
    rows, width = queries[0].shape
    return call(
        functools.partial(cross_body, per_span=per_span),
        "cross",
        (1,),
        [whole(q) for q in queries] + [whole(kv)],
        [
            pl.BlockSpec((4, rows, width), lambda *_: (0, 0, 0)),
            pl.BlockSpec((4, count, rows), lambda *_: (0, 0, 0)),
        ],
        [shape_of((4, rows, width), BF), shape_of((4, count, rows), F32)],
        (t, slots, *queries, kv),
        scratch=[
            pltpu.VMEM((4 * rows, width), BF),
            pltpu.VMEM((4 * rows, width), F32),
            pltpu.VMEM((4 * rows, LANES), F32),
        ],
        prefetch=2,
        flops=8 * kv.shape[0] * SPAN * width,
    )


def cross_back_body(
    t_ref, slot_ref, q0, q1, q2, q3, d0, d1, d2, d3, s0, s1, s2, s3, kv_ref, dkv_ref, dq_ref,
    q_ref, d_ref, st_ref, acc_ref, *, per_span,
):
    t = t_ref[0]
    rows, width = q0.shape
    blocks = slot_ref.shape[0]
    length = kv_ref.shape[0] // blocks
    count = s0.shape[0]
    for rel, (a, b, c) in enumerate(zip((q0, q1, q2, q3), (d0, d1, d2, d3), (s0, s1, s2, s3))):
        place = slice(rel * rows, (rel + 1) * rows)
        q_ref[place, :] = a[...]
        d_ref[place, :] = b[...]
        filler = jnp.zeros((LANES - count, rows), F32)
        st_ref[place, :] = jnp.concatenate([c[...], filler], 0).T
    acc_ref[...] = jnp.zeros_like(acc_ref)

    def one_block(p, carry):
        place = pl.ds(span_place(t, slot_ref[p], per_span, rows), SPAN)
        keys = pl.ds(pl.multiple_of(p * length, length), length)
        stats = st_ref[place, :]
        lane = lax.broadcasted_iota(jnp.int32, stats.shape, 1)

        def column(index):
            return jnp.sum(jnp.where(lane == index, stats, 0.0), 1, keepdims=True)

        for j in range(width // LANES):
            cut = slice(j * LANES, (j + 1) * LANES)
            value_cut = slice(width + j * LANES, width + (j + 1) * LANES)
            query, grad = split_pair(q_ref[place, cut]), split_pair(d_ref[place, cut])
            key, value = kv_ref[keys, cut], kv_ref[keys, value_cut]
            lse = jnp.concatenate([column(2 * j), column(2 * j + 1)], 0)
            delta = jnp.concatenate([column(count // 2 + 2 * j), column(count // 2 + 2 * j + 1)], 0)
            prob = jnp.exp(nt(query, key) - lse)
            grad_scores = (prob * (nt(grad, value) - delta)).astype(BF)
            dkv_ref[keys, cut] = tn(grad_scores, query).astype(BF)
            dkv_ref[keys, value_cut] = tn(prob.astype(BF), grad).astype(BF)
            acc_ref[place, cut] += join_pair(nn(grad_scores, key))
        return carry

    lax.fori_loop(0, blocks, one_block, 0)
    for rel in range(4):
        dq_ref[rel] = acc_ref[rel * rows : (rel + 1) * rows, :].astype(BF)


def cross_back(t, slots, queries, grads, stats, kv, per_span):
    rows, width = queries[0].shape
    return call(
        functools.partial(cross_back_body, per_span=per_span),
        "cross_back",
        (1,),
        [whole(q) for q in (*queries, *grads, *stats)] + [whole(kv)],
        [pl.BlockSpec(kv.shape, lambda *_: (0, 0)), pl.BlockSpec((4, rows, width), lambda *_: (0, 0, 0))],
        [shape_of(kv.shape, BF), shape_of((4, rows, width), BF)],
        (t, slots, *queries, *grads, *stats, kv),
        scratch=[
            pltpu.VMEM((4 * rows, width), BF),
            pltpu.VMEM((4 * rows, width), BF),
            pltpu.VMEM((4 * rows, LANES), F32),
            pltpu.VMEM((4 * rows, width), F32),
        ],
        prefetch=2,
        flops=20 * kv.shape[0] * SPAN * width,
    )


def feed_body(m_ref, g_ref, w1_ref, w2_ref, b1_ref, out_ref, dm_ref, h_ref, du_ref, db_ref):
    u = nn(m_ref[...], w1_ref[...]) + b1_ref[...]
    curve = math.sqrt(2.0 / math.pi)
    square = u * u
    bent = jnp.tanh(curve * (u + 0.044715 * u * square))
    half = 0.5 * (1.0 + bent)
    h = (u * half).astype(BF)
    h_ref[...] = h
    out_ref[...] = nn(h, w2_ref[...]).astype(BF)
    slope = half + 0.5 * u * (1.0 - bent * bent) * (curve * (1.0 + 3.0 * 0.044715 * square))
    du = (nt(g_ref[...], w2_ref[...]) * slope).astype(BF)
    du_ref[...] = du
    dm_ref[...] = nt(du, w1_ref[...]).astype(BF)
    add_rows(db_ref, [column_sum(du.astype(F32))])


def feed(rel, m, g, w1, w2, b1):
    rows, width = m.shape
    hidden = w1.shape[1]
    tile = min(256, rows)
    return call(
        feed_body,
        f"feed_{rel}",
        (rows // tile,),
        [rows_of(tile, width)] * 2 + [whole(w1), whole(w2), whole(b1)],
        [rows_of(tile, width)] * 2 + [rows_of(tile, hidden)] * 2 + [pl.BlockSpec((8, hidden), lambda i: (0, 0))],
        [shape_of((rows, width), BF)] * 2 + [shape_of((rows, hidden), BF)] * 2 + [shape_of((8, hidden), F32)],
        (m, g, w1, w2, b1),
        flops=8 * rows * width * hidden,
    )


def weight_body(*refs):
    count = (len(refs) - 1) // 2
    total = None
    for left, right in zip(refs[:count], refs[count:-1]):
        part = tn(left[...], right[...])
        total = part if total is None else total + part
    refs[-1][...] = total.astype(BF)


def weight(name, lefts, rights):
    rows, out_rows = lefts[0].shape
    width = rights[0].shape[1]
    tile = 256
    return call(
        weight_body,
        name,
        (out_rows // tile,),
        [pl.BlockSpec((rows, tile), lambda i: (0, i))] * len(lefts) + [whole(r) for r in rights],
        rows_of(tile, width),
        shape_of((out_rows, width), BF),
        (*lefts, *rights),
        flops=2 * len(lefts) * rows * out_rows * width,
    )


def cross_weight_body(
    t_ref, dqc_ref, b_ref, o0, o1, o2, o3, g1_ref, dkv_ref, memory_ref, co_ref, g2_ref, out_ref, bias_ref
):
    t = t_ref[0]
    local = out_ref.shape[2]
    width = out_ref.shape[3]

    def place(index, grad):
        for group in range(4):
            out_ref[t ^ group, index] = grad[group * local : (group + 1) * local].astype(BF)

    place(0, tn(dqc_ref[...], b_ref[...]))
    for rel, o_ref in enumerate((o0, o1, o2, o3)):
        out_ref[rel, 1] = nn(o_ref[...], g1_ref[...]).astype(BF)
    place(2, tn(dkv_ref[:, :width], memory_ref[...]))
    place(3, tn(dkv_ref[:, width:], memory_ref[...]))
    place(4, tn(co_ref[...], g2_ref[...]))
    bias_ref[...] = column_sum(dkv_ref[:, width:].astype(F32))


def cross_weight(t, dqc, b, mixed, g1r, dkv, memory, co, g2r):
    width = b.shape[1]
    local = mixed[0].shape[0]
    args = (dqc, b, *mixed, g1r, dkv, memory, co, g2r)
    return call(
        cross_weight_body,
        "cross_weight",
        (1,),
        [whole(a) for a in args],
        [
            pl.BlockSpec((4, 5, local, width), lambda *_: (0, 0, 0, 0)),
            pl.BlockSpec((1, width), lambda *_: (0, 0)),
        ],
        [shape_of((4, 5, local, width), BF), shape_of((1, width), F32)],
        (t, *args),
        prefetch=1,
        flops=2 * width * width * (3 * b.shape[0] + 2 * memory.shape[0]),
    )


def input_grad_body(x_ref, da_ref, db_ref, g1_ref, gain_ref, out_ref):
    normed, inverse = standardize(x_ref[...].astype(F32))
    grad = da_ref[...].astype(F32) + db_ref[...].astype(F32)
    out_ref[...] = g1_ref[...] + norm_pull(grad, normed, inverse, gain_ref[0:1, :])


def input_grad(x, da, db, g1, gain):
    rows, width = x.shape
    tile = min(256, rows)
    row = rows_of(tile, width)
    return call(
        input_grad_body,
        "input_grad",
        (rows // tile,),
        [row] * 4 + [whole(gain)],
        row,
        shape_of((rows, width), F32),
        (x, da, db, g1, gain),
        flops=rows * width * 16,
    )


def padded_tables(length):
    half = HEAD_DIM // 2
    frequency = 10000.0 ** (-jnp.arange(half, dtype=F32) / half)
    angles = jnp.arange(length, dtype=F32)[:, None] * frequency[None, :]
    cosine, sine = jnp.cos(angles), jnp.sin(angles)
    zero = jnp.zeros_like(sine)
    return (
        jnp.concatenate([cosine, cosine, zero, zero], 1),
        jnp.concatenate([-sine, zero, zero, zero], 1),
        jnp.concatenate([zero, sine, zero, zero], 1),
    )


def mask_lanes(segments):
    lane = lax.broadcasted_iota(jnp.int32, (segments.shape[0], LANES), 1)
    is_mask = (lane >= MASK_LANE) & (lane < MASK_LANE + DOCS)
    same = is_mask & (lane - MASK_LANE == segments[:, None])
    is_lse = (lane >= LSE_LANE) & (lane < LSE_LANE + 3)
    query_lanes = jnp.where(same, 1.0, 0.0).astype(BF)
    key_lanes = jnp.where(is_mask & ~same, NEGATIVE, jnp.where(is_lse, 1.0, 0.0)).astype(BF)
    return query_lanes, key_lanes


def pad_heads(values):
    lead = values.shape[:-1]
    heads = values.shape[-1] // HEAD_DIM
    values = values.reshape(lead + (heads, HEAD_DIM))
    values = jnp.pad(values, [(0, 0)] * (len(lead) + 1) + [(0, LANES - HEAD_DIM)])
    return values.reshape(lead[:-1] + (-1,))


def shards(
    layer_input,
    norm_gain,
    norm_bias,
    self_input_weight,
    self_input_bias,
    self_output_weight,
    out_bias,
    cross_query_weight,
    b_cross_q,
    w_cross_kv,
    b_cross_v,
    cross_output_weight,
    expand_weight_1,
    expand_bias_1,
    contract_weight_2,
    neighbours,
    segment_ids,
    span_map,
    cotangent,
):
    x = layer_input[0]
    rows, width = x.shape
    length = segment_ids.shape[1]
    local = self_input_weight.shape[2]
    heads = local // HEAD_DIM
    all_heads = width // HEAD_DIM
    count = -(-all_heads // 16) * 16
    blocks, block_rows = neighbours.shape[1], neighbours.shape[2]
    per_span = span_map.shape[1] // (length // SPAN)
    memory = neighbours[0].reshape(blocks * block_rows, width)
    grad_out = cotangent[0]
    index = lax.axis_index("tp")
    t = index.astype(jnp.int32).reshape(1)
    partners = [[(i, i ^ step) for i in range(4)] for step in (1, 2, 3)]

    xs = spread(x, partners)
    bias_parts = []
    for bias in (b_cross_q, b_cross_v):
        high = lax.reduce_precision(bias, 8, 7)
        bias_parts += [high, bias - high]
    pack = jnp.concatenate(
        [
            cross_query_weight.T,
            self_output_weight,
            w_cross_kv[:, 0].T,
            w_cross_kv[:, 1].T,
            cross_output_weight,
            jnp.pad(jnp.concatenate(bias_parts).astype(BF)[None], ((0, 15), (0, 0))),
        ],
        0,
    )
    pack, _ = lax.optimization_barrier((pack, xs[2]))
    packs = spread(pack, partners)
    gathered, _ = lax.optimization_barrier((grad_out.astype(BF), packs[2]))
    gs = spread(gathered, partners)

    tables = padded_tables(length)
    w_pad = pad_heads(self_input_weight)
    b_pad = pad_heads(self_input_bias)[None]
    normed_first, chunks = [], []
    for rel in range(4):
        a, chunk = project_rows(rel, t, xs[rel], norm_gain, norm_bias, w_pad, b_pad, tables, heads)
        normed_first.append(a)
        chunks.append(chunk)
    qx, kx = mask_lanes(segment_ids[0])
    lane = lax.broadcasted_iota(jnp.int32, (1, LANES), 1)
    vx = jnp.where((lane >= HEAD_DIM) & (lane < HEAD_DIM + 3), 1.0, 0.0).astype(BF)
    qe, ke, ve, ot, lse = attend(t, chunks, qx, kx, vx)
    mixed = exchange([ot[0], ot[1], ot[2], ot[3]], partners)

    weights = jnp.zeros((4,) + pack.shape, BF)
    for rel in range(4):
        weights = lax.dynamic_update_slice(weights, packs[rel][None], (index ^ rel, 0, 0))
    bias_rows = weights[:, 5 * local].astype(F32).reshape(4, 4, local)
    bq = (bias_rows[:, 0] + bias_rows[:, 1]).reshape(1, width)
    bv = (bias_rows[:, 2] + bias_rows[:, 3]).reshape(1, width)
    weight_kv = jnp.concatenate(
        [weights[:, k * local : (k + 1) * local].reshape(width, width) for k in (2, 3)], 0
    )
    memory_kv = (
        lax.dot_general(memory, weight_kv, (((1,), (1,)), ((), ())), preferred_element_type=F32)
        + jnp.concatenate([jnp.zeros_like(bv), bv], 1)
    ).astype(BF)
    block_ids = index * blocks + jnp.arange(blocks, dtype=jnp.int32)
    slot_ids = jnp.arange(span_map.shape[1], dtype=jnp.int32)
    slots = jnp.sum(jnp.where(span_map[0][None, :] == block_ids[:, None], slot_ids[None, :], 0), 1)

    x1, b, cq = after_attend(x, mixed, packs, weights, out_bias, norm_gain, norm_bias, bq)
    queries = spread(cq, partners)
    parts, part_lse = cross(t, slots, queries, memory_kv, per_span, count)
    core, chip, _ = partners
    far, far_lse = lax.ppermute(parts[3], "tp", core), lax.ppermute(part_lse[3], "tp", core)
    near, near_lse = lax.ppermute(parts[1], "tp", core), lax.ppermute(part_lse[1], "tp", core)
    sent, sent_lse = merge(2, parts, part_lse, far, far_lse)
    across, across_lse = lax.ppermute(sent, "tp", chip), lax.ppermute(sent_lse, "tp", chip)
    kept, kept_lse = merge(0, parts, part_lse, near, near_lse)
    co, cross_lse, x2, m = after_cross(
        kept, kept_lse, across, across_lse, x1, weights, local, out_bias, norm_gain, norm_bias
    )

    ms = spread(m, partners)
    fed = [
        feed(rel, ms[rel], gs[rel], expand_weight_1, contract_weight_2, expand_bias_1[None])
        for rel in range(4)
    ]
    dm = collect([f[1] for f in fed], partners)
    out = collect([f[0] for f in fed], partners)
    grad_w1 = weight("weight_1", ms, [f[3] for f in fed])
    grad_w2 = weight("weight_2", [f[2] for f in fed], gs)
    grad_b1 = fed[0][4] + fed[1][4] + fed[2][4] + fed[3][4]
    summed_feed = lax.psum(jnp.concatenate([grad_w1, grad_w2, grad_b1.astype(BF)], 0), "dp")
    layer_output = x2 + (out[0].astype(F32) + out[1].astype(F32)) + out_bias[2]

    g2, g2r, dco, delta, small_two = before_cross(
        x2, dm[0], dm[1], grad_out, co, weights, local, norm_gain, count
    )
    grads = spread(dco, partners)
    half = count
    stats = spread(jnp.concatenate([cross_lse[:half], delta[:half]], 0), partners)
    dkv, dq_parts = cross_back(t, slots, queries, grads, stats, memory_kv, per_span)
    dq = collect([dq_parts[r] for r in range(4)], partners)
    grad_memory = lax.dot_general(
        dkv, weight_kv, (((1,), (0,)), ((), ())), preferred_element_type=F32
    ).reshape(neighbours.shape)
    g1, g1r, dqc, *dos, small_one = before_attend(x1, dq[0], dq[1], g2, weights, packs, local, norm_gain)

    dos = exchange(dos, partners)
    grad_cross, grad_bv = cross_weight(t, dqc, b, mixed, g1r, dkv, memory, co, g2r)
    dp = attend_back(t, qe, ke, ve, dos, ot, lse, tables)
    grad_rows = [input_back(rel, xs[rel], dp, w_pad) for rel in (3, 1, 2, 0)][::-1]
    grad_rows = [grad_rows[0], grad_rows[2], grad_rows[1], grad_rows[3]]
    da = collect([g[0] for g in grad_rows], partners)
    grad_qkv, grad_bqkv = qkv_weight(dp, normed_first)
    grad_input = input_grad(x, da[0], da[1], g1, norm_gain)

    grad_far = lax.ppermute(jnp.stack([grad_cross[1], grad_cross[3]]), "tp", core)
    sent = (grad_cross[2].astype(F32) + grad_far[1].astype(F32)).astype(BF)
    across = lax.ppermute(sent, "tp", chip)
    own = (grad_cross[0].astype(F32) + grad_far[0].astype(F32) + across.astype(F32)).astype(BF)
    small_zero = grad_rows[0][1] + grad_rows[1][1] + grad_rows[2][1] + grad_rows[3][1]
    small = jnp.concatenate([small_zero[:2], small_one[:4], small_two[:4], grad_bv, jnp.zeros((5, width), F32)], 0)
    small = small + lax.ppermute(small, "tp", core)
    small = small + lax.ppermute(small, "tp", chip)
    bqkv_row = jnp.pad(grad_bqkv.reshape(3, heads, LANES)[:, :, :HEAD_DIM].reshape(1, -1), ((0, 15), (0, width - 3 * local)))
    last = jnp.concatenate([grad_qkv, own.reshape(5 * local, width), small.astype(BF), bqkv_row.astype(BF)], 0)
    last, summed_feed = lax.optimization_barrier((last, summed_feed))
    summed = lax.psum(last, "dp").astype(F32)

    summed_feed = summed_feed.astype(F32)
    hidden = expand_weight_1.shape[1]
    grad_w1, grad_w2, grad_b1 = summed_feed[:width], summed_feed[width : width + hidden], summed_feed[width + hidden]
    grad_qkv = summed[: 3 * local].T.reshape(width, 3, local)
    own = summed[3 * local : 8 * local].reshape(5, local, width)
    small = summed[8 * local : 8 * local + 16]
    bqkv = summed[8 * local + 16, : 3 * local].reshape(3, local)

    def mine(row):
        return lax.dynamic_slice_in_dim(row, index * local, local, 0)

    return (
        layer_output[None],
        grad_input[None],
        grad_memory,
        jnp.stack([small[0], small[2], small[6]]),
        jnp.stack([small[1], small[3], small[7]]),
        grad_qkv,
        bqkv,
        own[1],
        jnp.stack([small[4], small[9], small[8]]),
        own[0].T,
        mine(small[5]),
        jnp.stack([own[2].T, own[3].T], 1),
        mine(small[10]),
        own[4],
        grad_w1,
        grad_b1,
        grad_w2,
    )


def solution(mesh):
    return jax.shard_map(
        shards,
        mesh=mesh,
        in_specs=(
            P("dp", "tp", None),
            P(),
            P(),
            P(None, None, "tp"),
            P(None, "tp"),
            P("tp", None),
            P(),
            P(None, "tp"),
            P("tp"),
            P(None, None, "tp"),
            P("tp"),
            P("tp", None),
            P(None, "tp"),
            P("tp"),
            P("tp", None),
            P("dp", "tp", None, None),
            P("dp", None),
            P("dp", None),
            P("dp", "tp", None),
        ),
        out_specs=(
            P("dp", "tp", None),
            P("dp", "tp", None),
            P("dp", "tp", None, None),
            P(),
            P(),
            P(None, None, "tp"),
            P(None, "tp"),
            P("tp", None),
            P(),
            P(None, "tp"),
            P("tp"),
            P(None, None, "tp"),
            P("tp"),
            P("tp", None),
            P(None, "tp"),
            P("tp"),
            P("tp", None),
        ),
        check_vma=False,
    )
```

time: 1480 us -> 664 us (0.45)
  waiting for transfers between devices: 687 us -> 257 us
  matrix products: 307 us -> 17.4 us
  Pallas kernels: 0 us -> 242 us
  other arithmetic: 182 us -> 42.7 us
  local copies, waits for them, and re-layouts: 185 us -> 52.4 us
  blocking collectives: 77.4 us -> 0 us
  starting transfers between devices: 1.43 us -> 30.5 us
    dot_general x52 -> x2, matrix products: 288 us -> 17.4 us  [the longest x1 9.61 us: shards(): lax.dot_general(dkv, weight_kv, (((1,), (0,)), ((), ())), preferred_eleme...]
    pallas_call x0 -> x27, Pallas kernels: none -> 242 us  [call(): pl.pallas_call(body, out_shape=out_shape, grid_spec=pltpu.PrefetchScalarG...]
    all_gather x7 -> x0, waiting for transfers between devices: 239 us -> none  [the longest x6 163 us: spread_rows(): return lax.all_gather(values, 'tp', axis=1, tiled=True)]
    reduce_scatter x7 -> x0, waiting for transfers between devices: 177 us -> none  [the longest x6 177 us: collect_rows(): lax.psum_scatter(values.astype(jnp.bfloat16), 'tp', scatter_dimension=1,...]
    psum x1 -> x2, waiting for transfers between devices: 270 us -> 121 us  [the longest x1 93.7 us: shards(): summed = lax.psum(last, 'dp').astype(F32)]
    ppermute x0 -> x49, waiting for transfers between devices: none -> 136 us  [the longest x7 74.8 us: spread(): across = lax.ppermute(values, 'tp', chip)]
    psum x2 -> x0, blocking collectives: 77.4 us -> none  [the longest x1 40.2 us: shards(): lax.psum((jnp.stack([grad_gain_zero, grad_gain_one, grad_gain_two]), jnp....]
    reduce_sum x20 -> x1, other arithmetic: 64.7 us -> 0.69 us  [shards(): jnp.sum(jnp.where(span_map[0][None, :] == block_ids[:, None], slot_ids[No...]
  transfers between devices with their start and end apart: 15 -> 51, of which waited for: 13 -> 22; matrix products, arithmetic and copies ran while one was open for 14% -> 13% of each run, Pallas kernels for 0% -> 24%
where the time goes in v1:
time: 664 us; the launch traced here: 658 us
  waiting for transfers between devices  257 us (39%)
  Pallas kernels  242 us (36%)
  local copies, waits for them, and re-layouts  52.4 us (8%)
  other arithmetic  42.7 us (6%)
  starting transfers between devices  30.5 us (5%)
  matrix products  17.4 us (3%)
  between operations  15 us (2%)
    pallas_call x27, Pallas kernels, call(): pl.pallas_call(body, out_shape=out_shape, grid_spec=pltpu.PrefetchScalarG...  242 us
    psum x1, waiting for transfers between devices, shards(): summed = lax.psum(last, 'dp').astype(F32)  93.7 us
    ppermute x7, waiting for transfers between devices, spread(): across = lax.ppermute(values, 'tp', chip)  74.8 us
    psum x1, waiting for transfers between devices, shards(): lax.psum(jnp.concatenate([grad_w1, grad_w2, grad_b1.astype(BF)], 0), 'dp')  27.4 us
    ppermute x4, waiting for transfers between devices, collect(): across = lax.ppermute(sent, 'tp', chip)  27.3 us
    unnamed x132, local copies, waits for them, and re-layouts  18.4 us
  transfers between devices with their start and end apart: 51, of which 22 were waited for; matrix products, arithmetic and copies ran while one was open for 13% of the time, Pallas kernels for 24%

profile of v1, /device:TPU:0, one launch (start us, length us, event | category | flops | bytes accessed | tf_op | source)
XLA Modules:
  0.0 657.9 jit_solution(10969021533821683427)
XLA Ops:
  20.8 7.2 %collective-permute-done.1.x_ref = bf16[512,768]{1,0:T(8,128)(2,1)S(1)} collective-permute-done((bf16[512,768]{1,0:T(8,128)(2,1)}, bf16[512,768]{1,0:T(8,128)(2,1)S(1)}, u32[]{:S(2)}, u32[]{:S(2)}) %collective-permute-start.1) | collective-permute-done | bytes 786464 | tf_op jit(solution)/shard_map/ppermute | solution.py:102
  66.9 18.0 %attend.1 = (bf16[3,2048,128]{2,1,0:T(8,128)(2,1)}, bf16[3,2048,128]{2,1,0:T(8,128)(2,1)}, bf16[3,2048,128]{2,1,0:T(8,128)(2,1)}, bf16[4,192,512]{2,1,0:T(8,128)(2,1)}, f32[3,1,2048]{2,1,0:T(1,128)}) custom-call(s32[1]{0:T(128)} %bitcast.t_ref, bf16[3,3,512,128]{3,2,1,0:T(8,128)(2,1)} %get-tuple-element.94.c0, ...), custom_call_target="tpu_custom_call" | custom-call | flops 6442450944 | bytes 11297028 | tf_op jit(solution)/shard_map/attend/pallas_call | solution.py:41
  108.9 15.3 %collective-permute-done.10.q2 = bf16[512,768]{1,0:T(8,128)(2,1)S(1)} collective-permute-done((bf16[512,768]{1,0:T(8,128)(2,1)}, bf16[512,768]{1,0:T(8,128)(2,1)S(1)}, u32[]{:S(2)}, u32[]{:S(2)}) %collective-permute-start.10) | collective-permute-done | bytes 786464 | tf_op jit(solution)/shard_map/ppermute | solution.py:102
  124.2 7.8 %fusion.kv_ref = bf16[2048,1536]{1,0:T(8,128)(2,1)} fusion(bf16[2048,768]{1,0:T(8,128)(2,1)S(1)} %bitcast.108, f32[1536]{0:T(1024)S(1)} %pad_reduce_fusion, bf16[768,768]{1,0:T(8,128)(2,1)S(1)} %bitcast.99, bf16[768,768]{1,0:T(8,128)(2,1)S(1)} %bitcast.97), kind=kOutput, calls=%fused_computation.1 | convolution fusion | flops 4842848256 | bytes 11802624 | tf_op jit(solution)/shard_map/dot_general | solution.py:957
  133.7 33.3 %cross.1 = (bf16[4,512,768]{2,1,0:T(8,128)(2,1)}, f32[4,16,512]{2,1,0:T(8,128)}) custom-call(s32[1]{0:T(128)} %bitcast.t_ref, s32[16]{0:T(128)} %select_reduce_fusion.slot_ref, bf16[512,768]{1,0:T(8,128)(2,1)} %get-tuple-element.100.q0, bf16[512,768]{1,0:T(8,128)(2,1)} %copy-done.7, bf16[512,768]{1,0:T(8,128)(2,1)} %copy-done.6, bf16[512,768]{1,0:T(8,128)(2,1)} %copy-done.8, ...), custom_call_target="tpu_custom_call" | custom-call | flops 805306368 | bytes 12714052 | tf_op jit(solution)/shard_map/cross/pallas_call | solution.py:41
  183.4 13.3 %collective-permute-done.17.bl_ref = f32[16,512]{1,0:T(8,128)S(1)} collective-permute-done((f32[16,512]{1,0:T(8,128)}, f32[16,512]{1,0:T(8,128)S(1)}, u32[]{:S(2)}, u32[]{:S(2)}) %collective-permute-start.17) | collective-permute-done | bytes 32800 | tf_op jit(solution)/shard_map/ppermute | solution.py:971
  204.1 9.4 %collective-permute-done.22.g_ref.refs_6_ = bf16[512,768]{1,0:T(8,128)(2,1)S(1)} collective-permute-done((bf16[512,768]{1,0:T(8,128)(2,1)S(1)}, bf16[512,768]{1,0:T(8,128)(2,1)S(1)}, u32[]{:S(2)}, u32[]{:S(2)}) %collective-permute-start.22) | collective-permute-done | bytes 786464 | tf_op jit(solution)/shard_map/ppermute | solution.py:102
  213.5 16.3 %collective-permute-done.21.m_ref.refs_2_ = bf16[512,768]{1,0:T(8,128)(2,1)S(1)} collective-permute-done((bf16[512,768]{1,0:T(8,128)(2,1)}, bf16[512,768]{1,0:T(8,128)(2,1)S(1)}, u32[]{:S(2)}, u32[]{:S(2)}) %collective-permute-start.21) | collective-permute-done | bytes 786464 | tf_op jit(solution)/shard_map/ppermute | solution.py:102
  248.2 6.5 feed_2.1
  266.1 9.6 %collective-permute-done.29.db_ref = bf16[512,768]{1,0:T(8,128)(2,1)S(1)} collective-permute-done((bf16[512,768]{1,0:T(8,128)(2,1)S(1)}, bf16[512,768]{1,0:T(8,128)(2,1)S(1)}, u32[]{:S(2)}, u32[]{:S(2)}) %collective-permute-start.29) | collective-permute-done | bytes 786464 | tf_op jit(solution)/shard_map/ppermute | solution.py:112
  276.7 6.4 before_cross.1
  284.6 17.6 %collective-permute-done.31.d2 = bf16[512,768]{1,0:T(8,128)(2,1)S(1)} collective-permute-done((bf16[512,768]{1,0:T(8,128)(2,1)}, bf16[512,768]{1,0:T(8,128)(2,1)S(1)}, u32[]{:S(2)}, u32[]{:S(2)}) %collective-permute-start.31) | collective-permute-done | bytes 786464 | tf_op jit(solution)/shard_map/ppermute | solution.py:102
  310.6 35.9 %cross_back.1 = (bf16[2048,1536]{1,0:T(8,128)(2,1)}, bf16[4,512,768]{2,1,0:T(8,128)(2,1)}) custom-call(s32[1]{0:T(128)} %bitcast.t_ref, s32[16]{0:T(128)} %select_reduce_fusion.slot_ref, bf16[512,768]{1,0:T(8,128)(2,1)} %get-tuple-element.100.q0, bf16[512,768]{1,0:T(8,128)(2,1)} %copy-done.7, bf16[512,768]{1,0:T(8,128)(2,1)} %copy-done.6, ...), custom_call_target="tpu_custom_call" | custom-call | flops 2013265920 | bytes 22282308 | tf_op jit(solution)/shard_map/cross_back/pallas_call | solution.py:41
  355.6 16.9 %collective-permute-done.38.qb_ref = bf16[512,768]{1,0:T(8,128)(2,1)S(1)} collective-permute-done((bf16[512,768]{1,0:T(8,128)(2,1)S(1)}, bf16[512,768]{1,0:T(8,128)(2,1)S(1)}, u32[]{:S(2)}, u32[]{:S(2)}) %collective-permute-start.38) | collective-permute-done | bytes 786464 | tf_op jit(solution)/shard_map/ppermute | solution.py:112
  373.4 6.8 %before_attend.1 = (f32[512,768]{1,0:T(8,128)}, bf16[512,768]{1,0:T(8,128)(2,1)}, bf16[512,768]{1,0:T(8,128)(2,1)}, bf16[192,512]{1,0:T(8,128)(2,1)}, bf16[192,5...) custom-call(f32[512,768]{1,0:T(8,128)} %get-tuple-element.107.x1_ref, ...), custom_call_target="tpu_custom_call" | custom-call | flops 1207959552 | bytes 20677632 | tf_op jit(solution)/shard_map/before_attend/pallas_call | solution.py:41
  380.2 14.7 %cross_weight.1 = (bf16[4,5,192,768]{3,2,1,0:T(8,128)(2,1)}, f32[1,768]{1,0:T(1,128)}) custom-call(s32[1]{0:T(128)} %bitcast.t_ref, bf16[512,768]{1,0:T(8,128)(2,1)} %get-tuple-element.144.dqc_ref, bf16[512,768]{1,0:T(8,128)(2,1)} %get-tuple-element.145.b_ref, bf16[192,512]{1,0:T(8,128)(2,1)} %get-tuple-element.204.o0, ...), custom_call_target="tpu_custom_call" | custom-call | flops 6643777536 | bytes 20057092 | tf_op jit(solution)/shard_map/cross_weight/pallas_call | solution.py:41
  401.3 6.4 weight_2.1
  407.8 6.5 weight_1.1
  429.3 25.3 %attend_back.1.dp_ref = bf16[4,3,3,512,128]{4,3,2,1,0:T(8,128)(2,1)} custom-call(s32[1]{0:T(128)} %bitcast.t_ref, bf16[3,2048,128]{2,1,0:T(8,128)(2,1)} %get-tuple-element.115.qe_ref, bf16[3,2048,128]{2,1,0:T(8,128)(2,1)} %get-tuple-element.116.ke_ref, bf16[3,2048,128]{2,1,0:T(8,128)(2,1)} %get-tuple-element.117.ve_ref, ...), custom_call_target="tpu_custom_call" | custom-call | flops 16106127360 | bytes 14180356 | tf_op jit(solution)/shard_map/attend_back/pallas_call | solution.py:41
  475.5 7.7 %qkv_weight.1 = (bf16[576,768]{1,0:T(8,128)(2,1)}, f32[3,1,384]{2,1,0:T(1,128)}) custom-call(bf16[4,3,3,512,128]{4,3,2,1,0:T(8,128)(2,1)} %attend_back.1.dp_ref, bf16[512,768]{1,0:T(8,128)(2,1)} %get-tuple-element.139.a0, bf16[512,768]{1,0:T(8,128)(2,1)} %get-tuple-element.140.a1, bf16[512,768]{1,0:T(8,128)(2,1)} %get-tuple-element.141.a2, ...), custom_call_target="tpu_custom_call" | custom-call | flops 3623878656 | bytes 8753664 | tf_op jit(solution)/shard_map/qkv_weight/pallas_call | solution.py:41
  485.6 7.3 %collective-permute-done.48 = f32[16,768]{1,0:T(8,128)S(1)} collective-permute-done((f32[16,768]{1,0:T(8,128)S(1)}, f32[16,768]{1,0:T(8,128)S(1)}, u32[]{:S(2)}, u32[]{:S(2)}) %collective-permute-start.48) | collective-permute-done | bytes 49184 | tf_op jit(solution)/shard_map/ppermute | solution.py:1019
  500.3 27.4 %all-reduce.9.cloned.1.call-done = bf16[1544,768]{1,0:T(8,128)(2,1)} async-done(((bf16[1544,768]{1,0:T(8,128)(2,1)}), bf16[1544,768]{1,0:T(8,128)(2,1)}) %all-reduce.9.cloned.1.call-update) | async-done | bytes 2371600 | tf_op jit(solution)/shard_map/psum | solution.py:987
  527.7 9.6 %fusion.6 = f32[2048,768]{1,0:T(8,128)} fusion(bf16[2048,1536]{1,0:T(8,128)(2,1)} %get-tuple-element.138.dkv_ref, bf16[768,768]{1,0:T(8,128)(2,1)S(1)} %bitcast.100, bf16[768,768]{1,0:T(8,128)(2,1)S(1)} %bitcast.98), kind=kOutput, calls=%fused_computation.22 | convolution fusion | flops 4836556800 | bytes 14942208 | tf_op jit(solution)/shard_map/dot_general | solution.py:998
  546.8 93.7 %all-reduce.11.cloned.1.call-done = bf16[1568,768]{1,0:T(8,128)(2,1)} async-done(((bf16[1568,768]{1,0:T(8,128)(2,1)}), bf16[1568,768]{1,0:T(8,128)(2,1)}) %all-reduce.11.cloned.1.call-update) | async-done | bytes 2408464 | tf_op jit(solution)/shard_map/psum | solution.py:1023
  (327 shorter events, 223.9 us)
Async XLA Ops:
  7.2 520.5 %all-reduce.9.cloned.1.call-start = ((), (), s32[]{:S(2)}) async-start(), calls=%async_computation | async-start | bytes 4743168 | tf_op jit(solution)/shard_map/psum | solution.py:987
  7.2 20.8 %collective-permute-start.1 = (bf16[512,768]{1,0:T(8,128)(2,1)}, bf16[512,768]{1,0:T(8,128)(2,1)S(1)}, u32[]{:S(2)}, u32[]{:S(2)}) collective-permute-start(bf16[512,768]{1,0:T(8,128)(2,1)} %bitcast.86), channel_id=1, source_target_pairs={{0,2},{1,3},{2,0},{3,1},{4,6},{5,7},{6,4},{7,5},{8,10},{9,11},{10,... | collective-permute-start | bytes 2359304 | tf_op jit(solution)/shard_map/ppermute | solution.py:102
  10.3 40.6 %collective-permute-start = (bf16[512,768]{1,0:T(8,128)(2,1)}, bf16[512,768]{1,0:T(8,128)(2,1)}, u32[]{:S(2)}, u32[]{:S(2)}) collective-permute-start(bf16[512,768]{1,0:T(8,128)(2,1)} %bitcast.87), channel_id=1, source_target_pairs={{0,1},{1,0},{2,3},{3,2},{4,5},{5,4},{6,7},{7,6},{8,9},{9,8},{10,11... | collective-permute-start | bytes 2359304 | tf_op jit(solution)/shard_map/ppermute | solution.py:103
  28.0 34.1 %collective-permute-start.7 = (bf16[976,768]{1,0:T(8,128)(2,1)S(1)}, bf16[976,768]{1,0:T(8,128)(2,1)}, u32[]{:S(2)}, u32[]{:S(2)}) collective-permute-start(bf16[976,768]{1,0:T(8,128)(2,1)S(1)} %fusion.18.w0), channel_id=1, source_target_pairs={{0,2},{1,3},{2,0},{3,1},{4,6},{5,7},{6,4},{7,5},{8,10},{9,11},{10,... | collective-permute-start | bytes 4497416 | tf_op jit(solution)/shard_map/ppermute | solution.py:102
  30.9 31.2 %collective-permute-start.2 = (bf16[512,768]{1,0:T(8,128)(2,1)S(1)}, bf16[512,768]{1,0:T(8,128)(2,1)}, u32[]{:S(2)}, u32[]{:S(2)}) collective-permute-start(bf16[512,768]{1,0:T(8,128)(2,1)S(1)} %collective-permute-done.1.x_ref), channel_id=1, source_target_pairs={{0,1},{1,0},{2,3},{3,2},{4,5},{5,4},{6,7},{7,6},{8,9},{9,8},{10,11... | collective-permute-start | bytes 2359304 | tf_op jit(solution)/shard_map/ppermute | solution.py:104
  32.1 56.9 %collective-permute-start.6 = (bf16[976,768]{1,0:T(8,128)(2,1)S(1)}, bf16[976,768]{1,0:T(8,128)(2,1)}, u32[]{:S(2)}, u32[]{:S(2)}) collective-permute-start(bf16[976,768]{1,0:T(8,128)(2,1)S(1)} %fusion.18.w0), channel_id=1, source_target_pairs={{0,1},{1,0},{2,3},{3,2},{4,5},{5,4},{6,7},{7,6},{8,9},{9,8},{10,11... | collective-permute-start | bytes 4497416 | tf_op jit(solution)/shard_map/ppermute | solution.py:103
  62.1 29.9 %collective-permute-start.8 = (bf16[976,768]{1,0:T(8,128)(2,1)}, bf16[976,768]{1,0:T(8,128)(2,1)}, u32[]{:S(2)}, u32[]{:S(2)}) collective-permute-start(bf16[976,768]{1,0:T(8,128)(2,1)} %collective-permute-done.7.w2), channel_id=1, source_target_pairs={{0,1},{1,0},{2,3},{3,2},{4,5},{5,4},{6,7},{7,6},{8,9},{9,8},{10,11... | collective-permute-start | bytes 4497416 | tf_op jit(solution)/shard_map/ppermute | solution.py:104
  106.8 25.2 %collective-permute-start.9 = (bf16[512,768]{1,0:T(8,128)(2,1)}, bf16[512,768]{1,0:T(8,128)(2,1)S(1)}, u32[]{:S(2)}, u32[]{:S(2)}) collective-permute-start(bf16[512,768]{1,0:T(8,128)(2,1)} %get-tuple-element.100.q0), channel_id=1, source_target_pairs={{0,1},{1,0},{2,3},{3,2},{4,5},{5,4},{6,7},{7,6},{8,9},{9,8},{10,11... | collective-permute-start | bytes 2359304 | tf_op jit(solution)/shard_map/ppermute | solution.py:103
  175.4 21.3 %collective-permute-start.16 = (bf16[512,768]{1,0:T(8,128)(2,1)}, bf16[512,768]{1,0:T(8,128)(2,1)S(1)}, u32[]{:S(2)}, u32[]{:S(2)}) collective-permute-start(bf16[512,768]{1,0:T(8,128)(2,1)} %get-tuple-element.105), channel_id=1, source_target_pairs={{0,2},{1,3},{2,0},{3,1},{4,6},{5,7},{6,4},{7,5},{8,10},{9,11},{10,... | collective-permute-start | bytes 2359304 | tf_op jit(solution)/shard_map/ppermute | solution.py:971
  176.9 19.8 %collective-permute-start.17 = (f32[16,512]{1,0:T(8,128)}, f32[16,512]{1,0:T(8,128)S(1)}, u32[]{:S(2)}, u32[]{:S(2)}) collective-permute-start(f32[16,512]{1,0:T(8,128)} %get-tuple-element.106), channel_id=1, source_target_pairs={{0,2},{1,3},{2,0},{3,1},{4,6},{5,7},{6,4},{7,5},{8,10},{9,11},{10,... | collective-permute-start | bytes 98312 | tf_op jit(solution)/shard_map/ppermute | solution.py:971
  177.6 35.9 %collective-permute-start.22 = (bf16[512,768]{1,0:T(8,128)(2,1)S(1)}, bf16[512,768]{1,0:T(8,128)(2,1)S(1)}, u32[]{:S(2)}, u32[]{:S(2)}) collective-permute-start(bf16[512,768]{1,0:T(8,128)(2,1)S(1)} %bitcast_convert_fusion.g_ref.refs_4_), channel_id=1, source_target_pairs={{0,2},{1,3},{2,0},{3,1},{4,6},{5,7},{6,4},{7,5},{8,10},{9,11},{10,... | collective-permute-start | bytes 2359304 | tf_op jit(solution)/shard_map/ppermute | solution.py:102
  202.6 27.2 %collective-permute-start.21 = (bf16[512,768]{1,0:T(8,128)(2,1)}, bf16[512,768]{1,0:T(8,128)(2,1)S(1)}, u32[]{:S(2)}, u32[]{:S(2)}) collective-permute-start(bf16[512,768]{1,0:T(8,128)(2,1)} %get-tuple-element.109.m_ref.refs_0_), channel_id=1, source_target_pairs={{0,2},{1,3},{2,0},{3,1},{4,6},{5,7},{6,4},{7,5},{8,10},{9,11},{10,... | collective-permute-start | bytes 2359304 | tf_op jit(solution)/shard_map/ppermute | solution.py:102
  256.0 19.7 %collective-permute-start.29 = (bf16[512,768]{1,0:T(8,128)(2,1)S(1)}, bf16[512,768]{1,0:T(8,128)(2,1)S(1)}, u32[]{:S(2)}, u32[]{:S(2)}) collective-permute-start(bf16[512,768]{1,0:T(8,128)(2,1)S(1)} %add_convert_fusion.4), channel_id=1, source_target_pairs={{0,2},{1,3},{2,0},{3,1},{4,6},{5,7},{6,4},{7,5},{8,10},{9,11},{10,... | collective-permute-start | bytes 2359304 | tf_op jit(solution)/shard_map/ppermute | solution.py:112
  284.6 24.2 %collective-permute-start.30 = (bf16[512,768]{1,0:T(8,128)(2,1)}, bf16[512,768]{1,0:T(8,128)(2,1)S(1)}, u32[]{:S(2)}, u32[]{:S(2)}) collective-permute-start(bf16[512,768]{1,0:T(8,128)(2,1)} %get-tuple-element.123.d0), channel_id=1, source_target_pairs={{0,1},{1,0},{2,3},{3,2},{4,5},{5,4},{6,7},{7,6},{8,9},{9,8},{10,11... | collective-permute-start | bytes 2359304 | tf_op jit(solution)/shard_map/ppermute | solution.py:103
  352.9 19.6 %collective-permute-start.38 = (bf16[512,768]{1,0:T(8,128)(2,1)S(1)}, bf16[512,768]{1,0:T(8,128)(2,1)S(1)}, u32[]{:S(2)}, u32[]{:S(2)}) collective-permute-start(bf16[512,768]{1,0:T(8,128)(2,1)S(1)} %get-tuple-element.180), channel_id=1, source_target_pairs={{0,2},{1,3},{2,0},{3,1},{4,6},{5,7},{6,4},{7,5},{8,10},{9,11},{10,... | collective-permute-start | bytes 2359304 | tf_op jit(solution)/shard_map/ppermute | solution.py:112
  355.0 63.3 %collective-permute-start.20 = (bf16[512,768]{1,0:T(8,128)(2,1)}, bf16[512,768]{1,0:T(8,128)(2,1)S(1)}, u32[]{:S(2)}, u32[]{:S(2)}) collective-permute-start(bf16[512,768]{1,0:T(8,128)(2,1)} %get-tuple-element.112), channel_id=1, source_target_pairs={{0,1},{1,0},{2,3},{3,2},{4,5},{5,4},{6,7},{7,6},{8,9},{9,8},{10,11... | collective-permute-start | bytes 2359304 | tf_op jit(solution)/shard_map/ppermute | solution.py:110
  355.1 43.7 %collective-permute-start.25 = (bf16[512,768]{1,0:T(8,128)(2,1)}, bf16[512,768]{1,0:T(8,128)(2,1)S(1)}, u32[]{:S(2)}, u32[]{:S(2)}) collective-permute-start(bf16[512,768]{1,0:T(8,128)(2,1)} %get-tuple-element.114), channel_id=1, source_target_pairs={{0,1},{1,0},{2,3},{3,2},{4,5},{5,4},{6,7},{7,6},{8,9},{9,8},{10,11... | collective-permute-start | bytes 2359304 | tf_op jit(solution)/shard_map/ppermute | solution.py:109
  398.8 55.8 %collective-permute-start.45 = (bf16[2,5,192,768]{3,2,1,0:T(8,128)(2,1)}, bf16[2,5,192,768]{3,2,1,0:T(8,128)(2,1)}, u32[]{:S(2)}, u32[]{:S(2)}) collective-permute-start(bf16[2,5,192,768]{3,2,1,0:T(8,128)(2,1)} %pad_maximum_fusion), channel_id=1, source_target_pairs={{0,1},{1,0},{2,3},{3,2},{4,5},{5,4},{6,7},{7,6},{8,9},{9,8},{10,11... | collective-permute-start | bytes 8847368 | tf_op jit(solution)/shard_map/ppermute | solution.py:1012
  399.9 20.3 %collective-permute-start.26 = (bf16[512,768]{1,0:T(8,128)(2,1)}, bf16[512,768]{1,0:T(8,128)(2,1)}, u32[]{:S(2)}, u32[]{:S(2)}) collective-permute-start(bf16[512,768]{1,0:T(8,128)(2,1)} %add_convert_fusion.6), channel_id=1, source_target_pairs={{0,2},{1,3},{2,0},{3,1},{4,6},{5,7},{6,4},{7,5},{8,10},{9,11},{10,... | collective-permute-start | bytes 2359304 | tf_op jit(solution)/shard_map/ppermute | solution.py:112
  417.4 223.1 %all-reduce.11.cloned.1.call-start = ((), (), s32[]{:S(2)}) async-start(), calls=%async_computation.1 | async-start | bytes 4816896 | tf_op jit(solution)/shard_map/psum | solution.py:1023
  456.7 39.3 %collective-permute-start.46 = (bf16[5,192,768]{2,1,0:T(8,128)(2,1)S(1)}, bf16[5,192,768]{2,1,0:T(8,128)(2,1)S(1)}, u32[]{:S(2)}, u32[]{:S(2)}) collective-permute-start(bf16[5,192,768]{2,1,0:T(8,128)(2,1)S(1)} %fusion.7), channel_id=1, source_target_pairs={{0,2},{1,3},{2,0},{3,1},{4,6},{5,7},{6,4},{7,5},{8,10},{9,11},{10,... | collective-permute-start | bytes 4423688 | tf_op jit(solution)/shard_map/ppermute | solution.py:1014
  461.6 31.3 %collective-permute-start.43 = (bf16[512,768]{1,0:T(8,128)(2,1)}, bf16[512,768]{1,0:T(8,128)(2,1)}, u32[]{:S(2)}, u32[]{:S(2)}) collective-permute-start(bf16[512,768]{1,0:T(8,128)(2,1)} %get-tuple-element.136), channel_id=1, source_target_pairs={{0,1},{1,0},{2,3},{3,2},{4,5},{5,4},{6,7},{7,6},{8,9},{9,8},{10,11... | collective-permute-start | bytes 2359304 | tf_op jit(solution)/shard_map/ppermute | solution.py:109
  485.4 51.9 %collective-permute-start.42 = (bf16[512,768]{1,0:T(8,128)(2,1)}, bf16[512,768]{1,0:T(8,128)(2,1)}, u32[]{:S(2)}, u32[]{:S(2)}) collective-permute-start(bf16[512,768]{1,0:T(8,128)(2,1)} %get-tuple-element.134), channel_id=1, source_target_pairs={{0,1},{1,0},{2,3},{3,2},{4,5},{5,4},{6,7},{7,6},{8,9},{9,8},{10,11... | collective-permute-start | bytes 2359304 | tf_op jit(solution)/shard_map/ppermute | solution.py:110
  495.4 44.2 %collective-permute-start.44 = (bf16[512,768]{1,0:T(8,128)(2,1)}, bf16[512,768]{1,0:T(8,128)(2,1)}, u32[]{:S(2)}, u32[]{:S(2)}) collective-permute-start(bf16[512,768]{1,0:T(8,128)(2,1)} %add_convert_fusion.2), channel_id=1, source_target_pairs={{0,2},{1,3},{2,0},{3,1},{4,6},{5,7},{6,4},{7,5},{8,10},{9,11},{10,... | collective-permute-start | bytes 2359304 | tf_op jit(solution)/shard_map/ppermute | solution.py:112
  (90 other events, 720.5 us)
Sparse Core Ops, SparseCore 0:
  417.5 110.1 all-reduce.8
  531.3 109.1 all-reduce.10

commit v2 on v1

v2 whole, which is shorter than its diff:
```python
import functools
import math

import jax
import jax.numpy as jnp
import numpy as np
from jax import lax
from jax.experimental import pallas as pl
from jax.experimental.pallas import tpu as pltpu
from jax.sharding import PartitionSpec as P

HEAD_DIM = 64
SPAN = 64
LANES = 128
QUERY_ROWS = 256
NEGATIVE = -1e30
NORM_EPS = 1e-05
BF = jnp.bfloat16
F32 = jnp.float32
VMEM_BYTES = 56 * 1024 * 1024

COST_US = {
    "prepare": 3.4,
    "qkv": 6.6,
    "attend": 18,
    "after_attend": 6,
    "memory_near": 12,
    "memory_far": 5,
    "cross": 6,
    "feed_near": 6.2,
    "feed_far": 6.2,
    "feed_weight": 11.4,
    "middle_back": 17.5,
    "cross_weight": 17.8,
    "attend_back": 25,
    "qkv_weight": 7.5,
    "input_back": 5.7,
    "block_grad": 6.8,
    "input_grad": 4,
    "return_blocks": 6,
}

DOCS = 5
MASK_LANE = HEAD_DIM
LSE_LANE = HEAD_DIM + DOCS


def nn(a, b):
    return lax.dot_general(a, b, (((1,), (0,)), ((), ())), preferred_element_type=F32)


def nt(a, b):
    return lax.dot_general(a, b, (((1,), (1,)), ((), ())), preferred_element_type=F32)


def tn(a, b):
    return lax.dot_general(a, b, (((0,), (0,)), ((), ())), preferred_element_type=F32)


def call(body, name, grid, in_specs, out_specs, out_shape, args, scratch=(), prefetch=0, aliases=None):
    return pl.pallas_call(
        body,
        out_shape=out_shape,
        grid_spec=pltpu.PrefetchScalarGridSpec(
            num_scalar_prefetch=prefetch,
            grid=grid,
            in_specs=in_specs,
            out_specs=out_specs,
            scratch_shapes=list(scratch),
        ),
        compiler_params=pltpu.CompilerParams(
            vmem_limit_bytes=VMEM_BYTES, dimension_semantics=("arbitrary",) * len(grid)
        ),
        cost_estimate=pl.CostEstimate(flops=int(COST_US[name.rstrip("_0123")] * 1e7), bytes_accessed=1, transcendentals=0),
        name=name,
        input_output_aliases=aliases or {},
    )(*args)


def whole(array):
    zeros = (0,) * len(array.shape)
    return pl.BlockSpec(array.shape, lambda *_: zeros)


def rows_of(tile, width):
    return pl.BlockSpec((tile, width), lambda i, *_: (i, 0))


def shape_of(shape, dtype):
    return jax.ShapeDtypeStruct(shape, dtype)


def standardize(values):
    centre = values - jnp.mean(values, -1, keepdims=True)
    inverse = lax.rsqrt(jnp.mean(centre * centre, -1, keepdims=True) + NORM_EPS)
    return centre * inverse, inverse


def norm_pull(grad, normed, inverse, gain):
    scaled = grad * gain
    return inverse * (
        scaled
        - jnp.mean(scaled, -1, keepdims=True)
        - normed * jnp.mean(scaled * normed, -1, keepdims=True)
    )


def column_sum(values):
    return jnp.sum(values, 0, keepdims=True)


def add_rows(out_ref, rows):
    @pl.when(pl.program_id(0) == 0)
    def _():
        out_ref[...] = jnp.zeros_like(out_ref)

    for index, row in enumerate(rows):
        out_ref[index : index + 1, :] += row


def follow(operand, earlier):
    return lax.optimization_barrier((operand, earlier))


def collect(parts, partners, earlier=None):
    core, chip, _ = partners
    far = lax.ppermute(parts[3], "tp", core)
    near = lax.ppermute(parts[1], "tp", core)
    sent = rounded_sum(parts[2], far)
    if earlier is not None:
        sent, earlier = follow(sent, earlier)
    return [parts[0], near, lax.ppermute(sent, "tp", chip)], earlier


def take_rows(values, part, rows):
    return lax.dynamic_slice_in_dim(values, part * rows, rows, 0)


def rounded_sum(*parts):
    return sum(part.astype(F32) for part in parts).astype(BF)


def swap(values, step, size):
    return lax.ppermute(values, "dp", [(i, i ^ step) for i in range(size)])


def sum_beside(values, size):
    device = lax.axis_index("dp")
    x, z = device & 1, device >> 1
    half = values.shape[0] // 2
    quarter = half // 4
    got = swap(take_rows(values, 1 - x, half), 1, size)
    part = rounded_sum(take_rows(values, x, half), got)
    got = [swap(take_rows(part, z ^ k, quarter), 2 * k, size) for k in (1, 2, 3)]
    own = rounded_sum(take_rows(part, z, quarter), *got)
    line = jnp.stack([own] + [swap(own, 2 * k, size) for k in (1, 2, 3)])
    both = jnp.concatenate([line, swap(line, 1, size)], 0)
    order = [(x ^ (i >> 2)) * 4 + (z ^ (i & 3)) for i in range(8)]
    return jnp.concatenate([lax.dynamic_index_in_dim(both, i, 0, keepdims=False) for i in order], 0)


def sum_along(values, size):
    device = lax.axis_index("dp")
    x, z = device & 1, device >> 1
    quarter = values.shape[0] // 4
    half = quarter // 2
    got = [swap(take_rows(values, z ^ k, quarter), 2 * k, size) for k in (1, 2, 3)]
    part = rounded_sum(take_rows(values, z, quarter), *got)
    own = rounded_sum(take_rows(part, x, half), swap(take_rows(part, 1 - x, half), 1, size))
    pair = jnp.stack([own, swap(own, 1, size)])
    both = jnp.concatenate([pair] + [swap(pair, 2 * k, size) for k in (1, 2, 3)], 0)
    order = [(z ^ (i >> 1)) * 2 + (x ^ (i & 1)) for i in range(8)]
    return jnp.concatenate([lax.dynamic_index_in_dim(both, i, 0, keepdims=False) for i in order], 0)


def sum_over_dp(values):
    size = lax.axis_size("dp")
    rows = values.shape[0]
    if size != 8:
        return lax.psum(values, "dp")
    unit = 8 * 16
    if rows <= 5 * unit:
        values = jnp.pad(values, ((0, -rows % unit), (0, 0)))
        return sum_beside(values, size)[:rows]
    first = -(-(rows * 5 // 8) // unit) * unit
    second = -(-(rows - first) // unit) * unit
    values = jnp.pad(values, ((0, first + second - rows), (0, 0)))
    return jnp.concatenate([sum_beside(values[:first], size), sum_along(values[first:], size)], 0)[:rows]


def exchange(parts, partners):
    return [parts[0]] + [lax.ppermute(parts[r], "tp", partners[r - 1]) for r in (1, 2, 3)]


def gather_rows(t_ref, refs, target, start=0):
    @pl.when(pl.program_id(0) == 0)
    def _():
        for rel, ref in enumerate(refs):
            count = ref.shape[0]
            target[pl.ds(pl.multiple_of((t_ref[0] ^ rel) * count + start, 16), count), :] = ref[...]


def gather_bias(t_ref, refs, start, local):
    rows = [ref[...].astype(F32)[0:1] for ref in refs]
    rows = [row[:, start : start + local] + row[:, start + local : start + 2 * local] for row in rows]
    groups = []
    for group in range(4):
        groups.append(sum(jnp.where(t_ref[0] ^ rel == group, row, 0.0) for rel, row in enumerate(rows)))
    return jnp.concatenate(groups, 1)


def pack_rows(local, width, part):
    return [pl.BlockSpec((local, width), lambda i, *_: (part, 0))] * 4


def prepare_body(qkv_ref, cq_ref, so_ref, kv_ref, co_ref, bq_ref, bv_ref, w_ref, pack_ref):
    local, width = so_ref.shape
    zeros = jnp.zeros((LANES - HEAD_DIM, width), BF)
    for j in range(3 * local // HEAD_DIM):
        part = qkv_ref[j * HEAD_DIM // local, j * HEAD_DIM % local : j * HEAD_DIM % local + HEAD_DIM, :]
        w_ref[j * LANES : j * LANES + HEAD_DIM, :] = part
        w_ref[j * LANES + HEAD_DIM : (j + 1) * LANES, :] = zeros
    for index, part in enumerate((cq_ref[...], so_ref[...], kv_ref[0], kv_ref[1], co_ref[...])):
        pack_ref[index * local : (index + 1) * local, :] = part
    parts = []
    for ref in (bq_ref, bv_ref):
        high = ref[...].astype(BF).astype(F32)
        parts += [high, ref[...] - high]
    row = jnp.concatenate(parts, 1)
    count = pack_ref.shape[0] - 5 * local
    first = lax.broadcasted_iota(jnp.int32, (count, width), 0) == 0
    pack_ref[5 * local :, :] = jnp.where(first, row, 0.0).astype(BF)


def prepare(qkv, cq, so, kv, co, bq, bv, pack_size):
    local, width = so.shape
    outs = [shape_of((3 * local // HEAD_DIM * LANES, width), BF), shape_of((pack_size, width), BF)]
    args = (qkv, cq, so, kv, co, bq, bv)
    return call(prepare_body, "prepare", (1,), [whole(a) for a in args], [whole(o) for o in outs], outs, args)


def qkv_body(t_ref, xa, xb, gain_ref, shift_ref, w_ref, b_ref, ca, sa, ta, cb, sb, tb, aa, ab, oa, ob):
    heads = oa.shape[1]
    for x_ref, cos_ref, left_ref, right_ref, a_ref, out_ref in ((xa, ca, sa, ta, aa, oa), (xb, cb, sb, tb, ab, ob)):
        normed, _ = standardize(x_ref[...].astype(F32))
        a = (normed * gain_ref[0:1, :] + shift_ref[0:1, :]).astype(BF)
        a_ref[...] = a
        proj = nt(a, w_ref[...]) + b_ref[...]
        cos, left, right = cos_ref[...], left_ref[...], right_ref[...]
        for j in range(3 * heads):
            part = proj[:, j * LANES : (j + 1) * LANES]
            if j < 2 * heads:
                part = part * cos + pltpu.roll(part, 96, 1) * left + pltpu.roll(part, 32, 1) * right
            if j < heads:
                part = part * (1.0 / math.sqrt(HEAD_DIM))
            out_ref[j // heads, j % heads] = part.astype(BF)


def project_rows(rels, t, xs, gain, shift, w, b, tables, heads):
    rows, width = xs[0].shape
    tile = min(256, rows)
    steps = rows // tile

    def table(rel):
        return pl.BlockSpec((tile, LANES), lambda i, t_ref: ((t_ref[0] ^ rel) * steps + i, 0))

    row = rows_of(tile, width)
    out = pl.BlockSpec((3, heads, tile, LANES), lambda i, t_ref: (0, 0, i, 0))
    return call(
        qkv_body,
        f"qkv_{rels[0]}{rels[1]}",
        (steps,),
        [row, row, whole(gain), whole(shift), whole(w), whole(b)] + [table(rels[0])] * 3 + [table(rels[1])] * 3,
        [row, row, out, out],
        [shape_of((rows, width), BF)] * 2 + [shape_of((3, heads, rows, LANES), BF)] * 2,
        (t, *xs, gain, shift, w, b, *tables, *tables),
        prefetch=1,
    )


def causal_corner(scores):
    keys = lax.broadcasted_iota(jnp.int32, scores.shape, 0)
    queries = lax.broadcasted_iota(jnp.int32, scores.shape, 1)
    return jnp.where(keys <= queries, scores, NEGATIVE)


def attend_body(t_ref, c0, c1, c2, c3, qx_ref, kx_ref, vx_ref, qe_ref, ke_ref, ve_ref, ot_ref, lse_ref, vt_ref):
    t = t_ref[0]
    rows = c0.shape[2]
    for rel, chunk in enumerate((c0, c1, c2, c3)):
        place = pl.ds(pl.multiple_of((t ^ rel) * rows, rows), rows)
        qe_ref[0, place, :] = chunk[0, 0] + qx_ref[place, :]
        ke_ref[0, place, :] = chunk[1, 0] + kx_ref[place, :]
        values = chunk[2, 0] + vx_ref[...]
        ve_ref[0, place, :] = values
        vt_ref[:, place] = values.astype(F32).T.astype(BF)
    step = QUERY_ROWS
    for low in range(0, qe_ref.shape[1], step):
        high = low + step
        query = qe_ref[0, low:high, :]
        corner = causal_corner(nt(ke_ref[0, low:high, :], query))
        top = jnp.max(corner, 0, keepdims=True)
        if low:
            earlier = nt(ke_ref[0, :low, :], query)
            top = jnp.maximum(top, jnp.max(earlier, 0, keepdims=True))
        mixed = nn(vt_ref[:, low:high], jnp.exp(corner - top).astype(BF))
        if low:
            mixed = mixed + nn(vt_ref[:, :low], jnp.exp(earlier - top).astype(BF))
        total = mixed[HEAD_DIM : HEAD_DIM + 1, :]
        lse_ref[0, :, low:high] = top + jnp.log(total)
        begin = low % rows
        ot_ref[t ^ (low // rows), :, begin : begin + step] = (mixed[:HEAD_DIM] / total).astype(BF)


def attend(t, chunks, qx, kx, vx):
    _, heads, rows, _ = chunks[0].shape
    length = qx.shape[0]
    chunk = pl.BlockSpec((3, 1, rows, LANES), lambda h, t_ref: (0, h, 0, 0))
    plane = pl.BlockSpec((1, length, LANES), lambda h, t_ref: (h, 0, 0))
    padded = shape_of((heads, length, LANES), BF)
    return call(
        attend_body,
        "attend",
        (heads,),
        [chunk] * 4 + [whole(qx), whole(kx), whole(vx)],
        [
            plane,
            plane,
            plane,
            pl.BlockSpec((4, HEAD_DIM, rows), lambda h, t_ref: (0, h, 0)),
            pl.BlockSpec((1, 1, length), lambda h, t_ref: (h, 0, 0)),
        ],
        [padded, padded, padded, shape_of((4, heads * HEAD_DIM, rows), BF), shape_of((heads, 1, length), F32)],
        (t, *chunks, qx, kx, vx),
        scratch=[pltpu.VMEM((LANES, length), BF)],
        prefetch=1,
    )


def three_parts(values):
    first = values.astype(BF).astype(F32)
    second = (values - first).astype(BF).astype(F32)
    return first, second, values - first - second


def attend_back_body(
    t_ref, qe_ref, ke_ref, ve_ref, d0, d1, d2, d3, ot_ref, lse_ref, cos_ref, sa_ref, sb_ref, out_ref,
    qt_ref, kt_ref, dt_ref, dk_ref, dv_ref,
):
    t = t_ref[0]
    rows = d0.shape[1]
    step = QUERY_ROWS
    length = qe_ref.shape[1]
    for rel, chunk in enumerate((d0, d1, d2, d3)):
        place = pl.ds(pl.multiple_of((t ^ rel) * rows, rows), rows)
        grad = chunk[...].astype(F32)
        delta = three_parts(jnp.sum(grad * ot_ref[rel].astype(F32), 0, keepdims=True))
        padded = jnp.concatenate([grad, jnp.zeros_like(grad)], 0)
        row = lax.broadcasted_iota(jnp.int32, padded.shape, 0)
        for index in range(3):
            padded = jnp.where(row == HEAD_DIM + index, -delta[index], padded)
        dt_ref[:, place] = padded.astype(BF)
    for low in range(0, length, rows):
        high = low + rows
        kt_ref[:, low:high] = ke_ref[0, low:high, :].astype(F32).T.astype(BF)
        turned = qe_ref[0, low:high, :].astype(F32).T
        row = lax.broadcasted_iota(jnp.int32, turned.shape, 0)
        pieces = three_parts(lse_ref[0, :, low:high])
        for index in range(3):
            turned = jnp.where(row == LSE_LANE + index, -pieces[index], turned)
        qt_ref[:, low:high] = turned.astype(BF)
    dk_ref[...] = jnp.zeros_like(dk_ref)
    dv_ref[...] = jnp.zeros_like(dv_ref)

    def unrotate(grad, place):
        return (
            grad * cos_ref[place, :]
            - pltpu.roll(grad, 96, 1) * sa_ref[place, :]
            - pltpu.roll(grad, 32, 1) * sb_ref[place, :]
        )

    for low in range(0, length, step):
        high = low + step
        query, query_t, grad_t = qe_ref[0, low:high, :], qt_ref[:, low:high], dt_ref[:, low:high]
        dq_t = None
        for begin, end in ((0, low), (low, high)):
            if begin == end:
                continue
            scores = nn(ke_ref[0, begin:end, :], query_t)
            if begin == low:
                scores = causal_corner(scores)
            prob = jnp.exp(scores)
            grad_scores = (prob * nn(ve_ref[0, begin:end, :], grad_t)).astype(BF)
            dv_ref[begin:end, :] += nt(prob.astype(BF), grad_t)
            dk_ref[begin:end, :] += nn(grad_scores, query)
            part = nn(kt_ref[:, begin:end], grad_scores)
            dq_t = part if dq_t is None else dq_t + part
        start = low % rows
        grad_query = unrotate(dq_t.T, slice(low, high)) * (1.0 / math.sqrt(HEAD_DIM))
        out_ref[t ^ (low // rows), 0, 0, start : start + step, :] = grad_query.astype(BF)
    for low in range(0, length, rows):
        place = slice(low, low + rows)
        rel = t ^ (low // rows)
        out_ref[rel, 1, 0] = unrotate(dk_ref[place, :], place).astype(BF)
        lane = lax.broadcasted_iota(jnp.int32, (rows, LANES), 1)
        out_ref[rel, 2, 0] = jnp.where(lane < HEAD_DIM, dv_ref[place, :], 0.0).astype(BF)


def attend_back(t, qe, ke, ve, grads, ot, lse, tables):
    heads, length, _ = qe.shape
    rows = grads[0].shape[1]
    plane = pl.BlockSpec((1, length, LANES), lambda h, t_ref: (h, 0, 0))
    grad = pl.BlockSpec((HEAD_DIM, rows), lambda h, t_ref: (h, 0))
    return call(
        attend_back_body,
        "attend_back",
        (heads,),
        [plane] * 3
        + [grad] * 4
        + [
            pl.BlockSpec((4, HEAD_DIM, rows), lambda h, t_ref: (0, h, 0)),
            pl.BlockSpec((1, 1, length), lambda h, t_ref: (h, 0, 0)),
        ]
        + [whole(table) for table in tables],
        pl.BlockSpec((4, 3, 1, rows, LANES), lambda h, t_ref: (0, 0, h, 0, 0)),
        shape_of((4, 3, heads, rows, LANES), BF),
        (t, qe, ke, ve, *grads, ot, lse, *tables),
        scratch=[pltpu.VMEM((LANES, length), BF)] * 3 + [pltpu.VMEM((length, LANES), F32)] * 2,
        prefetch=1,
    )


def input_back_body(xa, xb, da, db, w_ref, oa, ob, small_ref):
    heads = da.shape[2]
    totals = []
    for x_ref, dp_ref, out_ref in ((xa, da, oa), (xb, db, ob)):
        grads = jnp.concatenate([dp_ref[0, j // heads, j % heads] for j in range(3 * heads)], 1)
        grad = nn(grads, w_ref[...])
        normed, _ = standardize(x_ref[...].astype(F32))
        out_ref[...] = grad.astype(BF)
        totals.append((column_sum(grad * normed), column_sum(grad)))
    add_rows(small_ref, [totals[0][0] + totals[1][0], totals[0][1] + totals[1][1]])


def input_back(rels, xs, dp, w):
    rows, width = xs[0].shape
    heads = dp.shape[2]
    tile = min(256, rows)
    row = rows_of(tile, width)

    def part(rel):
        return pl.BlockSpec((1, 3, heads, tile, LANES), lambda i: (rel, 0, 0, i, 0))

    return call(
        input_back_body,
        f"input_back_{rels[0]}{rels[1]}",
        (rows // tile,),
        [row, row, part(rels[0]), part(rels[1]), whole(w)],
        [row, row, pl.BlockSpec((8, width), lambda i: (0, 0))],
        [shape_of((rows, width), BF)] * 2 + [shape_of((8, width), F32)],
        (*xs, dp, dp, w),
    )


def qkv_weight_body(dp_ref, a0, a1, a2, a3, out_ref, bias_ref):
    heads = dp_ref.shape[2]
    total, sums = None, None
    for rel, a_ref in enumerate((a0, a1, a2, a3)):
        grads = jnp.concatenate([dp_ref[rel, 0, h] for h in range(heads)], 1)
        part, part_sum = tn(grads, a_ref[...]), column_sum(grads.astype(F32))
        total = part if total is None else total + part
        sums = part_sum if sums is None else sums + part_sum
    for h in range(heads):
        out_ref[h * HEAD_DIM : (h + 1) * HEAD_DIM, :] = total[h * LANES : h * LANES + HEAD_DIM].astype(BF)
    bias_ref[0] = sums


def qkv_weight(dp, normed):
    _, _, heads, rows, _ = dp.shape
    width = normed[0].shape[1]
    local = heads * HEAD_DIM
    return call(
        qkv_weight_body,
        "qkv_weight",
        (3,),
        [pl.BlockSpec((4, 1, heads, rows, LANES), lambda j: (0, j, 0, 0, 0))] + [whole(a) for a in normed],
        [rows_of(local, width), pl.BlockSpec((1, 1, heads * LANES), lambda j: (j, 0, 0))],
        [shape_of((3 * local, width), BF), shape_of((3, 1, heads * LANES), F32)],
        (dp, *normed),
    )


def after_attend_body(
    t_ref, x_ref, o0, o1, o2, o3, w0, w1, w2, w3, q0, q1, q2, q3, b0, b1, b2, b3, bias_ref, gain_ref, shift_ref,
    x1_ref, b_ref, cq_ref, wq_ref,
):
    gather_rows(t_ref, (q0, q1, q2, q3), wq_ref)
    total = x_ref[...].astype(F32) + bias_ref[0:1, :]
    for o_ref, w_ref in ((o0, w0), (o1, w1), (o2, w2), (o3, w3)):
        total = total + tn(o_ref[...], w_ref[...])
    x1_ref[...] = total
    normed, _ = standardize(total)
    b = (normed * gain_ref[1:2, :] + shift_ref[1:2, :]).astype(BF)
    b_ref[...] = b
    bias = gather_bias(t_ref, (b0, b1, b2, b3), 0, w0.shape[0])
    cq_ref[...] = ((nt(b, wq_ref[...]) + bias) * (1.0 / math.sqrt(HEAD_DIM))).astype(BF)


def after_attend(t, x, mixed, packs, out_bias, gain, shift):
    rows, width = x.shape
    local = mixed[0].shape[0]
    tile = min(256, rows)
    return call(
        after_attend_body,
        "after_attend",
        (rows // tile,),
        [rows_of(tile, width)]
        + [pl.BlockSpec((local, tile), lambda i, *_: (0, i))] * 4
        + pack_rows(local, width, 1)
        + pack_rows(local, width, 0)
        + pack_rows(16, width, 5 * local // 16)
        + [whole(out_bias), whole(gain), whole(shift)],
        [rows_of(tile, width)] * 3,
        [shape_of((rows, width), F32), shape_of((rows, width), BF), shape_of((rows, width), BF)],
        (t, x, *mixed, *packs, *packs, *packs, out_bias, gain, shift),
        scratch=[pltpu.VMEM((width, width), BF)],
        prefetch=1,
    )


def split_pair(values):
    lane = lax.broadcasted_iota(jnp.int32, values.shape, 1)
    zero = jnp.zeros_like(values)
    return jnp.concatenate(
        [jnp.where(lane < HEAD_DIM, values, zero), jnp.where(lane >= HEAD_DIM, values, zero)], 0
    )


def join_pair(values):
    rows = values.shape[0] // 2
    lane = lax.broadcasted_iota(jnp.int32, (rows, values.shape[1]), 1)
    return jnp.where(lane < HEAD_DIM, values[:rows], values[rows:])


def lane_cuts(width):
    return [slice(start, start + LANES) for start in range(0, width, LANES)]


def cross_body(
    t_ref, cq_ref, kv_ref, x1_ref, w0, w1, w2, w3, bias_ref, gain_ref, shift_ref, co_ref, lse_ref, x2_ref, m_ref, w_ref
):
    gather_rows(t_ref, (w0, w1, w2, w3), w_ref)
    width = cq_ref.shape[1]
    spans, side, _ = lse_ref.shape
    keys = kv_ref.shape[0] // spans
    cuts = lane_cuts(width)
    for span in range(spans):
        place = slice(span * SPAN, (span + 1) * SPAN)
        query = cq_ref[place, :]
        key, value = kv_ref[span * keys : (span + 1) * keys, :width], kv_ref[span * keys : (span + 1) * keys, width:]
        scores = [nt(key[:, cut], split_pair(query[:, cut])) for cut in cuts]
        tops = [jnp.max(score, 0, keepdims=True) for score in scores]
        shifted = [jnp.exp(score - top) for score, top in zip(scores, tops)]
        totals = [jnp.sum(part, 0, keepdims=True) for part in shifted]
        probs = [(part * (1.0 / total)).astype(BF) for part, total in zip(shifted, totals)]
        mixed = [join_pair(tn(prob, value[:, cut])) for prob, cut in zip(probs, cuts)]
        co_ref[place, :] = jnp.concatenate(mixed, 1).astype(BF)
        rows = [top + jnp.log(total) for top, total in zip(tops, totals)]
        lse_ref[span] = jnp.concatenate(rows + [jnp.zeros((side - len(rows), LANES), F32)], 0)
    total = x1_ref[...] + nn(co_ref[...], w_ref[...]) + bias_ref[1:2, :]
    x2_ref[...] = total
    normed, _ = standardize(total)
    m_ref[...] = (normed * gain_ref[2:3, :] + shift_ref[2:3, :]).astype(BF)


def cross(t, half, cq, kv, x1, packs, local, out_bias, gain, shift):
    rows, width = x1.shape
    tile = rows // 2
    ratio = kv.shape[0] // rows
    side = -(-(width // LANES) // 8) * 8
    spans = tile // SPAN

    def rows_at(count, columns):
        return pl.BlockSpec((count, columns), lambda i, *_: (half, 0))

    row = rows_at(tile, width)
    outs = [
        shape_of((tile, width), BF),
        shape_of((spans, side, LANES), F32),
        shape_of((tile, width), F32),
        shape_of((tile, width), BF),
    ]
    return call(
        cross_body,
        f"cross_{half}",
        (1,),
        [row, rows_at(ratio * tile, 2 * width), row]
        + pack_rows(local, width, 4)
        + [whole(out_bias), whole(gain), whole(shift)],
        [whole(out) for out in outs],
        outs,
        (t, cq, kv, x1, *packs, out_bias, gain, shift),
        scratch=[pltpu.VMEM((width, width), BF)],
        prefetch=1,
    )


def middle_back_body(
    t_ref, x2a, x2b, da0, da1, da2, db0, db1, db2, lsea, lseb, g_ref, gain_ref, cq_ref, kv_ref, x1_ref,
    c0, c1, c2, c3, q0, q1, q2, q3, w0, w1, w2, w3,
    g2r_ref, dkv_ref, g1_ref, g1r_ref, dqc_ref, d0, d1, d2, d3, small_ref,
    dco_ref, dq_ref, x2_ref, dm_ref, lse_ref, co_w_ref, wq_ref,
):
    gather_rows(t_ref, (c0, c1, c2, c3), co_w_ref)
    gather_rows(t_ref, (q0, q1, q2, q3), wq_ref)
    for side, (x2, parts, lse) in enumerate(((x2a, (da0, da1, da2), lsea), (x2b, (db0, db1, db2), lseb))):

        @pl.when(pl.program_id(0) == side)
        def _(x2=x2, parts=parts, lse=lse):
            x2_ref[...] = x2[...]
            dm_ref[...] = sum(part[...].astype(F32) for part in parts)
            lse_ref[...] = lse[...]

    width = cq_ref.shape[1]
    spans = lse_ref.shape[0]
    keys = kv_ref.shape[0] // spans
    cuts = lane_cuts(width)
    grad_m = dm_ref[...]
    normed_m, inverse = standardize(x2_ref[...])
    g = g_ref[...]
    g2 = g + norm_pull(grad_m, normed_m, inverse, gain_ref[2:3, :])
    g2r = g2.astype(BF)
    g2r_ref[...] = g2r
    dco_ref[...] = nt(g2r, co_w_ref[...]).astype(BF)
    for span in range(spans):
        place = slice(span * SPAN, (span + 1) * SPAN)
        block = slice(span * keys, (span + 1) * keys)
        query, grad = cq_ref[place, :], dco_ref[place, :]
        key, value = kv_ref[block, :width], kv_ref[block, width:]
        stats = lse_ref[span]
        queries = [split_pair(query[:, cut]) for cut in cuts]
        grads = [split_pair(grad[:, cut]) for cut in cuts]
        probs = [jnp.exp(nt(key[:, cut], q) - stats[j : j + 1]) for j, (cut, q) in enumerate(zip(cuts, queries))]
        pulls = [nt(value[:, cut], part) for cut, part in zip(cuts, grads)]
        deltas = [jnp.sum(prob * pull, 0, keepdims=True) for prob, pull in zip(probs, pulls)]
        scores = [(prob * (pull - delta)).astype(BF) for prob, pull, delta in zip(probs, pulls, deltas)]
        keys_back = [nn(score, q).astype(BF) for score, q in zip(scores, queries)]
        values_back = [nn(prob.astype(BF), part).astype(BF) for prob, part in zip(probs, grads)]
        dkv_ref[block, :] = jnp.concatenate(keys_back + values_back, 1)
        dq_ref[place, :] = jnp.concatenate([join_pair(tn(score, key[:, cut])) for score, cut in zip(scores, cuts)], 1)
    dqc = (dq_ref[...] * (1.0 / math.sqrt(HEAD_DIM))).astype(BF)
    dqc_ref[...] = dqc
    grad_b = nn(dqc, wq_ref[...])
    normed_b, inverse = standardize(x1_ref[...])
    g1 = g2 + norm_pull(grad_b, normed_b, inverse, gain_ref[1:2, :])
    g1_ref[...] = g1
    g1r = g1.astype(BF)
    g1r_ref[...] = g1r
    for w_ref, d_ref in ((w0, d0), (w1, d1), (w2, d2), (w3, d3)):
        d_ref[...] = nt(w_ref[...], g1r).astype(BF)
    add_rows(
        small_ref,
        [
            column_sum(grad_b * normed_b),
            column_sum(grad_b),
            column_sum(grad_m * normed_m),
            column_sum(grad_m),
            column_sum(g1),
            column_sum(g2),
            column_sum(g),
            column_sum(dqc.astype(F32)),
            column_sum(dkv_ref[:, width:].astype(F32)),
        ],
    )


def middle_back(t, x2, dm, lse, g, packs, local, gain, cq, kv, x1):
    rows, width = x1.shape
    tile = rows // 2
    ratio = kv.shape[0] // rows
    row = rows_of(tile, width)
    wide = rows_of(ratio * tile, 2 * width)
    turned = pl.BlockSpec((local, tile), lambda i, *_: (0, i))
    half = shape_of((rows, width), BF)
    halves = (*x2, *dm[0], *dm[1], *lse)
    return call(
        middle_back_body,
        "middle_back",
        (2,),
        [whole(value) for value in halves]
        + [row, whole(gain), row, wide, row]
        + pack_rows(local, width, 4)
        + pack_rows(local, width, 0)
        + pack_rows(local, width, 1),
        [row, wide, row, row, row] + [turned] * 4 + [pl.BlockSpec((16, width), lambda i, *_: (0, 0))],
        [half, shape_of(kv.shape, BF), shape_of((rows, width), F32), half, half]
        + [shape_of((local, rows), BF)] * 4
        + [shape_of((16, width), F32)],
        (t, *halves, g, gain, cq, kv, x1, *packs, *packs, *packs),
        scratch=[
            pltpu.VMEM((tile, width), BF),
            pltpu.VMEM((tile, width), F32),
            pltpu.VMEM((tile, width), F32),
            pltpu.VMEM((tile, width), F32),
            pltpu.VMEM(lse[0].shape, F32),
            pltpu.VMEM((width, width), BF),
            pltpu.VMEM((width, width), BF),
        ],
        prefetch=1,
    )


def block_place(block, blocks, t, piece):
    rel, start, count = piece
    inside = block % blocks - start
    held = ((block // blocks) ^ t == rel) & (inside >= 0) & (inside < count)
    return held, jnp.where(held, inside, 0)


def anywhere():
    return pl.BlockSpec(memory_space=pl.ANY)


def fetch_block(t_ref, block, blocks, refs, pieces, target, semaphore):
    found = False
    for ref, piece in zip(refs, pieces):
        held, index = block_place(block, blocks, t_ref[0], piece)

        @pl.when(held)
        def _(ref=ref, index=index):
            pltpu.make_async_copy(ref.at[index], target, semaphore).start()

        found = held | found
    return found


def gather_pair(t_ref, refs, target):
    width = target.shape[1]
    local = refs[0].shape[0] // 2
    gather_rows(t_ref, [ref.at[:local, :] for ref in refs], target)
    gather_rows(t_ref, [ref.at[local:, :] for ref in refs], target, width)


def memory_body(t_ref, id_ref, *refs, pieces, first):
    count = len(pieces)
    packs, biases = refs[count : count + 4], refs[count + 4 : count + 8]
    kv_ref, chosen_ref, w_ref, x_ref, out_ref, in_sem, kv_sem, out_sem = refs[count + 8 + (0 if first else 2) :]
    blocks, length, width = x_ref.shape
    held = [
        fetch_block(t_ref, id_ref[slot], blocks, refs, pieces, x_ref.at[slot], in_sem.at[slot])
        for slot in range(blocks)
    ]
    gather_pair(t_ref, packs, w_ref)
    local = packs[0].shape[0] // 2
    bias = gather_bias(t_ref, biases, 2 * local, local)

    def copies(slot):
        rows = pl.ds(slot * length, length)
        return (
            pltpu.make_async_copy(out_ref.at[slot], kv_ref.at[rows, :], kv_sem.at[slot]),
            pltpu.make_async_copy(x_ref.at[slot], chosen_ref.at[rows, :], out_sem.at[slot]),
        )

    for slot in range(blocks):

        @pl.when(held[slot])
        def _(slot=slot):
            pltpu.make_async_copy(refs[0].at[0], x_ref.at[slot], in_sem.at[slot]).wait()
            kv = nt(x_ref[slot], w_ref[...])
            out_ref[slot, :, :width] = kv[:, :width].astype(BF)
            out_ref[slot, :, width:] = (kv[:, width:] + bias).astype(BF)
            for copy in copies(slot):
                copy.start()

    for slot in range(blocks):

        @pl.when(held[slot])
        def _(slot=slot):
            for copy in copies(slot):
                copy.wait()


def memory_rows(name, t, ids, memories, pieces, packs, local, earlier=None):
    blocks = ids.shape[0]
    _, length, width = memories[0].shape
    outs = [shape_of((blocks * length, 2 * width), BF), shape_of((blocks * length, width), BF)]
    more = () if earlier is None else tuple(earlier)
    count = 2 + len(memories) + 8
    return call(
        functools.partial(memory_body, pieces=pieces, first=earlier is None),
        name,
        (1,),
        [anywhere()] * len(memories)
        + pack_rows(2 * local, width, 1)
        + pack_rows(16, width, 5 * local // 16)
        + [anywhere()] * len(more),
        [anywhere()] * 2,
        outs,
        (t, ids, *memories, *packs, *packs, *more),
        scratch=[
            pltpu.VMEM((2 * width, width), BF),
            pltpu.VMEM((blocks, length, width), BF),
            pltpu.VMEM((blocks, length, 2 * width), BF),
            pltpu.SemaphoreType.DMA((blocks,)),
            pltpu.SemaphoreType.DMA((blocks,)),
            pltpu.SemaphoreType.DMA((blocks,)),
        ],
        prefetch=2,
        aliases={count: 0, count + 1: 1} if more else {},
    )


def block_grad_body(t_ref, dkv_ref, w0, w1, w2, w3, out_ref, w_ref):
    gather_pair(t_ref, (w0, w1, w2, w3), w_ref)
    out_ref[...] = nn(dkv_ref[...], w_ref[...]).astype(BF).reshape(out_ref.shape)


def block_grad(t, half, dkv, packs, local, blocks):
    rows, width = dkv.shape[0], dkv.shape[1] // 2
    length = rows // blocks
    steps = blocks // 4
    return call(
        block_grad_body,
        f"block_grad_{half}",
        (steps,),
        [pl.BlockSpec((2 * length, 2 * width), lambda i, *_: (half * steps + i, 0))] + pack_rows(2 * local, width, 1),
        pl.BlockSpec((2, length, width), lambda i, *_: (i, 0, 0)),
        shape_of((blocks // 2, length, width), BF),
        (t, dkv, *packs),
        scratch=[pltpu.VMEM((2 * width, width), BF)],
        prefetch=1,
    )


def return_body(t_ref, id_ref, *refs, pieces):
    out_ref, x_ref, semaphores = refs[len(pieces) :]
    blocks = id_ref.shape[0]
    step, steps = pl.program_id(0), pl.num_programs(0)
    sides = x_ref.shape[1]

    def fetch(at):
        for side in range(sides):
            slot = at % 2
            block = id_ref[at * sides + side]
            fetch_block(t_ref, block, blocks, refs, pieces, x_ref.at[slot, side], semaphores.at[slot, side])

    @pl.when(step == 0)
    def _():
        fetch(0)

    @pl.when(step + 1 < steps)
    def _():
        fetch(step + 1)

    now = step % 2
    for side in range(sides):
        pltpu.make_async_copy(refs[0].at[0], x_ref.at[now, side], semaphores.at[now, side]).wait()
        out_ref[side] = x_ref[now, side].astype(out_ref.dtype)


def return_blocks(t, slots, grads, pieces):
    blocks = slots.shape[0]
    sides = 4
    _, length, width = grads[0].shape
    return call(
        functools.partial(return_body, pieces=pieces),
        "return_blocks",
        (blocks // sides,),
        [anywhere()] * len(grads),
        pl.BlockSpec((sides, length, width), lambda i, *_: (i, 0, 0)),
        shape_of((blocks, length, width), F32),
        (t, slots, *grads),
        scratch=[pltpu.VMEM((2, sides, length, width), BF), pltpu.SemaphoreType.DMA((2, sides))],
        prefetch=2,
    )


def feed_body(ma, mb, ga, gb, w1_ref, w2_ref, b1_ref, oa, ob, da, db, ha, hb, ua, ub, sum_ref):
    curve = math.sqrt(2.0 / math.pi)
    total = None
    for m_ref, g_ref, out_ref, dm_ref, h_ref, du_ref in ((ma, ga, oa, da, ha, ua), (mb, gb, ob, db, hb, ub)):
        u = nn(m_ref[...], w1_ref[...]) + b1_ref[...]
        square = u * u
        bent = jnp.tanh(curve * (u + 0.044715 * u * square))
        half = 0.5 * (1.0 + bent)
        h = (u * half).astype(BF)
        h_ref[...] = h
        slope = half + 0.5 * u * (1.0 - bent * bent) * (curve * (1.0 + 3.0 * 0.044715 * square))
        du = (nt(g_ref[...], w2_ref[...]) * slope).astype(BF)
        du_ref[...] = du
        dm_ref[...] = nt(du, w1_ref[...]).astype(BF)
        out_ref[...] = nn(h, w2_ref[...]).astype(BF)
        part = column_sum(du.astype(F32))
        total = part if total is None else total + part
    add_rows(sum_ref, [total])


def feed(name, half, ms, gs, w1, w2, b1):
    rows, width = ms[0].shape
    hidden = w1.shape[1]
    row, wide = shape_of((rows, width), BF), shape_of((rows, hidden), BF)
    outs = [row] * 4 + [wide] * 4 + [shape_of((8, hidden), F32)]
    return list(call(
        feed_body,
        name,
        (1,),
        [whole(row)] * 2 + [pl.BlockSpec((rows, width), lambda i: (half, 0))] * 2 + [whole(w1), whole(w2), whole(b1)],
        [whole(out) for out in outs],
        outs,
        (*ms, *gs, w1, w2, b1),
    ))


def feed_weight_body(*refs):
    out_ref = refs[-1]
    count = (len(refs) - 1) // 7
    ms, dus, hs, gs = refs[: 2 * count], refs[2 * count : 4 * count], refs[4 * count : 6 * count], refs[6 * count : -1]
    rows = dus[0].shape[0]
    half = pl.num_programs(0) // 2

    @pl.when(pl.program_id(0) < half)
    def _():
        out_ref[...] = sum(tn(m[...], du[...]) for m, du in zip(ms, dus)).astype(BF)

    @pl.when(pl.program_id(0) >= half)
    def _():
        total = 0.0
        for index, h in enumerate(hs):
            side = index % 2
            total = total + tn(h[...], gs[index // 2][side * rows : (side + 1) * rows, :])
        out_ref[...] = total.astype(BF)


def feed_weight(ms, dus, hs, gs):
    rows, width = ms[0].shape
    hidden = hs[0].shape[1]
    tile = 256
    first, second = width // tile, hidden // tile
    return call(
        feed_weight_body,
        "feed_weight",
        (first + second,),
        [pl.BlockSpec((rows, tile), lambda i: (0, jnp.minimum(i, first - 1)))] * len(ms)
        + [whole(r) for r in dus]
        + [pl.BlockSpec((rows, tile), lambda i: (0, jnp.maximum(i - first, 0)))] * len(hs)
        + [whole(r) for r in gs],
        rows_of(tile, width),
        shape_of((width + hidden, width), BF),
        (*ms, *dus, *hs, *gs),
    )


def cross_weight_body(t_ref, *refs):
    count = (len(refs) - 5) // 2
    sources, (out0, out1, out2, out3), buffers, semaphores = refs[:count], refs[count : count + 4], refs[count + 4 : -1], refs[-1]
    outs = (out0, out1, out2, out3)
    local, width = out0.shape[1:]
    copies = [
        pltpu.make_async_copy(source, buffer, semaphores.at[index])
        for index, (source, buffer) in enumerate(zip(sources, buffers))
    ]
    for copy in copies:
        copy.start()
    dqc, b, o0, o1, o2, o3, g1, co_a, co_b, g2, memory, dkv = buffers

    def place(index, grad):
        for group in range(4):
            part = grad[group * local : (group + 1) * local].astype(BF)
            for rel, out_ref in enumerate(outs):

                @pl.when(t_ref[0] ^ rel == group)
                def _(out_ref=out_ref, part=part):
                    out_ref[index] = part

    copies[0].wait()
    copies[1].wait()
    place(0, tn(dqc[...], b[...]))
    for copy in copies[2:7]:
        copy.wait()
    for out_ref, o_ref in zip(outs, (o0, o1, o2, o3)):
        out_ref[1] = nn(o_ref[...], g1[...]).astype(BF)
    for copy in copies[7:10]:
        copy.wait()
    half = co_a.shape[0]
    place(4, tn(co_a[...], g2[:half, :]) + tn(co_b[...], g2[half:, :]))
    copies[10].wait()
    copies[11].wait()
    place(2, tn(dkv[:, :width], memory[...]))
    place(3, tn(dkv[:, width:], memory[...]))


def cross_weight(t, dqc, b, mixed, g1r, dkv, memory, co, g2r):
    width = b.shape[1]
    local = mixed[0].shape[0]
    args = (dqc, b, *mixed, g1r, *co, g2r, memory, dkv)
    out = shape_of((5, local, width), BF)
    return call(
        cross_weight_body,
        "cross_weight",
        (1,),
        [anywhere()] * len(args),
        [whole(out)] * 4,
        [out] * 4,
        (t, *args),
        scratch=[pltpu.VMEM(a.shape, a.dtype) for a in args] + [pltpu.SemaphoreType.DMA((len(args),))],
        prefetch=1,
    )


def input_grad_body(x_ref, da_ref, db_ref, dc_ref, g1_ref, gain_ref, out_ref):
    normed, inverse = standardize(x_ref[...].astype(F32))
    grad = da_ref[...].astype(F32) + db_ref[...].astype(F32) + dc_ref[...].astype(F32)
    out_ref[...] = g1_ref[...] + norm_pull(grad, normed, inverse, gain_ref[0:1, :])


def input_grad(x, parts, g1, gain):
    rows, width = x.shape
    tile = min(256, rows)
    row = rows_of(tile, width)
    return call(
        input_grad_body,
        "input_grad",
        (rows // tile,),
        [row] * 5 + [whole(gain)],
        row,
        shape_of((rows, width), F32),
        (x, *parts, g1, gain),
    )


def padded_tables(length):
    half = HEAD_DIM // 2
    frequency = np.float32(10000.0) ** (-np.arange(half, dtype=np.float32) / np.float32(half))
    angles = np.arange(length, dtype=np.float32)[:, None] * frequency[None, :]
    cosine = np.cos(angles.astype(np.float64)).astype(np.float32)
    sine = np.sin(angles.astype(np.float64)).astype(np.float32)
    zero = np.zeros_like(sine)
    return (
        jnp.asarray(np.concatenate([cosine, cosine, zero, zero], 1)),
        jnp.asarray(np.concatenate([-sine, zero, zero, zero], 1)),
        jnp.asarray(np.concatenate([zero, sine, zero, zero], 1)),
    )


def mask_lanes(segments):
    lane = lax.broadcasted_iota(jnp.int32, (segments.shape[0], LANES), 1)
    is_mask = (lane >= MASK_LANE) & (lane < MASK_LANE + DOCS)
    same = is_mask & (lane - MASK_LANE == segments[:, None])
    is_lse = (lane >= LSE_LANE) & (lane < LSE_LANE + 3)
    query_lanes = jnp.where(same, 1.0, 0.0).astype(BF)
    key_lanes = jnp.where(is_mask & ~same, NEGATIVE, jnp.where(is_lse, 1.0, 0.0)).astype(BF)
    return query_lanes, key_lanes


def pad_heads(values):
    lead = values.shape[:-1]
    heads = values.shape[-1] // HEAD_DIM
    values = values.reshape(lead + (heads, HEAD_DIM))
    values = jnp.pad(values, [(0, 0)] * (len(lead) + 1) + [(0, LANES - HEAD_DIM)])
    return values.reshape(lead[:-1] + (-1,))


def shards(
    layer_input,
    norm_gain,
    norm_bias,
    self_input_weight,
    self_input_bias,
    self_output_weight,
    out_bias,
    cross_query_weight,
    b_cross_q,
    w_cross_kv,
    b_cross_v,
    cross_output_weight,
    expand_weight_1,
    expand_bias_1,
    contract_weight_2,
    neighbours,
    segment_ids,
    span_map,
    cotangent,
):
    x = layer_input[0]
    rows, width = x.shape
    length = segment_ids.shape[1]
    local = self_input_weight.shape[2]
    heads = local // HEAD_DIM
    blocks, block_rows = neighbours.shape[1], neighbours.shape[2]
    grad_out = cotangent[0]
    index = lax.axis_index("tp")
    t = index.astype(jnp.int32).reshape(1)
    partners = [[(i, i ^ step) for i in range(4)] for step in (1, 2, 3)]

    tables = padded_tables(length)
    b_pad = pad_heads(self_input_bias)[None]
    piece = -(-(5 * local + 16) // (16 * lax.axis_size("dp"))) * 16
    w_pad, pack = prepare(
        self_input_weight.transpose(1, 2, 0),
        cross_query_weight.T,
        self_output_weight,
        w_cross_kv.transpose(1, 2, 0),
        cross_output_weight,
        b_cross_q[None],
        b_cross_v[None],
        piece * lax.axis_size("dp"),
    )
    qx, kx = mask_lanes(segment_ids[0])
    lane = lax.broadcasted_iota(jnp.int32, (1, LANES), 1)
    vx = jnp.where((lane >= HEAD_DIM) & (lane < HEAD_DIM + 3), 1.0, 0.0).astype(BF)
    core, chip, _ = partners

    half = blocks // 2

    across = lax.ppermute(x, "tp", chip)
    beside = lax.ppermute(x, "tp", core)
    a0, a1, c0, c1 = project_rows((0, 1), t, (x, beside), norm_gain, norm_bias, w_pad, b_pad, tables, heads)
    across, c0 = lax.optimization_barrier((across, c0))
    pack_piece, blocks_first, across = lax.optimization_barrier(
        (take_rows(pack, lax.axis_index("dp"), piece), neighbours[0][:half], across)
    )
    pack_piece = lax.ppermute(pack_piece, "tp", chip)
    blocks_first = lax.ppermute(blocks_first, "tp", chip)
    pack_across = lax.all_gather(pack_piece, "dp", axis=0, tiled=True)
    pack_beside = lax.ppermute(pack, "tp", core)
    xs = [x, beside, across, lax.ppermute(across, "tp", core)]
    blocks_beside = lax.ppermute(neighbours[0], "tp", core)
    a2, a3, c2, c3 = project_rows((2, 3), t, xs[2:], norm_gain, norm_bias, w_pad, b_pad, tables, heads)
    qe, ke, ve, ot, lse = attend(t, (c0, c1, c2, c3), qx, kx, vx)
    normed_first = [a0, a1, a2, a3]
    ot, blocks_first = follow(ot, blocks_first)
    mixed = exchange([ot[0], ot[1], ot[2], ot[3]], partners)
    blocks_second, mixed = follow(neighbours[0][half:], tuple(mixed))
    blocks_second = lax.ppermute(blocks_second, "tp", chip)
    packs = [pack, pack_beside, pack_across, lax.ppermute(pack_across, "tp", core)]

    block_ids = index * blocks + jnp.arange(blocks, dtype=jnp.int32)
    slot_ids = jnp.arange(span_map.shape[1], dtype=jnp.int32)
    slots = jnp.sum(jnp.where(span_map[0][None, :] == block_ids[:, None], slot_ids[None, :], 0), 1)
    chosen_ids = lax.dynamic_slice_in_dim(span_map[0], index * blocks, blocks, 0)

    x1, b, cq = after_attend(t, x, mixed, packs, out_bias, norm_gain, norm_bias)
    memories = [neighbours[0], blocks_beside, blocks_first, lax.ppermute(blocks_first, "tp", core)]
    pieces = [(0, 0, blocks), (1, 0, blocks), (2, 0, half), (3, 0, half)]
    memory_near = memory_rows("memory_near", t, chosen_ids, memories, pieces, packs, local)
    gathered, blocks_second, cq, memory_near = lax.optimization_barrier(
        (grad_out.astype(BF), blocks_second, cq, tuple(memory_near))
    )
    memories = [blocks_second, lax.ppermute(blocks_second, "tp", core)]
    pieces = [(2, half, half), (3, half, half)]
    grad_across = lax.ppermute(gathered, "tp", chip)
    grad_beside = lax.ppermute(gathered, "tp", core)
    kv, memory = memory_rows("memory_far", t, chosen_ids, memories, pieces, packs, local, memory_near)
    cross_args = (packs, local, out_bias, norm_gain, norm_bias)
    co_a, cross_lse_a, x2_a, m_a = cross(t, 0, cq, kv, x1, *cross_args)
    x1_late, m_a = lax.optimization_barrier((x1, m_a))
    co_b, cross_lse_b, x2_b, m_b = cross(t, 1, cq, kv, x1_late, *cross_args)

    feed_args = (expand_weight_1, contract_weight_2, expand_bias_1[None])
    m_a, grad_across = follow(m_a, grad_across)
    across_a = lax.ppermute(m_a, "tp", chip)
    beside_a = lax.ppermute(m_a, "tp", core)
    gs = [gathered, grad_beside, grad_across, lax.ppermute(grad_across, "tp", core)]
    near_a = feed("feed_near_0", 0, (m_a, beside_a), gs[:2], *feed_args)
    across_b = lax.ppermute(m_b, "tp", chip)
    beside_b = lax.ppermute(m_b, "tp", core)
    across_a, near_a[0] = lax.optimization_barrier((across_a, near_a[0]))
    diagonal_a = lax.ppermute(across_a, "tp", core)
    near_b = feed("feed_near_1", 1, (m_b, beside_b), gs[:2], *feed_args)
    diagonal_a, across_b, near_b[0] = lax.optimization_barrier((diagonal_a, across_b, near_b[0]))
    diagonal_b = lax.ppermute(across_b, "tp", core)
    far_a = feed("feed_far_0", 0, (across_a, diagonal_a), gs[2:], *feed_args)
    diagonal_b, far_a[0] = lax.optimization_barrier((diagonal_b, far_a[0]))
    far_b = feed("feed_far_1", 1, (across_b, diagonal_b), gs[2:], *feed_args)
    dm_a, _ = collect([*near_a[2:4], *far_a[2:4]], partners)
    dm_b, _ = collect([*near_b[2:4], *far_b[2:4]], partners)
    ms = [m_a, m_b, beside_a, beside_b, across_a, across_b, diagonal_a, diagonal_b]
    ordered = [(near_a, 0), (near_b, 0), (near_a, 1), (near_b, 1), (far_a, 0), (far_b, 0), (far_a, 1), (far_b, 1)]
    grad_feed = feed_weight(ms, [f[6 + i] for f, i in ordered], [f[4 + i] for f, i in ordered], gs)
    grad_b1 = near_a[8] + near_b[8] + far_a[8] + far_b[8]

    out_far = [lax.ppermute(part[1], "tp", core) for part in (far_a, far_b, near_a, near_b)]
    out_sent = (rounded_sum(far_a[0], out_far[0]), rounded_sum(far_b[0], out_far[1]))
    dm_a[2], dm_b[2], grad_feed = lax.optimization_barrier((dm_a[2], dm_b[2], grad_feed))
    summed_feed = lax.psum(grad_feed, "dp")
    g2r, dkv, g1, g1r, dqc, *dos, small_middle = middle_back(
        t, (x2_a, x2_b), (dm_a, dm_b), (cross_lse_a, cross_lse_b), grad_out, packs, local, norm_gain, cq, kv, x1
    )

    dos = exchange(dos, partners)
    dos[1], g1r = lax.optimization_barrier((dos[1], g1r))
    grad_cross = cross_weight(t, dqc, b, mixed, g1r, dkv, memory, (co_a, co_b), g2r)
    dos[2], dos[3], grad_cross, out_sent = lax.optimization_barrier((dos[2], dos[3], tuple(grad_cross), out_sent))
    out_across = tuple(lax.ppermute(part, "tp", chip) for part in out_sent)
    grad_far = [lax.ppermute(grad_cross[r], "tp", core) for r in (3, 1)]
    dp = attend_back(t, qe, ke, ve, dos, ot, lse, tables)
    dp, grad_far[0], out_across = lax.optimization_barrier((dp, grad_far[0], out_across))
    across = lax.ppermute(rounded_sum(grad_cross[2], grad_far[0]), "tp", chip)
    grad_qkv, grad_bqkv = qkv_weight(dp, normed_first)
    da3, da1, small_a = input_back((3, 1), (xs[3], xs[1]), dp, w_pad)
    da2, da0, small_b = input_back((2, 0), (xs[2], xs[0]), dp, w_pad)
    dkv, small_a, small_b = lax.optimization_barrier((dkv, small_a, small_b))
    grad_near = [block_grad(t, side, dkv, packs, local, blocks) for side in range(2)]
    (da0, da1, da2, da3, grad_qkv, small_zero, grad_near, grad_far[1], summed_feed) = lax.optimization_barrier(
        (da0, da1, da2, da3, grad_qkv, small_a + small_b, tuple(grad_near), grad_far[1], summed_feed)
    )

    da, across = collect([da0, da1, da2, da3], partners, across)
    grad_near, da[2] = follow(grad_near, da[2])
    own = rounded_sum(grad_cross[0], grad_far[1], across).reshape(5 * local, width)
    summed_cross = lax.psum(own, "dp")
    grad_first, grad_second = [lax.ppermute(value, "tp", chip) for value in grad_near]
    small = jnp.concatenate([small_zero[:2], small_middle[:9], jnp.zeros((5, width), F32)], 0)
    small = small + lax.ppermute(small, "tp", core)
    small = small + lax.ppermute(small, "tp", chip)
    returned = [*grad_near] + [lax.ppermute(value, "tp", core) for value in grad_near]
    returned += [grad_first, grad_second] + [lax.ppermute(value, "tp", core) for value in (grad_first, grad_second)]
    halves = [(rel, start, half) for rel in range(4) for start in (0, half)]
    grad_memory = return_blocks(t, slots, returned, halves)
    summed_cross, grad_memory = lax.optimization_barrier((summed_cross, grad_memory))
    grad_input = input_grad(x, da, g1, norm_gain)
    kept = jnp.concatenate([rounded_sum(near_a[0], out_far[2]), rounded_sum(near_b[0], out_far[3])], 0)
    layer_output = jnp.concatenate([x2_a, x2_b], 0) + kept.astype(F32) + jnp.concatenate(out_across, 0).astype(F32) + out_bias[2]

    bqkv_row = grad_bqkv.reshape(3, heads, LANES)[:, :, :HEAD_DIM].reshape(1, -1)
    bqkv_row = jnp.pad(bqkv_row, ((0, 0), (0, width - 3 * local)))
    tail = jnp.concatenate([bqkv_row, grad_b1[:1], jnp.zeros((14, width), F32)], 0)
    last = jnp.concatenate([grad_qkv, small.astype(BF), tail.astype(BF)], 0)
    summed = sum_over_dp(last).astype(F32)

    summed_feed = summed_feed.astype(F32)
    hidden = expand_weight_1.shape[1]
    grad_qkv = summed[: 3 * local].T.reshape(width, 3, local)
    summed_cross = summed_cross.astype(F32)
    own = summed_cross.reshape(5, local, width)
    small = summed[3 * local : 3 * local + 16]
    bqkv = summed[3 * local + 16, : 3 * local].reshape(3, local)

    def mine(row):
        return lax.dynamic_slice_in_dim(row, index * local, local, 0)

    return (
        layer_output[None],
        grad_input[None],
        grad_memory[None],
        jnp.stack([small[0], small[2], small[4]]),
        jnp.stack([small[1], small[3], small[5]]),
        grad_qkv,
        bqkv,
        own[1],
        jnp.stack([small[6], small[7], small[8]]),
        own[0].T,
        mine(small[9]),
        jnp.stack([own[2].T, own[3].T], 1),
        mine(small[10]),
        own[4],
        summed_feed[:width],
        summed[3 * local + 17],
        summed_feed[width : width + hidden],
    )


def solution(mesh):
    return jax.shard_map(
        shards,
        mesh=mesh,
        in_specs=(
            P("dp", "tp", None),
            P(),
            P(),
            P(None, None, "tp"),
            P(None, "tp"),
            P("tp", None),
            P(),
            P(None, "tp"),
            P("tp"),
            P(None, None, "tp"),
            P("tp"),
            P("tp", None),
            P(None, "tp"),
            P("tp"),
            P("tp", None),
            P("dp", "tp", None, None),
            P("dp", None),
            P("dp", None),
            P("dp", "tp", None),
        ),
        out_specs=(
            P("dp", "tp", None),
            P("dp", "tp", None),
            P("dp", "tp", None, None),
            P(),
            P(),
            P(None, None, "tp"),
            P(None, "tp"),
            P("tp", None),
            P(),
            P(None, "tp"),
            P("tp"),
            P(None, None, "tp"),
            P("tp"),
            P("tp", None),
            P(None, "tp"),
            P("tp"),
            P("tp", None),
        ),
        check_vma=False,
    )
```

time: 664 us -> 460 us (0.69)
  waiting for transfers between devices: 257 us -> 123 us
  Pallas kernels: 242 us -> 213 us
  other arithmetic: 42.7 us -> 24.9 us
  matrix products: 17.4 us -> 0 us
  local copies, waits for them, and re-layouts: 52.4 us -> 36.5 us
  starting transfers between devices: 30.5 us -> 43.5 us
    psum x2, waiting for transfers between devices: 121 us -> 18.7 us  [the longest x1 18.5 us: shards(): summed_cross = lax.psum(own, 'dp')]
    pallas_call x27 -> x24, Pallas kernels: 242 us -> 213 us  [call(): pl.pallas_call(body, out_shape=out_shape, grid_spec=pltpu.PrefetchScalarG...]
    ppermute x33 -> x46, waiting for transfers between devices: 119 us -> 92.8 us  [the longest x2 32.8 us: shards(): lax.ppermute(value, 'tp', chip)]
    dot_general x2 -> x0, matrix products: 17.4 us -> none  [the longest x1 9.61 us: shards(): lax.dot_general(dkv, weight_kv, (((1,), (0,)), ((), ())), preferred_eleme...]
    ppermute x33 -> x46, starting transfers between devices: 22.4 us -> 36.3 us  [the longest x8 10.9 us: swap(): return lax.ppermute(values, 'dp', [(i, i ^ step) for i in range(size)])]
    convert_element_type x14 -> x12, other arithmetic: 17.8 us -> 11.6 us  [the longest x8 9.73 us: rounded_sum(): return sum((part.astype(F32) for part in parts)).astype(BF)]
    unnamed x132 -> x108, local copies, waits for them, and re-layouts: 18.4 us -> 12.6 us
  transfers between devices with their start and end apart: 51 -> 63, of which waited for: 22 -> 24; matrix products, arithmetic and copies ran while one was open for 13% -> 10% of each run, Pallas kernels for 24% -> 47%
where the time goes in v2:
time: 460 us; the launch traced here: 455 us
  Pallas kernels  213 us (46%)
  waiting for transfers between devices  123 us (27%)
  starting transfers between devices  43.5 us (9%)
  local copies, waits for them, and re-layouts  36.5 us (8%)
  other arithmetic  24.9 us (5%)
  between operations  14.7 us (3%)
    pallas_call x24, Pallas kernels, call(): pl.pallas_call(body, out_shape=out_shape, grid_spec=pltpu.PrefetchScalarG...  213 us
    ppermute x2, waiting for transfers between devices, shards(): lax.ppermute(value, 'tp', chip)  32.8 us
    ppermute x8, waiting for transfers between devices, swap(): return lax.ppermute(values, 'dp', [(i, i ^ step) for i in range(size)])  24.8 us
    psum x1, waiting for transfers between devices, shards(): summed_cross = lax.psum(own, 'dp')  18.5 us
    unnamed x108, local copies, waits for them, and re-layouts  12.6 us
    ppermute x8, starting transfers between devices, swap(): return lax.ppermute(values, 'dp', [(i, i ^ step) for i in range(size)])  10.9 us
    ppermute x1, waiting for transfers between devices, shards(): blocks_second = lax.ppermute(blocks_second, 'tp', chip)  9.84 us
    convert_element_type x8, other arithmetic, rounded_sum(): return sum((part.astype(F32) for part in parts)).astype(BF)  9.73 us
  transfers between devices with their start and end apart: 63, of which 24 were waited for; matrix products, arithmetic and copies ran while one was open for 10% of the time, Pallas kernels for 47%

profile of v2, /device:TPU:0, one launch (start us, length us, event | category | flops | bytes accessed | tf_op | source)
XLA Modules:
  0.0 455.4 jit_solution(11573176942810343042)
XLA Ops:
  20.3 6.6 %qkv_01.1 = (bf16[512,768]{1,0:T(8,128)(2,1)}, bf16[512,768]{1,0:T(8,128)(2,1)}, bf16[3,3,512,128]{3,2,1,0:T(8,128)(2,1)}, bf16[3,3,512,128]{3,2,1,0:T(8,128)(2,1)}) custom-call(s32[1]{0:T(128)} %bitcast.t_ref, bf16[512,768]{1,0:T(8,128)(2,1)} %bitcast.80, bf16[512,768]{1,0:T(8,128)(2,1)} %copy-done.9, f32[3,768]{1,0:T(4,128)} %gain_ref.13, ...), custom_call_target="tpu_custom_call" | custom-call | flops 66000000 | bytes 1 | tf_op jit(solution)/shard_map/qkv_01/pallas_call | solution.py:61
  45.7 6.6 %qkv_23.1 = (bf16[512,768]{1,0:T(8,128)(2,1)}, bf16[512,768]{1,0:T(8,128)(2,1)}, bf16[3,3,512,128]{3,2,1,0:T(8,128)(2,1)}, bf16[3,3,512,128]{3,2,1,0:T(8,128)(2,1)}) custom-call(s32[1]{0:T(128)} %bitcast.t_ref, bf16[512,768]{1,0:T(8,128)(2,1)} %copy-done.10, bf16[512,768]{1,0:T(8,128)(2,1)} %copy-done.11, f32[3,768]{1,0:T(4,128)} %gain_ref.13, ...), custom_call_target="tpu_custom_call" | custom-call | flops 66000000 | bytes 1 | tf_op jit(solution)/shard_map/qkv_23/pallas_call | solution.py:61
  52.3 18.0 %attend.1 = (bf16[3,2048,128]{2,1,0:T(8,128)(2,1)}, bf16[3,2048,128]{2,1,0:T(8,128)(2,1)}, bf16[3,2048,128]{2,1,0:T(8,128)(2,1)}, bf16[4,192,512]{2,1,0:T(8,128)(2,1)}, f32[3,1,2048]{2,1,0:T(1,128)}) custom-call(s32[1]{0:T(128)} %bitcast.t_ref, bf16[3,3,512,128]{3,2,1,0:T(8,128)(2,1)} %get-tuple-element.172.c0, ...), custom_call_target="tpu_custom_call" | custom-call | flops 180000000 | bytes 1 | tf_op jit(solution)/shard_map/attend/pallas_call | solution.py:61
  89.5 5.8 %after_attend.1 = (f32[512,768]{1,0:T(8,128)}, bf16[512,768]{1,0:T(8,128)(2,1)}, bf16[512,768]{1,0:T(8,128)(2,1)}) custom-call(s32[1]{0:T(128)} %bitcast.t_ref, bf16[512,768]{1,0:T(8,128)(2,1)} %bitcast.81, bf16[192,512]{1,0:T(8,128)(2,1)} %get-tuple-element.183.o0.refs_2_, bf16[192,512]{1,0:T(8,128)(2,1)} %collective-permute-done.4.o1.refs_3_, ...), custom_call_target="tpu_custom_call" | custom-call | flops 60000000 | bytes 1 | tf_op jit(solution)/shard_map/after_attend/pallas_call | solution.py:61
  95.3 17.6 %memory_near.1 = (bf16[2048,1536]{1,0:T(8,128)(2,1)}, bf16[2048,768]{1,0:T(8,128)(2,1)}) custom-call(s32[1]{0:T(128)} %bitcast.t_ref, s32[16]{0:T(128)} %fusion.6.id_ref, bf16[16,128,768]{2,1,0:T(8,128)(2,1)} %bitcast.16.refs_0_, bf16[16,128,768]{2,1,0:T(8,128)(2,1)} %collective-permute-done.11.refs_1_, bf16[8,128,768]{2,1,0:T(8,128)(2,1)} %copy-done.21, ...), custom_call_target="tpu_custom_call" | custom-call | flops 120000000 | bytes 1 | tf_op jit(solution)/shard_map/memory_near/pallas_call | solution.py:61
  112.9 9.8 %collective-permute-done.7.refs_0_ = bf16[8,128,768]{2,1,0:T(8,128)(2,1)} collective-permute-done((bf16[8,128,768]{2,1,0:T(8,128)(2,1)}, bf16[8,128,768]{2,1,0:T(8,128)(2,1)}, u32[]{:S(2)}, u32[]{:S(2)}) %collective-permute-start.7) | collective-permute-done | bytes 1572896 | tf_op jit(solution)/shard_map/ppermute | solution.py:1134
  127.5 6.4 %memory_far.1 = (bf16[2048,1536]{1,0:T(8,128)(2,1)}, bf16[2048,768]{1,0:T(8,128)(2,1)}) custom-call(s32[1]{0:T(128)} %bitcast.t_ref, s32[16]{0:T(128)} %fusion.6.id_ref, bf16[8,128,768]{2,1,0:T(8,128)(2,1)} %collective-permute-done.7.refs_0_, bf16[8,128,768]{2,1,0:T(8,128)(2,1)} %copy-done.14, ...), custom_call_target="tpu_custom_call", output_to_operand_aliasing={{0}: (12, {}), {1}: (13, {})} | custom-call | flops 50000000 | bytes 1 | tf_op jit(solution)/shard_map/memory_far/pallas_call | solution.py:61
  134.0 5.9 %cross_0.1 = (bf16[256,768]{1,0:T(8,128)(2,1)}, f32[4,8,128]{2,1,0:T(8,128)}, f32[256,768]{1,0:T(8,128)}, bf16[256,768]{1,0:T(8,128)(2,1)}) custom-call(s32[1]{0:T(128)} %bitcast.t_ref, bf16[512,768]{1,0:T(8,128)(2,1)} %get-tuple-element.192.cq_ref, bf16[2048,1536]{1,0:T(8,128)(2,1)} %get-tuple-element.196.kv_ref, f32[512,768]{1,0:T(8,128)} %get-tuple-element.200.x1_ref, ...), custom_call_target="tpu_custom_call" | custom-call | flops 60000000 | bytes 1 | tf_op jit(solution)/shard_map/cross_0/pallas_call | solution.py:61
  147.1 5.9 %cross_1.1 = (bf16[256,768]{1,0:T(8,128)(2,1)}, f32[4,8,128]{2,1,0:T(8,128)}, f32[256,768]{1,0:T(8,128)}, bf16[256,768]{1,0:T(8,128)(2,1)}) custom-call(s32[1]{0:T(128)} %bitcast.t_ref, bf16[512,768]{1,0:T(8,128)(2,1)} %get-tuple-element.192.cq_ref, bf16[2048,1536]{1,0:T(8,128)(2,1)} %get-tuple-element.196.kv_ref, f32[512,768]{1,0:T(8,128)} %get-tuple-element.200.x1_ref, ...), custom_call_target="tpu_custom_call" | custom-call | flops 60000000 | bytes 1 | tf_op jit(solution)/shard_map/cross_1/pallas_call | solution.py:61
  155.2 6.2 %feed_near_0.1 = (bf16[256,768]{1,0:T(8,128)(2,1)}, bf16[256,768]{1,0:T(8,128)(2,1)}, bf16[256,768]{1,0:T(8,128)(2,1)}, bf16[256,768]{1,0:T(8,128)(2,1)}, bf16[2...) custom-call(bf16[256,768]{1,0:T(8,128)(2,1)} %get-tuple-element.204., ...), custom_call_target="tpu_custom_call" | custom-call | flops 62000000 | bytes 1 | tf_op jit(solution)/shard_map/feed_near_0/pallas_call | solution.py:61
  162.4 6.2 %feed_near_1.1 = (bf16[256,768]{1,0:T(8,128)(2,1)}, bf16[256,768]{1,0:T(8,128)(2,1)}, bf16[256,768]{1,0:T(8,128)(2,1)}, bf16[256,768]{1,0:T(8,128)(2,1)}, bf16[2...) custom-call(bf16[256,768]{1,0:T(8,128)(2,1)} %get-tuple-element.209., ...), custom_call_target="tpu_custom_call" | custom-call | flops 62000000 | bytes 1 | tf_op jit(solution)/shard_map/feed_near_1/pallas_call | solution.py:61
  170.3 6.5 %feed_far_0.1 = (bf16[256,768]{1,0:T(8,128)(2,1)}, bf16[256,768]{1,0:T(8,128)(2,1)}, bf16[256,768]{1,0:T(8,128)(2,1)}, bf16[256,768]{1,0:T(8,128)(2,1)}, bf16[25...) custom-call(bf16[256,768]{1,0:T(8,128)(2,1)} %copy-done.16, ...), custom_call_target="tpu_custom_call" | custom-call | flops 62000000 | bytes 1 | tf_op jit(solution)/shard_map/feed_far_0/pallas_call | solution.py:61
  178.0 6.2 %feed_far_1.1 = (bf16[256,768]{1,0:T(8,128)(2,1)}, bf16[256,768]{1,0:T(8,128)(2,1)}, bf16[256,768]{1,0:T(8,128)(2,1)}, bf16[256,768]{1,0:T(8,128)(2,1)}, bf16[25...) custom-call(bf16[256,768]{1,0:T(8,128)(2,1)} %copy-done.18, ...), custom_call_target="tpu_custom_call" | custom-call | flops 62000000 | bytes 1 | tf_op jit(solution)/shard_map/feed_far_1/pallas_call | solution.py:61
  189.0 11.5 %feed_weight.1 = bf16[1536,768]{1,0:T(8,128)(2,1)} custom-call(bf16[256,768]{1,0:T(8,128)(2,1)} %get-tuple-element.204.ma.refs_0_, bf16[256,768]{1,0:T(8,128)(2,1)} %get-tuple-element.209.ma.refs_1_, bf16[256,768]{1,0:T(8,128)(2,1)} %copy-done.15, bf16[256,768]{1,0:T(8,128)(2,1)} %copy-done.17, bf16[256,768]{1,0:T(8,128)(2,1)} %copy-done.16, ...), custom_call_target="tpu_custom_call" | custom-call | flops 114000000 | bytes 1 | tf_op jit(solution)/shard_map/feed_weight/pallas_call | solution.py:61
  205.4 17.8 %middle_back.1 = (bf16[512,768]{1,0:T(8,128)(2,1)}, bf16[2048,1536]{1,0:T(8,128)(2,1)}, f32[512,768]{1,0:T(8,128)}, bf16[512,768]{1,0:T(8,128)(2,1)}, bf16[512,7...) custom-call(s32[1]{0:T(128)} %bitcast.t_ref, ...), custom_call_target="tpu_custom_call" | custom-call | flops 175000000 | bytes 1 | tf_op jit(solution)/shard_map/middle_back/pallas_call | solution.py:61
  225.4 15.4 %cross_weight.1 = (bf16[5,192,768]{2,1,0:T(8,128)(2,1)}, bf16[5,192,768]{2,1,0:T(8,128)(2,1)}, bf16[5,192,768]{2,1,0:T(8,128)(2,1)}, bf16[5,192,768]{2,1,0:T(8,128)(2,1)}) custom-call(s32[1]{0:T(128)} %bitcast.t_ref, bf16[512,768]{1,0:T(8,128)(2,1)} %get-tuple-element.255.refs_0_, bf16[512,768]{1,0:T(8,128)(2,1)} %get-tuple-element.256.refs_1_, ...), custom_call_target="tpu_custom_call" | custom-call | flops 178000000 | bytes 1 | tf_op jit(solution)/shard_map/cross_weight/pallas_call | solution.py:61
  249.7 25.1 %attend_back.1.da.db.dp_ref = bf16[4,3,3,512,128]{4,3,2,1,0:T(8,128)(2,1)} custom-call(s32[1]{0:T(128)} %bitcast.t_ref, bf16[3,2048,128]{2,1,0:T(8,128)(2,1)} %get-tuple-element.213.qe_ref, bf16[3,2048,128]{2,1,0:T(8,128)(2,1)} %get-tuple-element.214.ke_ref, bf16[3,2048,128]{2,1,0:T(8,128)(2,1)} %get-tuple-element.215.ve_ref, ...), custom_call_target="tpu_custom_call" | custom-call | flops 250000000 | bytes 1 | tf_op jit(solution)/shard_map/attend_back/pallas_call | solution.py:61
  284.7 5.8 %input_back_31.1 = (bf16[512,768]{1,0:T(8,128)(2,1)}, bf16[512,768]{1,0:T(8,128)(2,1)}, f32[8,768]{1,0:T(8,128)}) custom-call(bf16[512,768]{1,0:T(8,128)(2,1)} %copy-done.11, bf16[512,768]{1,0:T(8,128)(2,1)} %copy-done.9, bf16[4,3,3,512,128]{4,3,2,1,0:T(8,128)(2,1)} %attend_back.1.da.db.dp_ref, bf16[4,3,3,512,128]{4,3,2,1,0:T(8,128)(2,1)} %attend_back.1.da.db.dp_ref, ...), custom_call_target="tpu_custom_call" | custom-call | flops 57000000 | bytes 1 | tf_op jit(solution)/shard_map/input_back_31/pallas_call | solution.py:61
  291.3 6.5 %block_grad_1.1.refs_1_ = bf16[8,128,768]{2,1,0:T(8,128)(2,1)} custom-call(s32[1]{0:T(128)} %bitcast.t_ref, bf16[2048,1536]{1,0:T(8,128)(2,1)} %get-tuple-element.293.refs_11_.dkv_ref, bf16[1024,768]{1,0:T(8,128)(2,1)} %get-tuple-element.174.w0.q0.b0.refs_4_.refs_8_.refs_2_.refs_6_.c0, bf16[1024,768]{1,0:T(8,128)(2,1)} %copy-done.1, ...), custom_call_target="tpu_custom_call" | custom-call | flops 68000000 | bytes 1 | tf_op jit(solution)/shard_map/block_grad_1/pallas_call | solution.py:61
  297.8 6.5 %block_grad_0.1.refs_0_ = bf16[8,128,768]{2,1,0:T(8,128)(2,1)} custom-call(s32[1]{0:T(128)} %bitcast.t_ref, bf16[2048,1536]{1,0:T(8,128)(2,1)} %get-tuple-element.293.refs_11_.dkv_ref, bf16[1024,768]{1,0:T(8,128)(2,1)} %get-tuple-element.174.w0.q0.b0.refs_4_.refs_8_.refs_2_.refs_6_.c0, bf16[1024,768]{1,0:T(8,128)(2,1)} %copy-done.1, ...), custom_call_target="tpu_custom_call" | custom-call | flops 68000000 | bytes 1 | tf_op jit(solution)/shard_map/block_grad_0/pallas_call | solution.py:61
  304.2 7.7 %qkv_weight.1 = (bf16[576,768]{1,0:T(8,128)(2,1)}, f32[3,1,384]{2,1,0:T(1,128)}) custom-call(bf16[4,3,3,512,128]{4,3,2,1,0:T(8,128)(2,1)} %attend_back.1.da.db.dp_ref, bf16[512,768]{1,0:T(8,128)(2,1)} %get-tuple-element.284.a0, bf16[512,768]{1,0:T(8,128)(2,1)} %get-tuple-element.285.a1, bf16[512,768]{1,0:T(8,128)(2,1)} %get-tuple-element.286.a2, ...), custom_call_target="tpu_custom_call" | custom-call | flops 75000000 | bytes 1 | tf_op jit(solution)/shard_map/qkv_weight/pallas_call | solution.py:61
  363.1 14.4 %collective-permute-done.59 = bf16[4,80,768]{2,1,0:T(8,128)(2,1)S(1)} collective-permute-done((bf16[4,80,768]{2,1,0:T(8,128)(2,1)S(1)}, bf16[4,80,768]{2,1,0:T(8,128)(2,1)S(1)}, u32[]{:S(2)}, u32[]{:S(2)}) %collective-permute-start.59) | collective-permute-done | bytes 491552 | tf_op jit(solution)/shard_map/ppermute | solution.py:144
  380.6 30.4 %collective-permute-done.47.refs_5_ = bf16[8,128,768]{2,1,0:T(8,128)(2,1)} collective-permute-done((bf16[8,128,768]{2,1,0:T(8,128)(2,1)S(1)}, bf16[8,128,768]{2,1,0:T(8,128)(2,1)}, u32[]{:S(2)}, u32[]{:S(2)}) %collective-permute-start.47) | collective-permute-done | bytes 1572896 | tf_op jit(solution)/shard_map/ppermute | solution.py:1212
  425.6 18.5 %all-reduce.8.cloned.1.call-done = bf16[960,768]{1,0:T(8,128)(2,1)} async-done(((bf16[960,768]{1,0:T(8,128)(2,1)}), bf16[960,768]{1,0:T(8,128)(2,1)}) %all-reduce.8.cloned.1.call-update) | async-done | bytes 1474576 | tf_op jit(solution)/shard_map/psum | solution.py:1211
  (299 shorter events, 173.3 us)
Async XLA Ops:
  7.2 74.5 %all-gather.2.cloned.1.call-start = ((), (), s32[]{:S(2)}) async-start(), calls=%async_computation | async-start | bytes 1769472 | tf_op jit(solution)/shard_map/all_gather | solution.py:1124
  7.8 20.9 %collective-permute-start = (bf16[512,768]{1,0:T(8,128)(2,1)}, bf16[512,768]{1,0:T(8,128)(2,1)S(1)}, u32[]{:S(2)}, u32[]{:S(2)}) collective-permute-start(bf16[512,768]{1,0:T(8,128)(2,1)} %bitcast.79), channel_id=1, source_target_pairs={{0,2},{1,3},{2,0},{3,1},{4,6},{5,7},{6,4},{7,5},{8,10},{9,11},{10,... | collective-permute-start | bytes 2359304 | tf_op jit(solution)/shard_map/ppermute | solution.py:1115
  36.0 276.1 %all-reduce.6.cloned.1.call-start = ((), (), s32[]{:S(2)}) async-start(), calls=%async_computation.1 | async-start | bytes 4718592 | tf_op jit(solution)/shard_map/psum | solution.py:1185
  36.4 35.3 %collective-permute-start.3 = (bf16[8,128,768]{2,1,0:T(8,128)(2,1)S(1)}, bf16[8,128,768]{2,1,0:T(8,128)(2,1)S(1)}, u32[]{:S(2)}, u32[]{:S(2)}) collective-permute-start(bf16[8,128,768]{2,1,0:T(8,128)(2,1)S(1)} %get-tuple-element.180), channel_id=1, source_target_pairs={{0,2},{1,3},{2,0},{3,1},{4,6},{5,7},{6,4},{7,5},{8,10},{9,11},{10,... | collective-permute-start | bytes 4718600 | tf_op jit(solution)/shard_map/ppermute | solution.py:1123
  38.0 57.3 %collective-permute-start.11 = (bf16[16,128,768]{2,1,0:T(8,128)(2,1)}, bf16[16,128,768]{2,1,0:T(8,128)(2,1)}, u32[]{:S(2)}, u32[]{:S(2)}) collective-permute-start(bf16[16,128,768]{2,1,0:T(8,128)(2,1)} %bitcast.16.refs_0_), channel_id=1, source_target_pairs={{0,1},{1,0},{2,3},{3,2},{4,5},{5,4},{6,7},{7,6},{8,9},{9,8},{10,11... | collective-permute-start | bytes 9437192 | tf_op jit(solution)/shard_map/ppermute | solution.py:1127
  85.7 37.0 %collective-permute-start.7 = (bf16[8,128,768]{2,1,0:T(8,128)(2,1)}, bf16[8,128,768]{2,1,0:T(8,128)(2,1)}, u32[]{:S(2)}, u32[]{:S(2)}) collective-permute-start(bf16[8,128,768]{2,1,0:T(8,128)(2,1)} %get-tuple-element.182), channel_id=1, source_target_pairs={{0,2},{1,3},{2,0},{3,1},{4,6},{5,7},{6,4},{7,5},{8,10},{9,11},{10,... | collective-permute-start | bytes 4718600 | tf_op jit(solution)/shard_map/ppermute | solution.py:1134
  122.7 20.0 %collective-permute-start.14 = (bf16[512,768]{1,0:T(8,128)(2,1)S(1)}, bf16[512,768]{1,0:T(8,128)(2,1)S(1)}, u32[]{:S(2)}, u32[]{:S(2)}) collective-permute-start(bf16[512,768]{1,0:T(8,128)(2,1)S(1)} %bitcast_convert_fusion.ga.refs_24_), channel_id=1, source_target_pairs={{0,2},{1,3},{2,0},{3,1},{4,6},{5,7},{6,4},{7,5},{8,10},{9,11},{10,... | collective-permute-start | bytes 2359304 | tf_op jit(solution)/shard_map/ppermute | solution.py:1151
  123.0 30.5 %collective-permute-start.17 = (bf16[512,768]{1,0:T(8,128)(2,1)S(1)}, bf16[512,768]{1,0:T(8,128)(2,1)S(1)}, u32[]{:S(2)}, u32[]{:S(2)}) collective-permute-start(bf16[512,768]{1,0:T(8,128)(2,1)S(1)} %bitcast_convert_fusion.ga.refs_24_), channel_id=1, source_target_pairs={{0,1},{1,0},{2,3},{3,2},{4,5},{5,4},{6,7},{7,6},{8,9},{9,8},{10,11... | collective-permute-start | bytes 2359304 | tf_op jit(solution)/shard_map/ppermute | solution.py:1152
  146.5 22.6 %collective-permute-start.24 = (bf16[512,768]{1,0:T(8,128)(2,1)S(1)}, bf16[512,768]{1,0:T(8,128)(2,1)S(1)}, u32[]{:S(2)}, u32[]{:S(2)}) collective-permute-start(bf16[512,768]{1,0:T(8,128)(2,1)S(1)} %collective-permute-done.14.ga.refs_26_), channel_id=1, source_target_pairs={{0,1},{1,0},{2,3},{3,2},{4,5},{5,4},{6,7},{7,6},{8,9},{9,8},{10,11... | collective-permute-start | bytes 2359304 | tf_op jit(solution)/shard_map/ppermute | solution.py:1163
  189.0 36.2 %collective-permute-start.35 = (bf16[256,768]{1,0:T(8,128)(2,1)}, bf16[256,768]{1,0:T(8,128)(2,1)S(1)}, u32[]{:S(2)}, u32[]{:S(2)}) collective-permute-start(bf16[256,768]{1,0:T(8,128)(2,1)} %get-tuple-element.270), channel_id=1, source_target_pairs={{0,1},{1,0},{2,3},{3,2},{4,5},{5,4},{6,7},{7,6},{8,9},{9,8},{10,11... | collective-permute-start | bytes 1179656 | tf_op jit(solution)/shard_map/ppermute | solution.py:1182
  204.5 239.7 %all-reduce.8.cloned.1.call-start = ((), (), s32[]{:S(2)}) async-start(), calls=%async_computation.2 | async-start | bytes 2949120 | tf_op jit(solution)/shard_map/psum | solution.py:1211
  241.4 33.5 %collective-permute-start.36 = (bf16[5,192,768]{2,1,0:T(8,128)(2,1)}, bf16[5,192,768]{2,1,0:T(8,128)(2,1)}, u32[]{:S(2)}, u32[]{:S(2)}) collective-permute-start(bf16[5,192,768]{2,1,0:T(8,128)(2,1)} %get-tuple-element.274), channel_id=1, source_target_pairs={{0,1},{1,0},{2,3},{3,2},{4,5},{5,4},{6,7},{7,6},{8,9},{9,8},{10,11... | collective-permute-start | bytes 4423688 | tf_op jit(solution)/shard_map/ppermute | solution.py:1195
  241.7 70.2 %collective-permute-start.39 = (bf16[5,192,768]{2,1,0:T(8,128)(2,1)}, bf16[5,192,768]{2,1,0:T(8,128)(2,1)S(1)}, u32[]{:S(2)}, u32[]{:S(2)}) collective-permute-start(bf16[5,192,768]{2,1,0:T(8,128)(2,1)} %get-tuple-element.294), channel_id=1, source_target_pairs={{0,1},{1,0},{2,3},{3,2},{4,5},{5,4},{6,7},{7,6},{8,9},{9,8},{10,11... | collective-permute-start | bytes 4423688 | tf_op jit(solution)/shard_map/ppermute | solution.py:1195
  243.0 31.9 %collective-permute-start.37 = (bf16[256,768]{1,0:T(8,128)(2,1)S(1)}, bf16[256,768]{1,0:T(8,128)(2,1)}, u32[]{:S(2)}, u32[]{:S(2)}) collective-permute-start(bf16[256,768]{1,0:T(8,128)(2,1)S(1)} %copy-done.34), channel_id=1, source_target_pairs={{0,2},{1,3},{2,0},{3,1},{4,6},{5,7},{6,4},{7,5},{8,10},{9,11},{10,... | collective-permute-start | bytes 1179656 | tf_op jit(solution)/shard_map/ppermute | solution.py:1194
  244.2 30.7 %collective-permute-start.38 = (bf16[256,768]{1,0:T(8,128)(2,1)S(1)}, bf16[256,768]{1,0:T(8,128)(2,1)}, u32[]{:S(2)}, u32[]{:S(2)}) collective-permute-start(bf16[256,768]{1,0:T(8,128)(2,1)S(1)} %add_convert_fusion.4), channel_id=1, source_target_pairs={{0,2},{1,3},{2,0},{3,1},{4,6},{5,7},{6,4},{7,5},{8,10},{9,11},{10,... | collective-permute-start | bytes 1179656 | tf_op jit(solution)/shard_map/ppermute | solution.py:1194
  248.3 30.6 %collective-permute-start.18 = (bf16[256,768]{1,0:T(8,128)(2,1)}, bf16[256,768]{1,0:T(8,128)(2,1)S(1)}, u32[]{:S(2)}, u32[]{:S(2)}) collective-permute-start(bf16[256,768]{1,0:T(8,128)(2,1)} %get-tuple-element.207), channel_id=1, source_target_pairs={{0,1},{1,0},{2,3},{3,2},{4,5},{5,4},{6,7},{7,6},{8,9},{9,8},{10,11... | collective-permute-start | bytes 1179656 | tf_op jit(solution)/shard_map/ppermute | solution.py:1182
  277.8 47.0 %collective-permute-start.42 = (bf16[5,192,768]{2,1,0:T(8,128)(2,1)}, bf16[5,192,768]{2,1,0:T(8,128)(2,1)}, u32[]{:S(2)}, u32[]{:S(2)}) collective-permute-start(bf16[5,192,768]{2,1,0:T(8,128)(2,1)} %add_convert_fusion.1), channel_id=1, source_target_pairs={{0,2},{1,3},{2,0},{3,1},{4,6},{5,7},{6,4},{7,5},{8,10},{9,11},{10,... | collective-permute-start | bytes 4423688 | tf_op jit(solution)/shard_map/ppermute | solution.py:1198
  324.8 18.2 %collective-permute-start.43 = (bf16[512,768]{1,0:T(8,128)(2,1)S(1)}, bf16[512,768]{1,0:T(8,128)(2,1)S(1)}, u32[]{:S(2)}, u32[]{:S(2)}) collective-permute-start(bf16[512,768]{1,0:T(8,128)(2,1)S(1)} %add_convert_fusion.2), channel_id=1, source_target_pairs={{0,2},{1,3},{2,0},{3,1},{4,6},{5,7},{6,4},{7,5},{8,10},{9,11},{10,... | collective-permute-start | bytes 2359304 | tf_op jit(solution)/shard_map/ppermute | solution.py:132
  343.0 37.6 %collective-permute-start.46 = (bf16[8,128,768]{2,1,0:T(8,128)(2,1)}, bf16[8,128,768]{2,1,0:T(8,128)(2,1)}, u32[]{:S(2)}, u32[]{:S(2)}) collective-permute-start(bf16[8,128,768]{2,1,0:T(8,128)(2,1)} %block_grad_0.1.refs_0_), channel_id=1, source_target_pairs={{0,2},{1,3},{2,0},{3,1},{4,6},{5,7},{6,4},{7,5},{8,10},{9,11},{10,... | collective-permute-start | bytes 4718600 | tf_op jit(solution)/shard_map/ppermute | solution.py:1212
  344.4 66.6 %collective-permute-start.47 = (bf16[8,128,768]{2,1,0:T(8,128)(2,1)S(1)}, bf16[8,128,768]{2,1,0:T(8,128)(2,1)}, u32[]{:S(2)}, u32[]{:S(2)}) collective-permute-start(bf16[8,128,768]{2,1,0:T(8,128)(2,1)S(1)} %copy-done.7), channel_id=1, source_target_pairs={{0,2},{1,3},{2,0},{3,1},{4,6},{5,7},{6,4},{7,5},{8,10},{9,11},{10,... | collective-permute-start | bytes 4718600 | tf_op jit(solution)/shard_map/ppermute | solution.py:1212
  355.1 60.7 %collective-permute-start.40 = (bf16[512,768]{1,0:T(8,128)(2,1)}, bf16[512,768]{1,0:T(8,128)(2,1)}, u32[]{:S(2)}, u32[]{:S(2)}) collective-permute-start(bf16[512,768]{1,0:T(8,128)(2,1)} %get-tuple-element.297), channel_id=1, source_target_pairs={{0,1},{1,0},{2,3},{3,2},{4,5},{5,4},{6,7},{7,6},{8,9},{9,8},{10,11... | collective-permute-start | bytes 2359304 | tf_op jit(solution)/shard_map/ppermute | solution.py:128
  377.6 42.3 %collective-permute-start.44 = (bf16[8,128,768]{2,1,0:T(8,128)(2,1)}, bf16[8,128,768]{2,1,0:T(8,128)(2,1)}, u32[]{:S(2)}, u32[]{:S(2)}) collective-permute-start(bf16[8,128,768]{2,1,0:T(8,128)(2,1)} %block_grad_0.1.refs_0_), channel_id=1, source_target_pairs={{0,1},{1,0},{2,3},{3,2},{4,5},{5,4},{6,7},{7,6},{8,9},{9,8},{10,11... | collective-permute-start | bytes 4718600 | tf_op jit(solution)/shard_map/ppermute | solution.py:1216
  377.7 42.2 %collective-permute-start.45 = (bf16[8,128,768]{2,1,0:T(8,128)(2,1)S(1)}, bf16[8,128,768]{2,1,0:T(8,128)(2,1)}, u32[]{:S(2)}, u32[]{:S(2)}) collective-permute-start(bf16[8,128,768]{2,1,0:T(8,128)(2,1)S(1)} %copy-done.7), channel_id=1, source_target_pairs={{0,1},{1,0},{2,3},{3,2},{4,5},{5,4},{6,7},{7,6},{8,9},{9,8},{10,11... | collective-permute-start | bytes 4718600 | tf_op jit(solution)/shard_map/ppermute | solution.py:1216
  380.6 39.2 %collective-permute-start.48 = (bf16[8,128,768]{2,1,0:T(8,128)(2,1)}, bf16[8,128,768]{2,1,0:T(8,128)(2,1)}, u32[]{:S(2)}, u32[]{:S(2)}) collective-permute-start(bf16[8,128,768]{2,1,0:T(8,128)(2,1)} %collective-permute-done.46.refs_4_), channel_id=1, source_target_pairs={{0,1},{1,0},{2,3},{3,2},{4,5},{5,4},{6,7},{7,6},{8,9},{9,8},{10,11... | collective-permute-start | bytes 4718600 | tf_op jit(solution)/shard_map/ppermute | solution.py:1217
  (88 other events, 753.0 us)
Sparse Core Ops, SparseCore 0:
  36.2 45.4 all-gather.1
  204.6 107.4 all-reduce.5
  354.7 89.3 all-reduce.7
